TPU v7x, 32 devices: a whole 2x2x4 slice. The times are simulated.
32 devices in a mesh: grp: 2 (over y), arc: 2 (over x), reg: 4 (over z), sat: 2 (over core).
Axes of the slice: x: 2, y: 2, z: 4, core: 2. Of those that a mesh axis runs over, the one named last changes fastest.
Arguments:
- partials: bfloat16 [64, 8, 2, 128, 256], P(('grp', 'arc', 'reg'), None, 'sat'), parts along dimension 0, may hold values from -0.09375 to 0.09375
- regions: int32 [64, 8], P(('grp', 'arc', 'reg')), parts along dimension 0, may hold values from 0 to 1920, as said below
- observed: float32 [64, 128], P(('grp', 'arc', 'reg')), parts along dimension 0, may hold values from -6 to 6
- weights: float32 [64, 128], P(('grp', 'arc', 'reg')), parts along dimension 0, may hold values from 0.25 to 4
- mascons: float32 [480, 8, 256], P(None, ('grp', 'reg')), parts along dimension 1, may hold values from -6 to 6
- prior: float32 [256], replicated, may hold values from 0.05 to 0.5
Outputs:
- gradient: float32 [480, 8, 256], P(('arc', 'sat'), ('grp', 'reg')), parts along dimension 1
There are 2 independent parts, one for each index of `grp`. A program takes and returns all parts, laid end to end along the dimension named above; an argument that names none is the same for every part. Nothing has to cross between parts.
Inputs may be any that keep to these rules, and one draw needn't show every extreme that they name: Within the 4 arcs of one device along arc+reg (aligned blocks of 4 arcs), at most 8 slots name regions of one owner (region // 480); in every draw some owner gets exactly 8 from every such block. Region 1920 marks an empty slot.
All inputs are finite; a program needn't handle non-finite values.
Results may differ from a plain program's by a relative error of at most 0.0028.
Values may be sent and summed in bfloat16 or wider, within the bound.
No kernel may reach another device: no remote copies, remote signals or barrier semaphores. Data moves between devices by JAX's collectives and lax.ppermute only.
A program may use at most 64 MiB of HBM per device.

v0:
```python
import jax
import jax.numpy as jnp
from jax import lax
from jax.sharding import PartitionSpec as P


def per_device(partials, regions, observed, weights, mascons, prior):
    owners = lax.axis_size("reg")
    arcs_here, slots = regions.shape
    reg_group = mascons.shape[0]
    width = mascons.shape[2]
    count = arcs_here * slots
    capacity = count // owners
    flat_ids = regions.reshape(count)
    owner = flat_ids // reg_group
    local = flat_ids % reg_group
    valid = owner < owners
    member = (owner[:, None] == jnp.arange(owners)[None, :]).astype(jnp.int32)
    rank = jnp.sum(member * (jnp.cumsum(member, axis=0) - 1), axis=1)
    place = jnp.where(valid, owner * capacity + rank, owners * capacity)
    select = place[:, None] == jnp.arange(owners * capacity)[None, :]
    sent_ids = jnp.max(jnp.where(select, local[:, None], -1), axis=0)
    sent_ids = jnp.where(sent_ids < 0, reg_group, sent_ids).reshape(owners, capacity)
    values = mascons.astype(jnp.bfloat16)
    table = values.reshape(reg_group, width)
    asked = lax.all_to_all(sent_ids, "reg", split_axis=0, concat_axis=0, tiled=True)
    items = asked.shape[1]
    onehot = (asked.reshape(owners * items, 1) == jnp.arange(reg_group)[None, :]).astype(
        jnp.bfloat16
    )
    found = jnp.dot(onehot, table, preferred_element_type=jnp.float32).astype(jnp.bfloat16)
    returned = lax.all_to_all(
        found.reshape(owners, items, width), "reg", split_axis=0, concat_axis=0, tiled=True
    )
    rows_b = jnp.dot(
        select.astype(jnp.bfloat16),
        returned.reshape(owners * capacity, width),
        preferred_element_type=jnp.float32,
    ).astype(jnp.bfloat16)
    rows_b = rows_b.reshape(arcs_here, slots, width)
    sign = 1.0 - 2.0 * lax.axis_index("sat").astype(jnp.float32)
    own_part = jnp.einsum("akstm,akm->at", partials, rows_b, preferred_element_type=jnp.float32)
    predicted = lax.psum(sign * own_part, "sat")
    weighted = (weights * (observed - predicted)).astype(jnp.bfloat16)
    contribution = sign * jnp.einsum(
        "akstm,at->akm", partials, weighted, preferred_element_type=jnp.float32
    )
    outgoing = jnp.dot(
        select.astype(jnp.float32).T,
        contribution.reshape(count, width),
        precision=lax.Precision.HIGHEST,
    )
    arrived_ids, arrived = (
        lax.all_to_all(sent_ids, "reg", split_axis=0, concat_axis=0, tiled=True),
        lax.all_to_all(
            outgoing.reshape(owners, capacity, width),
            "reg",
            split_axis=0,
            concat_axis=0,
            tiled=True,
        ),
    )
    placing = (arrived_ids.reshape(owners * capacity, 1) == jnp.arange(reg_group)[None, :]).astype(
        jnp.float32
    )
    owner_sum = jnp.dot(
        placing.T, arrived.reshape(owners * capacity, width), precision=lax.Precision.HIGHEST
    )
    share = reg_group // (lax.axis_size("arc") * lax.axis_size("sat"))
    block_index = lax.axis_index("arc") * lax.axis_size("sat") + lax.axis_index("sat")
    summed = lax.psum_scatter(owner_sum, ("arc", "sat"), scatter_dimension=0, tiled=True)
    current = lax.dynamic_slice_in_dim(
        mascons.reshape(reg_group, width), block_index * share, share, 0
    )
    result = summed - prior[None, :] * current
    return result.reshape(share, 1, width)


def solution(mesh):
    placed = (
        P(("grp", "arc", "reg"), None, "sat", None, None),
        P(("grp", "arc", "reg"), None),
        P(("grp", "arc", "reg"), None),
        P(("grp", "arc", "reg"), None),
        P(None, ("grp", "reg"), None),
        P(),
    )
    return jax.shard_map(
        per_device,
        mesh=mesh,
        in_specs=placed,
        out_specs=P(("arc", "sat"), ("grp", "reg"), None),
        check_vma=False,
    )
```

profile of v0, /device:TPU:0, one launch (start us, length us, event | category | flops | bytes accessed | tf_op | source)
XLA Modules:
  0.0 74.0 jit_solution(958121566146988754)
XLA Ops:
  6.5 0.8 %broadcast_divide_fusion = (s32[4,8]{1,0:T(4,128)S(1)}, s32[4,8]{1,0:T(4,128)S(1)}) fusion(s32[4,8]{1,0:T(4,128)} %param.7), kind=kLoop, calls=%fused_computation.44 | loop fusion | flops 64 | bytes 384 | tf_op jit(solution)/shard_map/jit(floor_divide)/div | solution.py:15
  7.4 0.7 sign_compare_fusion
  8.1 0.1 div.17
  8.2 0.1 rem.31
  8.2 0.1 ne.50
  8.3 0.1 fusion.20
  8.4 0.1 reduce_window_sum.11
  8.5 0.2 select_reduce_fusion.1
  8.7 0.1 select_reduce_fusion
  8.8 0.1 reduce_max.12
  8.8 0.6 compare_select_fusion
  9.4 6.3 %all-to-all-start = ((s32[4,1,8]{2,1,0:T(1,128)}), s32[4,1,8]{2,1,0:T(1,128)S(1)}, u32[]{:S(2)}, u32[]{:S(2)}) async-start(s32[4,1,8]{2,1,0:T(1,128)} %bitcast), calls=%async_computation | async-start | bytes 4096 | tf_op jit(solution)/shard_map/all_to_all | solution.py:54
  15.7 1.4 %convert_element_type.26 = bf16[480,1,256]{2,1,0:T(2,128)(2,1)S(1)} convert(f32[480,1,256]{2,1,0:T(1,128)} %param.10) | non-fusion elementwise | flops 122880 | bytes 737280 | tf_op jit(solution)/shard_map/convert_element_type | solution.py:24
  17.1 4.1 %all-to-all-done = s32[4,1,8]{2,1,0:T(1,128)S(1)} async-done(((s32[4,1,8]{2,1,0:T(1,128)}), s32[4,1,8]{2,1,0:T(1,128)S(1)}, u32[]{:S(2)}, u32[]{:S(2)}) %all-to-all-start) | async-done | bytes 160 | tf_op jit(solution)/shard_map/all_to_all | solution.py:54
  21.2 0.5 broadcast.124
  21.7 0.7 reduce.3
  22.4 0.1 eq.78
  22.5 0.8 %fusion.4 = bf16[4,8,256]{2,1,0:T(8,128)(2,1)} fusion(bf16[480,1,256]{2,1,0:T(2,128)(2,1)S(1)} %convert_element_type.26, s32[32]{0:T(128)S(1)} %eq.78), kind=kOutput, calls=%fused_computation.6 | convolution fusion | flops 7887872 | bytes 262272 | tf_op jit(solution)/shard_map/dot_general | solution.py:31
  23.3 3.3 %all-to-all-start.1 = ((bf16[4,8,256]{2,1,0:T(8,128)(2,1)}), bf16[4,8,256]{2,1,0:T(8,128)(2,1)S(1)}, u32[]{:S(2)}, u32[]{:S(2)}) async-start(bf16[4,8,256]{2,1,0:T(8,128)(2,1)} %fusion.4), calls=%async_computation.1 | async-start | bytes 32768 | tf_op jit(solution)/shard_map/all_to_all | solution.py:32
  26.5 0.0 reduce-scatter.2.cloned.1.call-start
  26.6 5.5 %all-to-all-done.1 = bf16[4,8,256]{2,1,0:T(8,128)(2,1)S(1)} async-done(((bf16[4,8,256]{2,1,0:T(8,128)(2,1)}), bf16[4,8,256]{2,1,0:T(8,128)(2,1)S(1)}, u32[]{:S(2)}, u32[]{:S(2)}) %all-to-all-start.1) | async-done | bytes 16416 | tf_op jit(solution)/shard_map/all_to_all | solution.py:32
  32.1 0.2 fusion.5
  32.3 0.6 fusion.2
  33.0 2.6 %psum.7 = f32[4,128]{1,0:T(4,128)S(1)} all-reduce(f32[4,128]{1,0:T(4,128)S(1)} %broadcast_multiply_fusion), channel_id=1, replica_groups=mesh['grp'=2,'arc'=2,'reg'=4,'sat'=2] {'sat'}, use_global_device_ids=true, to_apply=%region_3.4 | all-reduce | flops 512 | bytes 4096 | tf_op jit(solution)/shard_map/psum | solution.py:43
  35.6 0.4 fusion
  36.0 0.2 fusion.11
  36.2 8.0 %all_to_all.17 = f32[4,8,256]{2,1,0:T(8,128)S(1)} all-to-all(f32[4,8,256]{2,1,0:T(8,128)S(1)} %fusion.11), channel_id=1, replica_groups=mesh['grp'=2,'arc'=2,'reg'=4,'sat'=2] {'reg'}, dimensions={0} | all-to-all | bytes 65536 | tf_op jit(solution)/shard_map/all_to_all | solution.py:55
  44.2 1.3 %fusion.10 = f32[480,256]{1,0:T(8,128)} fusion(f32[4,8,256]{2,1,0:T(8,128)S(1)} %all_to_all.17, s32[32]{0:T(128)S(1)} %eq.78), kind=kOutput, calls=%fused_computation.14 | convolution fusion | flops 47201280 | bytes 524416 | tf_op jit(solution)/shard_map/dot_general | solution.py:66
  45.5 0.9 %constant_dynamic-slice_fusion = f32[120,1,256]{2,1,0:T(1,128)S(1)} fusion(f32[480,1,256]{2,1,0:T(1,128)} %param.10, s32[]{:T(128)S(6)} %select_n.55), kind=kLoop, calls=%fused_computation.46 | loop fusion | bytes 245764 | tf_op jit(solution)/shard_map/dynamic_slice | solution.py:72
  46.4 19.0 %reduce-scatter.2.cloned.1.call-done = f32[120,256]{1,0:T(8,128)} async-done(((f32[480,256]{1,0:T(8,128)}), f32[120,256]{1,0:T(8,128)}) %reduce-scatter.2.cloned.1.call-update) | async-done | bytes 122896 | tf_op jit(solution)/shard_map/reduce_scatter | solution.py:71
  65.4 0.9 %fusion.9 = f32[120,1,256]{2,0,1:T(8,128)S(1)} fusion(f32[120,256]{1,0:T(8,128)} %reduce-scatter.2.cloned.1.call-done, f32[120,1,256]{2,1,0:T(1,128)S(1)} %constant_dynamic-slice_fusion, f32[256]{0:T(256)S(1)} %copy-done.3), kind=kLoop, calls=%fused_computation.12 | loop fusion | flops 61440 | bytes 369664 | tf_op jit(solution)/shard_map/reshape | solution.py:76
  66.3 0.8 %copy.11 = f32[120,1,256]{2,1,0:T(1,128)} copy(f32[120,1,256]{2,0,1:T(8,128)S(1)} %fusion.9) | data formatting | bytes 245760 | tf_op jit(solution)/shard_map/reshape | solution.py:76
  (14 shorter events, 0.1 us)
Async XLA Ops:
  6.5 25.8 %copy-start = (bf16[4,8,1,128,256]{4,3,2,1,0:T(8,128)(2,1)S(1)}, bf16[4,8,1,128,256]{4,3,2,1,0:T(8,128)(2,1)}, u32[]{:S(2)}) copy-start(bf16[4,8,1,128,256]{4,3,2,1,0:T(8,128)(2,1)} %param.6) | copy-start | bytes 6291460
  6.5 29.0 %copy-start.2 = (f32[4,128]{1,0:T(4,128)S(1)}, f32[4,128]{1,0:T(4,128)}, u32[]{:S(2)}) copy-start(f32[4,128]{1,0:T(4,128)} %param.8) | copy-start | bytes 6148
  6.5 29.0 %copy-start.1 = (f32[4,128]{1,0:T(4,128)S(1)}, f32[4,128]{1,0:T(4,128)}, u32[]{:S(2)}) copy-start(f32[4,128]{1,0:T(4,128)} %param.9) | copy-start | bytes 6148
  9.4 11.8 %all-to-all-start = ((s32[4,1,8]{2,1,0:T(1,128)}), s32[4,1,8]{2,1,0:T(1,128)S(1)}, u32[]{:S(2)}, u32[]{:S(2)}) async-start(s32[4,1,8]{2,1,0:T(1,128)} %bitcast), calls=%async_computation | async-start | bytes 4096 | tf_op jit(solution)/shard_map/all_to_all | solution.py:54
  23.3 8.8 %all-to-all-start.1 = ((bf16[4,8,256]{2,1,0:T(8,128)(2,1)}), bf16[4,8,256]{2,1,0:T(8,128)(2,1)S(1)}, u32[]{:S(2)}, u32[]{:S(2)}) async-start(bf16[4,8,256]{2,1,0:T(8,128)(2,1)} %fusion.4), calls=%async_computation.1 | async-start | bytes 32768 | tf_op jit(solution)/shard_map/all_to_all | solution.py:32
  26.5 38.9 %reduce-scatter.2.cloned.1.call-start = ((), (), s32[]{:S(2)}) async-start(), calls=%async_computation.4 | async-start | bytes 614400 | tf_op jit(solution)/shard_map/reduce_scatter | solution.py:71
  33.0 32.5 %copy-start.3 = (f32[256]{0:T(256)S(1)}, f32[256]{0:T(256)}, u32[]{:S(2)}) copy-start(f32[256]{0:T(256)} %param.11) | copy-start | bytes 3076
Sparse Core Ops, SparseCore 0:
  45.6 19.7 reduce-scatter.1
where the time goes:
time: 74.4 us; the launch traced here: 74 us
  waiting for transfers between devices  28.7 us (39%)
  between operations  13.5 us (18%)
  blocking collectives  10.6 us (14%)
  starting transfers between devices  9.61 us (13%)
  other arithmetic  5.5 us (7%)
  matrix products  3.48 us (5%)
  local copies, waits for them, and re-layouts  2.63 us (4%)
    reduce_scatter x1, waiting for transfers between devices, per_device(): lax.psum_scatter(owner_sum, ('arc', 'sat'), scatter_dimension=0, tiled=True)  19 us
    all_to_all x1, blocking collectives, per_device(): lax.all_to_all(outgoing.reshape(owners, capacity, width), 'reg', split_ax...  8.01 us
    all_to_all x1, starting transfers between devices, per_device(): lax.all_to_all(sent_ids, 'reg', split_axis=0, concat_axis=0, tiled=True)  6.32 us
    all_to_all x1, waiting for transfers between devices, per_device(): lax.all_to_all(found.reshape(owners, items, width), 'reg', split_axis=0,...  5.51 us
    all_to_all x1, waiting for transfers between devices, per_device(): lax.all_to_all(sent_ids, 'reg', split_axis=0, concat_axis=0, tiled=True)  4.1 us
    all_to_all x1, starting transfers between devices, per_device(): lax.all_to_all(found.reshape(owners, items, width), 'reg', split_axis=0,...  3.25 us
    psum x1, blocking collectives, per_device(): predicted = lax.psum(sign * own_part, 'sat')  2.6 us
  transfers between devices with their start and end apart: 3, of which 3 were waited for; matrix products, arithmetic and copies ran while one was open for 3% of the time, Pallas kernels for 0%

commit v1 on v0

v1 whole, which is shorter than its diff:
```python
import functools

import jax
import jax.numpy as jnp
from jax import lax
from jax.experimental import pallas as pl
from jax.experimental.pallas import tpu as pltpu
from jax.sharding import PartitionSpec as P

F32, BF16, I32 = jnp.float32, jnp.bfloat16, jnp.int32
VMEM = pltpu.VMEM


def iota(shape, dim):
    return lax.broadcasted_iota(I32, shape, dim)


def transposed_dot(a, b):
    return lax.dot_general(a, b, (((0,), (0,)), ((), ())), preferred_element_type=F32)


def column(refs):
    arcs, slots = refs[0].shape
    rows = [jnp.broadcast_to(ref[a : a + 1, :], (slots, slots)) for ref in refs for a in range(arcs)]
    spread = jnp.concatenate(rows, axis=0)
    mine = iota(spread.shape, 1) == iota(spread.shape, 0) % slots
    return jnp.sum(jnp.where(mine, spread, 0), axis=1, keepdims=True)


def lookup_kernel(cap, *refs):
    n = (len(refs) - 1) // 2
    ids, table, outs = refs[:n], refs[n], refs[n + 1 :]
    group = table.shape[0]
    col = column(ids)
    count = col.shape[0]
    each = count // n
    local = col - lax.axis_index("reg") * group
    owned = (local >= 0) & (local < group)
    onehot = (local == iota((count, group), 1)).astype(F32).astype(BF16)
    dense = jnp.dot(onehot, table[...].astype(BF16), preferred_element_type=F32).astype(BF16)
    row, other = iota((count, count), 0), iota((count, count), 1)
    before = ((other < row) & (other // each == row // each)).astype(F32).astype(BF16)
    members = jnp.broadcast_to(owned.astype(F32), (count, n * cap)).astype(BF16)
    rank = jnp.dot(before, members, preferred_element_type=F32).astype(I32)
    place = rank + (iota(rank.shape, 0) // each) * cap
    pack = (owned & (place == iota(rank.shape, 1))).astype(F32).astype(BF16)
    packed = transposed_dot(pack, dense)
    for k in range(n):
        outs[k][...] = packed[k * cap : (k + 1) * cap].astype(BF16)


def plan_kernel(cap, owners, group, ids, near_ref, far_ref, names_ref):
    me = lax.axis_index("reg")
    col = column([ids])
    count = col.shape[0]
    owner = col // group
    local = col - owner * group
    member = (owner == iota((count, owners), 1)).astype(F32)
    before = (iota((count, count), 1) < iota((count, count), 0)).astype(F32).astype(BF16)
    ahead = jnp.dot(before, member.astype(BF16), preferred_element_type=F32)
    rank = jnp.sum(member * ahead, axis=1, keepdims=True).astype(I32)
    spot = iota((count, owners * cap), 1)
    valid = owner < owners
    near = (valid & (spot == (owner ^ me) * cap + rank)).astype(F32)
    far = (valid & (spot == owner * cap + rank)).astype(F32)
    width = names_ref.shape[1]
    digit = jnp.where(iota((count, width), 1) < width // 2, local // 16, local % 16)
    names = transposed_dot(far.astype(BF16), digit.astype(F32).astype(BF16))
    near_ref[...] = near
    far_ref[...] = far
    names_ref[...] = names


def solve_kernel(cap, copies, *refs):
    n = len(refs) - 7
    rows_in = refs[:n]
    near_ref, far_ref, names_ref, diff, observed, weights, out = refs[n:]
    arcs = observed.shape[1]
    slots = diff.shape[0] // arcs
    came = jnp.concatenate([r[...].astype(F32) for r in rows_in], axis=0).astype(BF16)
    rows = jnp.dot(near_ref[...].astype(BF16), came, preferred_element_type=F32)
    parts = []
    for a in range(arcs):
        total = None
        for k in range(slots):
            i = a * slots + k
            term = diff[i] * rows[i : i + 1, :]
            total = term if total is None else total + term
        predicted = jnp.sum(total, axis=1, keepdims=True)
        weighted = weights[:, a : a + 1] * (observed[:, a : a + 1] - predicted)
        weighted = weighted.astype(BF16).astype(F32)
        for k in range(slots):
            parts.append(jnp.sum(diff[a * slots + k] * weighted, axis=0, keepdims=True))
    contribution = jnp.concatenate(parts, axis=0).astype(BF16)
    packed = transposed_dot(far_ref[...].astype(BF16), contribution)
    for o in range(n):
        both = jnp.concatenate(
            [packed[o * cap : (o + 1) * cap], names_ref[o * cap : (o + 1) * cap]], axis=0
        ).astype(BF16)
        for c in range(copies):
            out[c * n + o] = both


def place_kernel(cap, arrived, current, prior, out):
    sources, _, width = arrived.shape
    share = current.shape[0]
    block = lax.axis_index("arc") * lax.axis_size("sat") + lax.axis_index("sat")
    values, names = [], []
    for s in range(sources):
        got = arrived[s].astype(F32)
        values.append(got[:cap])
        names.append(got[cap:, : width // 2] * 16.0 + got[cap:, width // 2 :])
    values = jnp.concatenate(values, axis=0).astype(BF16)
    local = jnp.concatenate(names, axis=0).astype(I32)
    lanes = local.shape[1] * -(-share // local.shape[1])
    local = jnp.concatenate([local] * (lanes // local.shape[1]), axis=1)
    onehot = (local - block * share == iota(local.shape, 1)).astype(F32).astype(BF16)
    total = transposed_dot(onehot, values)
    out[...] = total[:share] - prior[...] * current[...]


def call(kernel, name, outs, args, flops, size, space=None):
    spec = pl.BlockSpec(memory_space=VMEM)
    return pl.pallas_call(
        kernel,
        out_shape=outs,
        in_specs=[spec] * len(args),
        out_specs=jax.tree.map(lambda _: spec, outs),
        compiler_params=pltpu.CompilerParams(vmem_limit_bytes=16 * 2**20),
        cost_estimate=pl.CostEstimate(flops=flops, bytes_accessed=size, transcendentals=0),
        name=name,
    )(*args)


def per_device(partials, regions, observed, weights, mascons, prior):
    owners, blocks = lax.axis_size("reg"), lax.axis_size("arc")
    arcs, slots = regions.shape
    epochs = observed.shape[1]
    group, width = mascons.shape[0], mascons.shape[2]
    count = arcs * slots
    cap = count // owners
    shape = jax.ShapeDtypeStruct

    def crossing(k):
        return [(r * 2 + s, (r ^ k) * 2 + (1 - s)) for r in range(owners) for s in range(2)]

    asked = [regions] + [lax.ppermute(regions, ("reg", "sat"), crossing(k)) for k in range(1, owners)]
    other = lax.ppermute(partials, "sat", [(0, 1), (1, 0)])
    sign = 1.0 - 2.0 * lax.axis_index("sat").astype(F32)
    diff = sign * (partials.astype(F32) - other.astype(F32))
    diff = diff.reshape(count, epochs, width)
    table = mascons.reshape(group, width)

    found = call(
        functools.partial(lookup_kernel, cap),
        "lookup",
        [shape((cap, width), BF16)] * owners,
        [*asked, table],
        2 * owners * count * group * width,
        group * width * 4,
    )
    came = [found[0]] + [
        lax.ppermute(found[k], ("reg", "sat"), crossing(k)) for k in range(1, owners)
    ]
    near, far, names = call(
        functools.partial(plan_kernel, cap, owners, group),
        "plan",
        [
            shape((count, owners * cap), F32),
            shape((count, owners * cap), F32),
            shape((owners * cap, width), F32),
        ],
        [regions],
        count * count * width,
        count * width * 4,
    )
    sent = call(
        functools.partial(solve_kernel, cap, blocks),
        "solve",
        shape((blocks * owners, 2 * cap, width), BF16),
        [*came, near, far, names, diff, observed.T, weights.T],
        4 * count * epochs * width,
        count * epochs * width * 4,
    )
    arrived = lax.all_to_all(sent, ("arc", "reg"), split_axis=0, concat_axis=0, tiled=True)
    share = group // (blocks * lax.axis_size("sat"))
    block = lax.axis_index("arc") * lax.axis_size("sat") + lax.axis_index("sat")
    current = lax.dynamic_slice_in_dim(table, block * share, share, 0)
    result = call(
        functools.partial(place_kernel, cap),
        "place",
        shape((share, width), F32),
        [arrived, current, prior.reshape(1, width)],
        2 * share * width * blocks * count,
        share * width * 8,
    )
    return result.reshape(share, 1, width)


def solution(mesh):
    placed = (
        P(("grp", "arc", "reg"), None, "sat", None, None),
        P(("grp", "arc", "reg"), None),
        P(("grp", "arc", "reg"), None),
        P(("grp", "arc", "reg"), None),
        P(None, ("grp", "reg"), None),
        P(),
    )
    return jax.shard_map(
        per_device,
        mesh=mesh,
        in_specs=placed,
        out_specs=P(("arc", "sat"), ("grp", "reg"), None),
        check_vma=False,
    )
```

time: 74.4 us -> 31.9 us (0.43)
  waiting for transfers between devices: 28.7 us -> 8.43 us
  between operations: 13.5 us -> 0.09 us
  blocking collectives: 10.6 us -> 0 us
  matrix products: 3.48 us -> 0 us
  starting transfers between devices: 9.61 us -> 12.9 us
  other arithmetic: 5.5 us -> 2.37 us
  Pallas kernels: 0 us -> 2.66 us
  local copies, waits for them, and re-layouts: 2.63 us -> 5.03 us
    reduce_scatter x1 -> x0, waiting for transfers between devices: 19 us -> none  [per_device(): lax.psum_scatter(owner_sum, ('arc', 'sat'), scatter_dimension=0, tiled=True)]
    ppermute x0 -> x7, starting transfers between devices: none -> 9.56 us  [the longest x3 4.89 us: per_device(): lax.ppermute(regions, ('reg', 'sat'), crossing(k))]
    all_to_all x1 -> x0, blocking collectives: 8.01 us -> none  [per_device(): lax.all_to_all(outgoing.reshape(owners, capacity, width), 'reg', split_ax...]
    all_to_all x2 -> x1, starting transfers between devices: 9.57 us -> 3.35 us  [per_device(): lax.all_to_all(sent, ('arc', 'reg'), split_axis=0, concat_axis=0, tiled=T...]
    all_to_all x2 -> x1, waiting for transfers between devices: 9.61 us -> 6 us  [per_device(): lax.all_to_all(sent, ('arc', 'reg'), split_axis=0, concat_axis=0, tiled=T...]
    dot_general x6 -> x0, matrix products: 3.48 us -> none  [the longest x1 1.26 us: per_device(): jnp.dot(placing.T, arrived.reshape(owners * capacity, width), precision=l...]
    unnamed x8, local copies, waits for them, and re-layouts: 0.02 us -> 3.33 us
    pallas_call x0 -> x4, Pallas kernels: none -> 2.66 us  [call(): pl.pallas_call(kernel, out_shape=outs, in_specs=[spec] * len(args), out_s...]
  transfers between devices with their start and end apart: 3 -> 8, of which waited for: 3 -> 3; matrix products, arithmetic and copies ran while one was open for 3% -> 19% of each run, Pallas kernels for 0% -> 3%
where the time goes in v1:
time: 31.9 us; the launch traced here: 31.5 us
  starting transfers between devices  12.9 us (40%)
  waiting for transfers between devices  8.43 us (26%)
  local copies, waits for them, and re-layouts  5.03 us (16%)
  Pallas kernels  2.66 us (8%)
  other arithmetic  2.37 us (7%)
    all_to_all x1, waiting for transfers between devices, per_device(): lax.all_to_all(sent, ('arc', 'reg'), split_axis=0, concat_axis=0, tiled=T...  6 us
    ppermute x3, starting transfers between devices, per_device(): lax.ppermute(regions, ('reg', 'sat'), crossing(k))  4.89 us
    ppermute x3, starting transfers between devices, per_device(): lax.ppermute(found[k], ('reg', 'sat'), crossing(k))  4.23 us
    all_to_all x1, starting transfers between devices, per_device(): lax.all_to_all(sent, ('arc', 'reg'), split_axis=0, concat_axis=0, tiled=T...  3.35 us
    unnamed x8, local copies, waits for them, and re-layouts  3.33 us
    pallas_call x4, Pallas kernels, call(): pl.pallas_call(kernel, out_shape=outs, in_specs=[spec] * len(args), out_s...  2.66 us
    mul x1, other arithmetic, per_device(): diff = sign * (partials.astype(F32) - other.astype(F32))  2.37 us
    ppermute x3, waiting for transfers between devices, per_device(): lax.ppermute(found[k], ('reg', 'sat'), crossing(k))  1.23 us
  transfers between devices with their start and end apart: 8, of which 3 were waited for; matrix products, arithmetic and copies ran while one was open for 19% of the time, Pallas kernels for 3%

profile of v1, /device:TPU:0, one launch (start us, length us, event | category | flops | bytes accessed | tf_op | source)
XLA Modules:
  0.0 31.5 jit_solution(9050325871550655966)
XLA Ops:
  0.0 0.5 %collective-permute-start.6 = (bf16[4,8,1,128,256]{4,3,2,1,0:T(8,128)(2,1)}, bf16[4,8,1,128,256]{4,3,2,1,0:T(8,128)(2,1)S(1)}, u32[]{:S(2)}, u32[]{:S(2)}) collective-permute-start(bf16[4,8,1,128,256]{4,3,2,1,0:T(8,128)(2,1)} %param.6), channel_id=1, source_target_pairs={{0,1},{1,0},{2,3},{3,2},{4,5},{5,4},{6,7},{7,6},{8,9},{9,8},{10,11... | collective-permute-start | bytes 6291464 | tf_op jit(solution)/shard_map/ppermute | solution.py:148
  0.5 2.7 %collective-permute-start = (s32[4,8]{1,0:T(4,128)}, s32[4,8]{1,0:T(4,128)S(1)}, u32[]{:S(2)}, u32[]{:S(2)}) collective-permute-start(s32[4,8]{1,0:T(4,128)} %ids.1), channel_id=1, source_target_pairs={{0,3},{1,2},{2,1},{3,0},{4,7},{5,6},{6,5},{7,4},{8,11},{9,10},{10,... | collective-permute-start | bytes 392 | tf_op jit(solution)/shard_map/ppermute | solution.py:147
  3.1 2.2 %collective-permute-start.1 = (s32[4,8]{1,0:T(4,128)}, s32[4,8]{1,0:T(4,128)S(1)}, u32[]{:S(2)}, u32[]{:S(2)}) collective-permute-start(s32[4,8]{1,0:T(4,128)} %ids.1), channel_id=1, source_target_pairs={{0,5},{1,4},{2,7},{3,6},{4,1},{5,0},{6,3},{7,2},{8,13},{9,12},{10,... | collective-permute-start | bytes 392 | tf_op jit(solution)/shard_map/ppermute | solution.py:147
  5.3 0.0 collective-permute-start.2
  5.3 1.1 %copy.14 = f32[480,1,256]{2,0,1:T(8,128)S(1)} copy(f32[480,1,256]{2,1,0:T(1,128)} %param.10) | data formatting | bytes 983040
  6.4 0.8 %copy.7 = f32[4,128]{0,1:T(8,128)S(1)} copy(f32[4,128]{1,0:T(4,128)} %param.8) | data formatting | bytes 4096 | tf_op args[2]
  7.2 0.8 %copy.8 = f32[4,128]{0,1:T(8,128)S(1)} copy(f32[4,128]{1,0:T(4,128)} %param.9) | data formatting | bytes 4096 | tf_op args[3]
  8.0 0.0 copy-start
  8.0 0.7 %copy-done = s32[4,8]{1,0:T(4,128)S(1)} copy-done((s32[4,8]{1,0:T(4,128)S(1)}, s32[4,8]{1,0:T(4,128)}, u32[]{:S(2)}) %copy-start) | copy-done | bytes 152
  8.7 0.5 %plan.1 = (f32[32,32]{1,0:T(8,128)S(1)}, f32[32,32]{1,0:T(8,128)S(1)}, f32[32,256]{1,0:T(8,128)S(1)}) custom-call(s32[4,8]{1,0:T(4,128)S(1)} %copy-done), custom_call_target="tpu_custom_call" | custom-call | flops 262144 | bytes 32768 | tf_op jit(solution)/shard_map/plan/pallas_call | solution.py:124
  9.2 0.0 collective-permute-done.refs_1_
  9.2 0.0 collective-permute-done.1.refs_2_
  9.2 1.2 %collective-permute-done.2.refs_3_ = s32[4,8]{1,0:T(4,128)S(1)} collective-permute-done((s32[4,8]{1,0:T(4,128)}, s32[4,8]{1,0:T(4,128)S(1)}, u32[]{:S(2)}, u32[]{:S(2)}) %collective-permute-start.2) | collective-permute-done | bytes 160 | tf_op jit(solution)/shard_map/ppermute | solution.py:147
  10.4 0.4 %lookup.1 = (bf16[8,256]{1,0:T(8,128)(2,1)S(1)}, bf16[8,256]{1,0:T(8,128)(2,1)S(1)}, bf16[8,256]{1,0:T(8,128)(2,1)S(1)}, bf16[8,256]{1,0:T(8,128)(2,1)S(1)}) custom-call(s32[4,8]{1,0:T(4,128)S(1)} %copy-done, s32[4,8]{1,0:T(4,128)S(1)} %collective-permute-done.refs_1_, s32[4,8]{1,0:T(4,128)S(1)} %collective-permute-done.1.refs_2_, ...), custom_call_target="tpu_custom_call" | custom-call | flops 31457280 | bytes 491520 | tf_op jit(solution)/shard_map/lookup/pallas_call | solution.py:124
  10.8 0.0 collective-permute-start.3
  10.8 3.0 %collective-permute-start.4 = (bf16[8,256]{1,0:T(8,128)(2,1)S(1)}, bf16[8,256]{1,0:T(8,128)(2,1)S(1)}, u32[]{:S(2)}, u32[]{:S(2)}) collective-permute-start(bf16[8,256]{1,0:T(8,128)(2,1)S(1)} %get-tuple-element.14), channel_id=1, source_target_pairs={{0,5},{1,4},{2,7},{3,6},{4,1},{5,0},{6,3},{7,2},{8,13},{9,12},{10,... | collective-permute-start | bytes 12296 | tf_op jit(solution)/shard_map/ppermute | solution.py:163
  13.8 1.2 %collective-permute-start.5 = (bf16[8,256]{1,0:T(8,128)(2,1)S(1)}, bf16[8,256]{1,0:T(8,128)(2,1)S(1)}, u32[]{:S(2)}, u32[]{:S(2)}) collective-permute-start(bf16[8,256]{1,0:T(8,128)(2,1)S(1)} %get-tuple-element.15), channel_id=1, source_target_pairs={{0,7},{1,6},{2,5},{3,4},{4,3},{5,2},{6,1},{7,0},{8,15},{9,14},{10,... | collective-permute-start | bytes 12296 | tf_op jit(solution)/shard_map/ppermute | solution.py:163
  15.0 0.0 collective-permute-done.6
  15.0 2.4 %subtract_multiply_fusion = f32[4,8,1,128,256]{4,3,2,1,0:T(8,128)S(1)} fusion(bf16[4,8,1,128,256]{4,3,2,1,0:T(8,128)(2,1)S(1)} %collective-permute-done.6, bf16[4,8,1,128,256]{4,3,2,1,0:T(8,128)(2,1)} %param.6, f32[]{:T(128)S(6)} %sub.6), kind=kLoop, calls=%fused_computation | loop fusion | flops 4194304 | bytes 8388612 | tf_op jit(solution)/shard_map/mul | solution.py:150
  17.4 0.0 copy-start.1
  17.4 0.0 collective-permute-done.3.refs_1_
  17.4 0.0 collective-permute-done.4.refs_2_
  17.4 1.2 %collective-permute-done.5.refs_3_ = bf16[8,256]{1,0:T(8,128)(2,1)S(1)} collective-permute-done((bf16[8,256]{1,0:T(8,128)(2,1)S(1)}, bf16[8,256]{1,0:T(8,128)(2,1)S(1)}, u32[]{:S(2)}, u32[]{:S(2)}) %collective-permute-start.5) | collective-permute-done | bytes 4128 | tf_op jit(solution)/shard_map/ppermute | solution.py:163
  18.7 1.6 %solve.1 = bf16[8,16,256]{2,1,0:T(8,128)(2,1)} custom-call(bf16[8,256]{1,0:T(8,128)(2,1)S(1)} %get-tuple-element.12.refs_0_, bf16[8,256]{1,0:T(8,128)(2,1)S(1)} %collective-permute-done.3.refs_1_, bf16[8,256]{1,0:T(8,128)(2,1)S(1)} %collective-permute-done.4.refs_2_, bf16[8,256]{1,0:T(8,128)(2,1)S(1)} %collective-permute-done.5.refs_3_, ...), custom_call_target="tpu_custom_call" | custom-call | flops 4194304 | bytes 4194304 | tf_op jit(solution)/shard_map/solve/pallas_call | solution.py:124
  20.2 3.4 %all-to-all-start = ((bf16[8,16,256]{2,1,0:T(8,128)(2,1)}), bf16[8,16,256]{2,1,0:T(8,128)(2,1)S(1)}, u32[]{:S(2)}, u32[]{:S(2)}) async-start(bf16[8,16,256]{2,1,0:T(8,128)(2,1)} %solve.1), calls=%async_computation | async-start | bytes 131072 | tf_op jit(solution)/shard_map/all_to_all | solution.py:185
  23.6 0.9 %constant_dynamic-slice_fusion = f32[120,1,256]{2,1,0:T(1,128)S(1)} fusion(f32[480,1,256]{2,1,0:T(1,128)} %param.10, s32[]{:T(128)S(6)} %select_n.3), kind=kLoop, calls=%fused_computation.3 | loop fusion | bytes 245764 | tf_op jit(solution)/shard_map/dynamic_slice | solution.py:188
  24.5 6.0 %all-to-all-done.arrived = bf16[8,16,256]{2,1,0:T(8,128)(2,1)S(1)} async-done(((bf16[8,16,256]{2,1,0:T(8,128)(2,1)}), bf16[8,16,256]{2,1,0:T(8,128)(2,1)S(1)}, u32[]{:S(2)}, u32[]{:S(2)}) %all-to-all-start) | async-done | bytes 65568 | tf_op jit(solution)/shard_map/all_to_all | solution.py:185
  30.5 0.0 copy-done.1
  30.5 0.2 place.1
  30.7 0.8 %copy.9 = f32[120,1,256]{2,1,0:T(1,128)} copy(f32[120,1,256]{2,0,1:T(8,128)S(1)} %bitcast.14) | data formatting | bytes 245760 | tf_op jit(solution)/shard_map/reshape | solution.py:197
  (1 shorter events, 0.0 us)
Async XLA Ops:
  0.0 15.0 %collective-permute-start.6 = (bf16[4,8,1,128,256]{4,3,2,1,0:T(8,128)(2,1)}, bf16[4,8,1,128,256]{4,3,2,1,0:T(8,128)(2,1)S(1)}, u32[]{:S(2)}, u32[]{:S(2)}) collective-permute-start(bf16[4,8,1,128,256]{4,3,2,1,0:T(8,128)(2,1)} %param.6), channel_id=1, source_target_pairs={{0,1},{1,0},{2,3},{3,2},{4,5},{5,4},{6,7},{7,6},{8,9},{9,8},{10,11... | collective-permute-start | bytes 6291464 | tf_op jit(solution)/shard_map/ppermute | solution.py:148
  0.5 8.7 %collective-permute-start = (s32[4,8]{1,0:T(4,128)}, s32[4,8]{1,0:T(4,128)S(1)}, u32[]{:S(2)}, u32[]{:S(2)}) collective-permute-start(s32[4,8]{1,0:T(4,128)} %ids.1), channel_id=1, source_target_pairs={{0,3},{1,2},{2,1},{3,0},{4,7},{5,6},{6,5},{7,4},{8,11},{9,10},{10,... | collective-permute-start | bytes 392 | tf_op jit(solution)/shard_map/ppermute | solution.py:147
  3.1 6.0 %collective-permute-start.1 = (s32[4,8]{1,0:T(4,128)}, s32[4,8]{1,0:T(4,128)S(1)}, u32[]{:S(2)}, u32[]{:S(2)}) collective-permute-start(s32[4,8]{1,0:T(4,128)} %ids.1), channel_id=1, source_target_pairs={{0,5},{1,4},{2,7},{3,6},{4,1},{5,0},{6,3},{7,2},{8,13},{9,12},{10,... | collective-permute-start | bytes 392 | tf_op jit(solution)/shard_map/ppermute | solution.py:147
  5.3 5.0 %collective-permute-start.2 = (s32[4,8]{1,0:T(4,128)}, s32[4,8]{1,0:T(4,128)S(1)}, u32[]{:S(2)}, u32[]{:S(2)}) collective-permute-start(s32[4,8]{1,0:T(4,128)} %ids.1), channel_id=1, source_target_pairs={{0,7},{1,6},{2,5},{3,4},{4,3},{5,2},{6,1},{7,0},{8,15},{9,14},{10,... | collective-permute-start | bytes 392 | tf_op jit(solution)/shard_map/ppermute | solution.py:147
  8.0 0.7 %copy-start = (s32[4,8]{1,0:T(4,128)S(1)}, s32[4,8]{1,0:T(4,128)}, u32[]{:S(2)}) copy-start(s32[4,8]{1,0:T(4,128)} %ids.1) | copy-start | bytes 388
  10.8 6.6 %collective-permute-start.3 = (bf16[8,256]{1,0:T(8,128)(2,1)S(1)}, bf16[8,256]{1,0:T(8,128)(2,1)S(1)}, u32[]{:S(2)}, u32[]{:S(2)}) collective-permute-start(bf16[8,256]{1,0:T(8,128)(2,1)S(1)} %get-tuple-element.13), channel_id=1, source_target_pairs={{0,3},{1,2},{2,1},{3,0},{4,7},{5,6},{6,5},{7,4},{8,11},{9,10},{10,... | collective-permute-start | bytes 12296 | tf_op jit(solution)/shard_map/ppermute | solution.py:163
  10.8 6.6 %collective-permute-start.4 = (bf16[8,256]{1,0:T(8,128)(2,1)S(1)}, bf16[8,256]{1,0:T(8,128)(2,1)S(1)}, u32[]{:S(2)}, u32[]{:S(2)}) collective-permute-start(bf16[8,256]{1,0:T(8,128)(2,1)S(1)} %get-tuple-element.14), channel_id=1, source_target_pairs={{0,5},{1,4},{2,7},{3,6},{4,1},{5,0},{6,3},{7,2},{8,13},{9,12},{10,... | collective-permute-start | bytes 12296 | tf_op jit(solution)/shard_map/ppermute | solution.py:163
  13.8 4.8 %collective-permute-start.5 = (bf16[8,256]{1,0:T(8,128)(2,1)S(1)}, bf16[8,256]{1,0:T(8,128)(2,1)S(1)}, u32[]{:S(2)}, u32[]{:S(2)}) collective-permute-start(bf16[8,256]{1,0:T(8,128)(2,1)S(1)} %get-tuple-element.15), channel_id=1, source_target_pairs={{0,7},{1,6},{2,5},{3,4},{4,3},{5,2},{6,1},{7,0},{8,15},{9,14},{10,... | collective-permute-start | bytes 12296 | tf_op jit(solution)/shard_map/ppermute | solution.py:163
  17.4 13.1 %copy-start.1 = (f32[256]{0:T(256)S(1)}, f32[256]{0:T(256)}, u32[]{:S(2)}) copy-start(f32[256]{0:T(256)} %param.11) | copy-start | bytes 3076
  20.2 10.3 %all-to-all-start = ((bf16[8,16,256]{2,1,0:T(8,128)(2,1)}), bf16[8,16,256]{2,1,0:T(8,128)(2,1)S(1)}, u32[]{:S(2)}, u32[]{:S(2)}) async-start(bf16[8,16,256]{2,1,0:T(8,128)(2,1)} %solve.1), calls=%async_computation | async-start | bytes 131072 | tf_op jit(solution)/shard_map/all_to_all | solution.py:185

commit v2 on v1

v2 whole, which is shorter than its diff:
```python
import functools

import jax
import jax.numpy as jnp
from jax import lax
from jax.experimental import pallas as pl
from jax.experimental.pallas import tpu as pltpu
from jax.sharding import PartitionSpec as P

F32, BF16, I32 = jnp.float32, jnp.bfloat16, jnp.int32
VMEM = pltpu.VMEM


def iota(shape, dim):
    return lax.broadcasted_iota(I32, shape, dim)


def transposed_dot(a, b):
    return lax.dot_general(a, b, (((0,), (0,)), ((), ())), preferred_element_type=F32)


def column(refs):
    arcs, slots = refs[0].shape
    rows = [jnp.broadcast_to(ref[a : a + 1, :], (slots, slots)) for ref in refs for a in range(arcs)]
    spread = jnp.concatenate(rows, axis=0)
    mine = iota(spread.shape, 1) == iota(spread.shape, 0) % slots
    return jnp.sum(jnp.where(mine, spread, 0), axis=1, keepdims=True)


def rows_of(local, table):
    onehot = (local == iota((local.shape[0], table.shape[0]), 1)).astype(F32).astype(BF16)
    return jnp.dot(onehot, table[...], preferred_element_type=F32)


def lookup_kernel(cap, *refs):
    n = (len(refs) - 1) // 2
    ids, table, outs = refs[:n], refs[n], refs[n + 1 :]
    group = table.shape[0]
    col = column(ids)
    count = col.shape[0]
    each = count // n
    local = col - lax.axis_index("reg") * group
    owned = (local >= 0) & (local < group)
    dense = rows_of(local, table).astype(BF16)
    row, other = iota((count, count), 0), iota((count, count), 1)
    before = ((other < row) & (other // each == row // each)).astype(F32).astype(BF16)
    members = jnp.broadcast_to(owned.astype(F32), (count, n * cap)).astype(BF16)
    rank = jnp.dot(before, members, preferred_element_type=F32).astype(I32)
    place = rank + (iota(rank.shape, 0) // each) * cap
    pack = (owned & (place == iota(rank.shape, 1))).astype(F32).astype(BF16)
    packed = transposed_dot(pack, dense)
    for k in range(n):
        outs[k][...] = packed[k * cap : (k + 1) * cap].astype(BF16)


def plan_kernel(cap, owners, *refs):
    ins, outs, scratch = refs[:5], refs[5:12], refs[12:]
    table_ref, own_ref, near_ref, far_ref, names_ref, turned_ref, damped_ref = outs
    *held, sems = scratch
    copies = [pltpu.make_async_copy(i, h, sems.at[j]) for j, (i, h) in enumerate(zip(ins, held))]
    for copy in copies:
        copy.start()
    ids, observed, weights, prior, mascons = held
    for copy in copies[:4]:
        copy.wait()
    me = lax.axis_index("reg")
    sign = 1.0 - 2.0 * lax.axis_index("sat").astype(F32)
    group = table_ref.shape[0]
    col = column([ids])
    count = col.shape[0]
    owner = col // group
    local = col - owner * group
    member = (owner == iota((count, owners), 1)).astype(F32)
    before = (iota((count, count), 1) < iota((count, count), 0)).astype(F32).astype(BF16)
    ahead = jnp.dot(before, member.astype(BF16), preferred_element_type=F32)
    rank = jnp.sum(member * ahead, axis=1, keepdims=True).astype(I32)
    valid = owner < owners
    step = owner ^ me
    spot = iota(near_ref.shape, 1)
    near = valid & (step > 0) & (spot == (step - 1) * cap + rank)
    far = (valid & (iota(far_ref.shape, 1) == owner * cap + rank)).astype(F32)
    width = names_ref.shape[1]
    digit = jnp.where(iota((count, width), 1) < width // 2, local // 16, local % 16)
    near_ref[...] = near.astype(F32) * sign
    far_ref[...] = far * sign
    names_ref[...] = transposed_dot(far.astype(BF16), digit.astype(F32).astype(BF16))
    turned_ref[...] = jnp.concatenate([observed[...], weights[...]], axis=0).T
    copies[4].wait()
    table_ref[...] = mascons[:, 0, :].astype(BF16)
    own_ref[...] = rows_of(col - me * group, table_ref) * sign
    share = damped_ref.shape[0]
    block = lax.axis_index("arc") * lax.axis_size("sat") + lax.axis_index("sat")
    damped_ref[...] = prior[...] * mascons[pl.ds(block * share, share), 0, :]


def differ_kernel(own, other, out, held, sems):
    parts = sems.shape[0]
    step = out.shape[0] // parts
    copies = []
    for p in range(parts):
        part = pl.ds(p * step, step)
        copies.append(pltpu.make_async_copy(own.at[part], held.at[part], sems.at[p]))
        copies[-1].start()
    for p in range(parts):
        copies[p].wait()
        for i in range(p * step, (p + 1) * step):
            out[i] = held[i].astype(F32) - other[i].astype(F32)


def solve_kernel(cap, copies, *refs):
    n = len(refs) - 7
    came = refs[:n]
    own_ref, near_ref, far_ref, names_ref, turned, diff, out = refs[n:]
    arcs = turned.shape[1] // 2
    slots = diff.shape[0] // arcs
    came = jnp.concatenate([r[...].astype(F32) for r in came], axis=0).astype(BF16)
    rows = own_ref[...] + jnp.dot(near_ref[...].astype(BF16), came, preferred_element_type=F32)
    parts = []
    for a in range(arcs):
        total = None
        for k in range(slots):
            i = a * slots + k
            term = diff[i] * rows[i : i + 1, :]
            total = term if total is None else total + term
        predicted = jnp.sum(total, axis=1, keepdims=True)
        weighted = turned[:, arcs + a : arcs + a + 1] * (turned[:, a : a + 1] - predicted)
        weighted = weighted.astype(BF16).astype(F32)
        for k in range(slots):
            parts.append(jnp.sum(diff[a * slots + k] * weighted, axis=0, keepdims=True))
    contribution = jnp.concatenate(parts, axis=0).astype(BF16)
    packed = transposed_dot(far_ref[...].astype(BF16), contribution)
    owners = out.shape[0] // copies
    for o in range(owners):
        both = jnp.concatenate(
            [packed[o * cap : (o + 1) * cap], names_ref[o * cap : (o + 1) * cap]], axis=0
        ).astype(BF16)
        for c in range(copies):
            out[c * owners + o] = both


def place_kernel(cap, arrived, damped, out):
    sources, _, width = arrived.shape
    share = out.shape[0]
    block = lax.axis_index("arc") * lax.axis_size("sat") + lax.axis_index("sat")
    values, names = [], []
    for s in range(sources):
        got = arrived[s].astype(F32)
        values.append(got[:cap])
        names.append(got[cap:, : width // 2] * 16.0 + got[cap:, width // 2 :])
    values = jnp.concatenate(values, axis=0).astype(BF16)
    local = jnp.concatenate(names, axis=0).astype(I32)
    local = jnp.concatenate([local] * -(-share // local.shape[1]), axis=1)
    onehot = (local - block * share == iota(local.shape, 1)).astype(F32).astype(BF16)
    total = transposed_dot(onehot, values)
    out[:, 0, :] = total[:share] - damped[...]


def call(kernel, name, outs, args, flops, size, scratch=(), anywhere=()):
    spec, raw = pl.BlockSpec(memory_space=VMEM), pl.BlockSpec(memory_space=pltpu.HBM)
    return pl.pallas_call(
        kernel,
        out_shape=outs,
        in_specs=[raw if i in anywhere else spec for i in range(len(args))],
        out_specs=jax.tree.map(lambda _: spec, outs),
        scratch_shapes=scratch,
        compiler_params=pltpu.CompilerParams(vmem_limit_bytes=16 * 2**20),
        cost_estimate=pl.CostEstimate(flops=flops, bytes_accessed=size, transcendentals=0),
        name=name,
    )(*(pltpu.with_memory_space_constraint(x, pltpu.HBM) if i in anywhere else x for i, x in enumerate(args)))


def per_device(partials, regions, observed, weights, mascons, prior):
    owners, blocks = lax.axis_size("reg"), lax.axis_size("arc")
    arcs, slots = regions.shape
    epochs = observed.shape[1]
    group, width = mascons.shape[0], mascons.shape[2]
    count = arcs * slots
    cap = count // owners
    shape = jax.ShapeDtypeStruct

    def crossing(k):
        return [(r * 2 + s, (r ^ k) * 2 + (1 - s)) for r in range(owners) for s in range(2)]

    names = ("reg", "sat")
    steps = range(1, owners)
    asked = [lax.ppermute(regions, names, crossing(k)) for k in steps]
    other = lax.ppermute(partials, "sat", [(0, 1), (1, 0)])
    share = group // (blocks * lax.axis_size("sat"))
    inputs = [regions, observed, weights, prior.reshape(1, width), mascons]
    table, own, near, far, named, turned, damped = call(
        functools.partial(plan_kernel, cap, owners),
        "plan",
        [
            shape((group, width), BF16),
            shape((count, width), F32),
            shape((count, (owners - 1) * cap), F32),
            shape((count, owners * cap), F32),
            shape((owners * cap, width), F32),
            shape((epochs, 2 * arcs), F32),
            shape((share, width), F32),
        ],
        inputs,
        count * count * width,
        group * width * 4,
        [*(VMEM(i.shape, i.dtype) for i in inputs), pltpu.SemaphoreType.DMA((len(inputs),))],
        range(len(inputs)),
    )
    found = call(
        functools.partial(lookup_kernel, cap),
        "lookup",
        [shape((cap, width), BF16)] * (owners - 1),
        [*asked, table],
        2 * owners * count * group * width,
        group * width * 4,
    )
    came = [lax.ppermute(found[k - 1], names, crossing(k)) for k in steps]
    whole = (count, epochs, width)
    diff = call(
        differ_kernel,
        "differ",
        shape(whole, F32),
        [partials.reshape(whole), other.reshape(whole)],
        count * epochs * width,
        count * epochs * width * 8,
        [VMEM(whole, BF16), pltpu.SemaphoreType.DMA((4,))],
        (0,),
    )
    sent = call(
        functools.partial(solve_kernel, cap, blocks),
        "solve",
        shape((blocks * owners, 2 * cap, width), BF16),
        [*came, own, near, far, named, turned, diff],
        4 * count * epochs * width,
        count * epochs * width * 4,
    )
    arrived = lax.all_to_all(sent, ("arc", "reg"), split_axis=0, concat_axis=0, tiled=True)
    return call(
        functools.partial(place_kernel, cap),
        "place",
        shape((share, 1, width), F32),
        [arrived, damped],
        2 * share * width * blocks * count,
        share * width * 8,
    )


def solution(mesh):
    placed = (
        P(("grp", "arc", "reg"), None, "sat", None, None),
        P(("grp", "arc", "reg"), None),
        P(("grp", "arc", "reg"), None),
        P(("grp", "arc", "reg"), None),
        P(None, ("grp", "reg"), None),
        P(),
    )
    return jax.shard_map(
        per_device,
        mesh=mesh,
        in_specs=placed,
        out_specs=P(("arc", "sat"), ("grp", "reg"), None),
        check_vma=False,
    )
```

time: 31.9 us -> 30.8 us (0.966)
  blocking collectives: 0 us -> 11.8 us
  waiting for transfers between devices: 8.43 us -> 3.14 us
  local copies, waits for them, and re-layouts: 5.03 us -> 0 us
  Pallas kernels: 2.66 us -> 6.02 us
  starting transfers between devices: 12.9 us -> 9.57 us
  other arithmetic: 2.37 us -> 0 us
    all_to_all x0 -> x1, blocking collectives: none -> 11.8 us  [per_device(): lax.all_to_all(sent, ('arc', 'reg'), split_axis=0, concat_axis=0, tiled=T...]
    all_to_all x1 -> x0, waiting for transfers between devices: 6 us -> none  [per_device(): lax.all_to_all(sent, ('arc', 'reg'), split_axis=0, concat_axis=0, tiled=T...]
    pallas_call x4 -> x5, Pallas kernels: 2.66 us -> 6.02 us  [call(): pl.pallas_call(kernel, out_shape=outs, in_specs=[raw if i in anywhere els...]
    all_to_all x1 -> x0, starting transfers between devices: 3.35 us -> none  [per_device(): lax.all_to_all(sent, ('arc', 'reg'), split_axis=0, concat_axis=0, tiled=T...]
    unnamed x8 -> x0, local copies, waits for them, and re-layouts: 3.33 us -> none
    mul x1 -> x0, other arithmetic: 2.37 us -> none  [per_device(): diff = sign * (partials.astype(F32) - other.astype(F32))]
    dynamic_slice x1 -> x0, local copies, waits for them, and re-layouts: 0.92 us -> none  [per_device(): current = lax.dynamic_slice_in_dim(table, block * share, share, 0)]
    reshape x1 -> x0, local copies, waits for them, and re-layouts: 0.78 us -> none  [per_device(): return result.reshape(share, 1, width)]
  transfers between devices with their start and end apart: 8 -> 7, of which waited for: 3 -> 2; matrix products, arithmetic and copies ran while one was open for 19% -> 0% of each run, Pallas kernels for 3% -> 13%
where the time goes in v2:
time: 30.8 us; the launch traced here: 30.6 us
  blocking collectives  11.8 us (38%)
  starting transfers between devices  9.57 us (31%)
  Pallas kernels  6.02 us (20%)
  waiting for transfers between devices  3.14 us (10%)
    all_to_all x1, blocking collectives, per_device(): lax.all_to_all(sent, ('arc', 'reg'), split_axis=0, concat_axis=0, tiled=T...  11.8 us
    pallas_call x5, Pallas kernels, call(): pl.pallas_call(kernel, out_shape=outs, in_specs=[raw if i in anywhere els...  6.02 us
    ppermute x3, starting transfers between devices, per_device(): asked = [lax.ppermute(regions, names, crossing(k)) for k in steps]  4.89 us
    ppermute x3, starting transfers between devices, per_device(): came = [lax.ppermute(found[k - 1], names, crossing(k)) for k in steps]  4.23 us
    ppermute x3, waiting for transfers between devices, per_device(): asked = [lax.ppermute(regions, names, crossing(k)) for k in steps]  2.95 us
  transfers between devices with their start and end apart: 7, of which 2 were waited for; matrix products, arithmetic and copies ran while one was open for 0% of the time, Pallas kernels for 13%

profile of v2, /device:TPU:0, one launch (start us, length us, event | category | flops | bytes accessed | tf_op | source)
XLA Modules:
  0.0 30.6 jit_solution(17877813537235541222)
XLA Ops:
  0.0 0.5 %collective-permute-start.6 = (bf16[4,8,1,128,256]{4,3,2,1,0:T(8,128)(2,1)}, bf16[4,8,1,128,256]{4,3,2,1,0:T(8,128)(2,1)S(1)}, u32[]{:S(2)}, u32[]{:S(2)}) collective-permute-start(bf16[4,8,1,128,256]{4,3,2,1,0:T(8,128)(2,1)} %param.6), channel_id=1, source_target_pairs={{0,1},{1,0},{2,3},{3,2},{4,5},{5,4},{6,7},{7,6},{8,9},{9,8},{10,11... | collective-permute-start | bytes 6291464 | tf_op jit(solution)/shard_map/ppermute | solution.py:187
  0.5 3.7 %collective-permute-start.1 = (s32[4,8]{1,0:T(4,128)}, s32[4,8]{1,0:T(4,128)S(1)}, u32[]{:S(2)}, u32[]{:S(2)}) collective-permute-start(s32[4,8]{1,0:T(4,128)} %refs_0_.1), channel_id=1, source_target_pairs={{0,5},{1,4},{2,7},{3,6},{4,1},{5,0},{6,3},{7,2},{8,13},{9,12},{10,... | collective-permute-start | bytes 392 | tf_op jit(solution)/shard_map/ppermute | solution.py:186
  4.2 1.2 %collective-permute-start = (s32[4,8]{1,0:T(4,128)}, s32[4,8]{1,0:T(4,128)S(1)}, u32[]{:S(2)}, u32[]{:S(2)}) collective-permute-start(s32[4,8]{1,0:T(4,128)} %refs_0_.1), channel_id=1, source_target_pairs={{0,3},{1,2},{2,1},{3,0},{4,7},{5,6},{6,5},{7,4},{8,11},{9,10},{10,... | collective-permute-start | bytes 392 | tf_op jit(solution)/shard_map/ppermute | solution.py:186
  5.3 0.0 collective-permute-start.2
  5.3 2.0 %plan.1 = (bf16[480,256]{1,0:T(8,128)(2,1)S(1)}, f32[32,256]{1,0:T(8,128)S(1)}, f32[32,24]{1,0:T(8,128)S(1)}, f32[32,32]{1,0:T(8,128)S(1)}, f32[32,256]{1,0:T(8,...) custom-call(s32[4,8]{1,0:T(4,128)} %refs_0_.1, f32[4,128]{1,0:T(4,128)} %refs_1_.1, f32[4,128]{1,0:T(4,128)} %refs_2_.1, ...), custom_call_target="tpu_custom_call" | custom-call | flops 262144 | bytes 491520 | tf_op jit(solution)/shard_map/plan/pallas_call | solution.py:160
  7.4 0.0 collective-permute-done.1.refs_1_
  7.4 0.0 collective-permute-done.refs_0_
  7.4 2.9 %collective-permute-done.2.refs_2_ = s32[4,8]{1,0:T(4,128)S(1)} collective-permute-done((s32[4,8]{1,0:T(4,128)}, s32[4,8]{1,0:T(4,128)S(1)}, u32[]{:S(2)}, u32[]{:S(2)}) %collective-permute-start.2) | collective-permute-done | bytes 160 | tf_op jit(solution)/shard_map/ppermute | solution.py:186
  10.4 0.4 %lookup.1 = (bf16[8,256]{1,0:T(8,128)(2,1)S(1)}, bf16[8,256]{1,0:T(8,128)(2,1)S(1)}, bf16[8,256]{1,0:T(8,128)(2,1)S(1)}) custom-call(s32[4,8]{1,0:T(4,128)S(1)} %collective-permute-done.refs_0_, s32[4,8]{1,0:T(4,128)S(1)} %collective-permute-done.1.refs_1_, s32[4,8]{1,0:T(4,128)S(1)} %collective-permute-done.2.refs_2_, ...), custom_call_target="tpu_custom_call" | custom-call | flops 31457280 | bytes 491520 | tf_op jit(solution)/shard_map/lookup/pallas_call | solution.py:160
  10.8 0.0 collective-permute-start.3
  10.8 1.3 %collective-permute-start.4 = (bf16[8,256]{1,0:T(8,128)(2,1)S(1)}, bf16[8,256]{1,0:T(8,128)(2,1)S(1)}, u32[]{:S(2)}, u32[]{:S(2)}) collective-permute-start(bf16[8,256]{1,0:T(8,128)(2,1)S(1)} %get-tuple-element.17), channel_id=1, source_target_pairs={{0,5},{1,4},{2,7},{3,6},{4,1},{5,0},{6,3},{7,2},{8,13},{9,12},{10,... | collective-permute-start | bytes 12296 | tf_op jit(solution)/shard_map/ppermute | solution.py:216
  12.0 3.0 %collective-permute-start.5 = (bf16[8,256]{1,0:T(8,128)(2,1)S(1)}, bf16[8,256]{1,0:T(8,128)(2,1)S(1)}, u32[]{:S(2)}, u32[]{:S(2)}) collective-permute-start(bf16[8,256]{1,0:T(8,128)(2,1)S(1)} %get-tuple-element.18), channel_id=1, source_target_pairs={{0,7},{1,6},{2,5},{3,4},{4,3},{5,2},{6,1},{7,0},{8,15},{9,14},{10,... | collective-permute-start | bytes 12296 | tf_op jit(solution)/shard_map/ppermute | solution.py:216
  15.0 0.0 collective-permute-done.6
  15.0 1.7 %differ.1.refs_8_ = f32[32,128,256]{2,1,0:T(8,128)S(1)} custom-call(bf16[32,128,256]{2,1,0:T(8,128)(2,1)} %bitcast.4, bf16[32,128,256]{2,1,0:T(8,128)(2,1)S(1)} %bitcast.3), custom_call_target="tpu_custom_call" | custom-call | flops 1048576 | bytes 8388608 | tf_op jit(solution)/shard_map/differ/pallas_call | solution.py:160
  16.7 0.0 collective-permute-done.3.refs_0_
  16.7 0.0 collective-permute-done.4.refs_1_
  16.7 0.2 collective-permute-done.5.refs_2_
  16.9 1.0 %solve.1 = bf16[8,16,256]{2,1,0:T(8,128)(2,1)S(1)} custom-call(bf16[8,256]{1,0:T(8,128)(2,1)S(1)} %collective-permute-done.3.refs_0_, bf16[8,256]{1,0:T(8,128)(2,1)S(1)} %collective-permute-done.4.refs_1_, bf16[8,256]{1,0:T(8,128)(2,1)S(1)} %collective-permute-done.5.refs_2_, f32[32,256]{1,0:T(8,128)S(1)} %get-tuple-element.19.refs_3_, ...), custom_call_target="tpu_custom_call" | custom-call | flops 4194304 | bytes 4194304 | tf_op jit(solution)/shard_map/solve/pallas_call | solution.py:160
  17.9 11.8 %all_to_all.5.arrived = bf16[8,16,256]{2,1,0:T(8,128)(2,1)S(1)} all-to-all(bf16[8,16,256]{2,1,0:T(8,128)(2,1)S(1)} %solve.1), channel_id=1, replica_groups=mesh['grp'=2,'arc'=2,'reg'=4,'sat'=2] {'arc','reg'}, dimensions={0} | all-to-all | bytes 131072 | tf_op jit(solution)/shard_map/all_to_all | solution.py:236
  29.7 0.9 %place.1 = f32[120,1,256]{2,1,0:T(1,128)} custom-call(bf16[8,16,256]{2,1,0:T(8,128)(2,1)S(1)} %all_to_all.5.arrived, f32[120,256]{1,0:T(8,128)S(1)} %get-tuple-element.24.damped), custom_call_target="tpu_custom_call" | custom-call | flops 3932160 | bytes 245760 | tf_op jit(solution)/shard_map/place/pallas_call | solution.py:160
Async XLA Ops:
  0.0 15.0 %collective-permute-start.6 = (bf16[4,8,1,128,256]{4,3,2,1,0:T(8,128)(2,1)}, bf16[4,8,1,128,256]{4,3,2,1,0:T(8,128)(2,1)S(1)}, u32[]{:S(2)}, u32[]{:S(2)}) collective-permute-start(bf16[4,8,1,128,256]{4,3,2,1,0:T(8,128)(2,1)} %param.6), channel_id=1, source_target_pairs={{0,1},{1,0},{2,3},{3,2},{4,5},{5,4},{6,7},{7,6},{8,9},{9,8},{10,11... | collective-permute-start | bytes 6291464 | tf_op jit(solution)/shard_map/ppermute | solution.py:187
  0.5 6.9 %collective-permute-start.1 = (s32[4,8]{1,0:T(4,128)}, s32[4,8]{1,0:T(4,128)S(1)}, u32[]{:S(2)}, u32[]{:S(2)}) collective-permute-start(s32[4,8]{1,0:T(4,128)} %refs_0_.1), channel_id=1, source_target_pairs={{0,5},{1,4},{2,7},{3,6},{4,1},{5,0},{6,3},{7,2},{8,13},{9,12},{10,... | collective-permute-start | bytes 392 | tf_op jit(solution)/shard_map/ppermute | solution.py:186
  4.2 3.3 %collective-permute-start = (s32[4,8]{1,0:T(4,128)}, s32[4,8]{1,0:T(4,128)S(1)}, u32[]{:S(2)}, u32[]{:S(2)}) collective-permute-start(s32[4,8]{1,0:T(4,128)} %refs_0_.1), channel_id=1, source_target_pairs={{0,3},{1,2},{2,1},{3,0},{4,7},{5,6},{6,5},{7,4},{8,11},{9,10},{10,... | collective-permute-start | bytes 392 | tf_op jit(solution)/shard_map/ppermute | solution.py:186
  5.3 5.0 %collective-permute-start.2 = (s32[4,8]{1,0:T(4,128)}, s32[4,8]{1,0:T(4,128)S(1)}, u32[]{:S(2)}, u32[]{:S(2)}) collective-permute-start(s32[4,8]{1,0:T(4,128)} %refs_0_.1), channel_id=1, source_target_pairs={{0,7},{1,6},{2,5},{3,4},{4,3},{5,2},{6,1},{7,0},{8,15},{9,14},{10,... | collective-permute-start | bytes 392 | tf_op jit(solution)/shard_map/ppermute | solution.py:186
  10.8 5.9 %collective-permute-start.3 = (bf16[8,256]{1,0:T(8,128)(2,1)S(1)}, bf16[8,256]{1,0:T(8,128)(2,1)S(1)}, u32[]{:S(2)}, u32[]{:S(2)}) collective-permute-start(bf16[8,256]{1,0:T(8,128)(2,1)S(1)} %get-tuple-element.16), channel_id=1, source_target_pairs={{0,3},{1,2},{2,1},{3,0},{4,7},{5,6},{6,5},{7,4},{8,11},{9,10},{10,... | collective-permute-start | bytes 12296 | tf_op jit(solution)/shard_map/ppermute | solution.py:216
  10.8 5.9 %collective-permute-start.4 = (bf16[8,256]{1,0:T(8,128)(2,1)S(1)}, bf16[8,256]{1,0:T(8,128)(2,1)S(1)}, u32[]{:S(2)}, u32[]{:S(2)}) collective-permute-start(bf16[8,256]{1,0:T(8,128)(2,1)S(1)} %get-tuple-element.17), channel_id=1, source_target_pairs={{0,5},{1,4},{2,7},{3,6},{4,1},{5,0},{6,3},{7,2},{8,13},{9,12},{10,... | collective-permute-start | bytes 12296 | tf_op jit(solution)/shard_map/ppermute | solution.py:216
  12.0 4.8 %collective-permute-start.5 = (bf16[8,256]{1,0:T(8,128)(2,1)S(1)}, bf16[8,256]{1,0:T(8,128)(2,1)S(1)}, u32[]{:S(2)}, u32[]{:S(2)}) collective-permute-start(bf16[8,256]{1,0:T(8,128)(2,1)S(1)} %get-tuple-element.18), channel_id=1, source_target_pairs={{0,7},{1,6},{2,5},{3,4},{4,3},{5,2},{6,1},{7,0},{8,15},{9,14},{10,... | collective-permute-start | bytes 12296 | tf_op jit(solution)/shard_map/ppermute | solution.py:216

commit v3 on v2

--- a/solution.py
+++ b/solution.py
@@ -77,7 +77,7 @@
     valid = owner < owners
     step = owner ^ me
     spot = iota(near_ref.shape, 1)
-    near = valid & (step > 0) & (spot == (step - 1) * cap + rank)
+    near = valid & (step > 0) & (spot == (owners - 1 - step) * cap + rank)
     far = (valid & (iota(far_ref.shape, 1) == owner * cap + rank)).astype(F32)
     width = names_ref.shape[1]
     digit = jnp.where(iota((count, width), 1) < width // 2, local // 16, local % 16)
@@ -182,8 +182,9 @@
         return [(r * 2 + s, (r ^ k) * 2 + (1 - s)) for r in range(owners) for s in range(2)]
 
     names = ("reg", "sat")
-    steps = range(1, owners)
-    asked = [lax.ppermute(regions, names, crossing(k)) for k in steps]
+    far_first = list(range(owners - 1, 0, -1))
+    askers = far_first[1:2] + far_first[:1] + far_first[2:]
+    asked = [lax.ppermute(regions, names, crossing(k)) for k in askers]
     other = lax.ppermute(partials, "sat", [(0, 1), (1, 0)])
     share = group // (blocks * lax.axis_size("sat"))
     inputs = [regions, observed, weights, prior.reshape(1, width), mascons]
@@ -213,7 +214,7 @@
         2 * owners * count * group * width,
         group * width * 4,
     )
-    came = [lax.ppermute(found[k - 1], names, crossing(k)) for k in steps]
+    came = [lax.ppermute(found[askers.index(k)], names, crossing(k)) for k in far_first]
     whole = (count, epochs, width)
     diff = call(
         differ_kernel,

time: 30.8 us -> 28.5 us (0.925)
  waiting for transfers between devices: 3.14 us -> 1.93 us
  blocking collectives: 11.8 us -> 11.1 us
  starting transfers between devices: 9.57 us -> 9.24 us
    ppermute x6, waiting for transfers between devices: 3.14 us -> 1.93 us  [the longest x3 1.84 us: per_device(): asked = [lax.ppermute(regions, names, crossing(k)) for k in askers]]
    all_to_all x1, blocking collectives: 11.8 us -> 11.1 us  [per_device(): lax.all_to_all(sent, ('arc', 'reg'), split_axis=0, concat_axis=0, tiled=T...]
    ppermute x6, starting transfers between devices: 9.12 us -> 8.79 us  [the longest x3 4.95 us: per_device(): asked = [lax.ppermute(regions, names, crossing(k)) for k in askers]]
  transfers between devices with their start and end apart: 7 -> 7, of which waited for: 2 -> 2; matrix products, arithmetic and copies ran while one was open for 0% -> 0% of each run, Pallas kernels for 13% -> 14%
where the time goes in v3:
time: 28.5 us; the launch traced here: 28.3 us
  blocking collectives  11.1 us (39%)
  starting transfers between devices  9.24 us (32%)
  Pallas kernels  6 us (21%)
  waiting for transfers between devices  1.93 us (7%)
    all_to_all x1, blocking collectives, per_device(): lax.all_to_all(sent, ('arc', 'reg'), split_axis=0, concat_axis=0, tiled=T...  11.1 us
    pallas_call x5, Pallas kernels, call(): pl.pallas_call(kernel, out_shape=outs, in_specs=[raw if i in anywhere els...  6 us
    ppermute x3, starting transfers between devices, per_device(): asked = [lax.ppermute(regions, names, crossing(k)) for k in askers]  4.95 us
    ppermute x3, starting transfers between devices, per_device(): lax.ppermute(found[askers.index(k)], names, crossing(k))  3.84 us
    ppermute x3, waiting for transfers between devices, per_device(): asked = [lax.ppermute(regions, names, crossing(k)) for k in askers]  1.84 us
  transfers between devices with their start and end apart: 7, of which 2 were waited for; matrix products, arithmetic and copies ran while one was open for 0% of the time, Pallas kernels for 14%

profile of v3, /device:TPU:0, one launch (start us, length us, event | category | flops | bytes accessed | tf_op | source)
XLA Modules:
  0.0 28.3 jit_solution(5730103257855305144)
XLA Ops:
  0.0 0.5 %collective-permute-start.6 = (bf16[4,8,1,128,256]{4,3,2,1,0:T(8,128)(2,1)}, bf16[4,8,1,128,256]{4,3,2,1,0:T(8,128)(2,1)S(1)}, u32[]{:S(2)}, u32[]{:S(2)}) collective-permute-start(bf16[4,8,1,128,256]{4,3,2,1,0:T(8,128)(2,1)} %param.6), channel_id=1, source_target_pairs={{0,1},{1,0},{2,3},{3,2},{4,5},{5,4},{6,7},{7,6},{8,9},{9,8},{10,11... | collective-permute-start | bytes 6291464 | tf_op jit(solution)/shard_map/ppermute | solution.py:188
  0.5 4.7 %collective-permute-start.1 = (s32[4,8]{1,0:T(4,128)}, s32[4,8]{1,0:T(4,128)S(1)}, u32[]{:S(2)}, u32[]{:S(2)}) collective-permute-start(s32[4,8]{1,0:T(4,128)} %refs_0_.1), channel_id=1, source_target_pairs={{0,7},{1,6},{2,5},{3,4},{4,3},{5,2},{6,1},{7,0},{8,15},{9,14},{10,... | collective-permute-start | bytes 392 | tf_op jit(solution)/shard_map/ppermute | solution.py:187
  5.2 0.0 collective-permute-start
  5.2 0.2 collective-permute-start.2
  5.4 2.0 %plan.1 = (bf16[480,256]{1,0:T(8,128)(2,1)S(1)}, f32[32,256]{1,0:T(8,128)S(1)}, f32[32,24]{1,0:T(8,128)S(1)}, f32[32,32]{1,0:T(8,128)S(1)}, f32[32,256]{1,0:T(8,...) custom-call(s32[4,8]{1,0:T(4,128)} %refs_0_.1, f32[4,128]{1,0:T(4,128)} %refs_1_.1, f32[4,128]{1,0:T(4,128)} %refs_2_.1, ...), custom_call_target="tpu_custom_call" | custom-call | flops 262144 | bytes 491520 | tf_op jit(solution)/shard_map/plan/pallas_call | solution.py:160
  7.4 0.0 collective-permute-done.1.refs_1_
  7.4 1.8 %collective-permute-done.refs_0_ = s32[4,8]{1,0:T(4,128)S(1)} collective-permute-done((s32[4,8]{1,0:T(4,128)}, s32[4,8]{1,0:T(4,128)S(1)}, u32[]{:S(2)}, u32[]{:S(2)}) %collective-permute-start) | collective-permute-done | bytes 160 | tf_op jit(solution)/shard_map/ppermute | solution.py:187
  9.3 0.0 collective-permute-done.2.refs_2_
  9.3 0.4 %lookup.1 = (bf16[8,256]{1,0:T(8,128)(2,1)S(1)}, bf16[8,256]{1,0:T(8,128)(2,1)S(1)}, bf16[8,256]{1,0:T(8,128)(2,1)S(1)}) custom-call(s32[4,8]{1,0:T(4,128)S(1)} %collective-permute-done.refs_0_, s32[4,8]{1,0:T(4,128)S(1)} %collective-permute-done.1.refs_1_, s32[4,8]{1,0:T(4,128)S(1)} %collective-permute-done.2.refs_2_, ...), custom_call_target="tpu_custom_call" | custom-call | flops 31457280 | bytes 491520 | tf_op jit(solution)/shard_map/lookup/pallas_call | solution.py:160
  9.7 1.7 %collective-permute-start.3 = (bf16[8,256]{1,0:T(8,128)(2,1)S(1)}, bf16[8,256]{1,0:T(8,128)(2,1)S(1)}, u32[]{:S(2)}, u32[]{:S(2)}) collective-permute-start(bf16[8,256]{1,0:T(8,128)(2,1)S(1)} %get-tuple-element.16), channel_id=1, source_target_pairs={{0,7},{1,6},{2,5},{3,4},{4,3},{5,2},{6,1},{7,0},{8,15},{9,14},{10,... | collective-permute-start | bytes 12296 | tf_op jit(solution)/shard_map/ppermute | solution.py:217
  11.4 0.1 collective-permute-start.4
  11.5 2.0 %collective-permute-start.5 = (bf16[8,256]{1,0:T(8,128)(2,1)S(1)}, bf16[8,256]{1,0:T(8,128)(2,1)S(1)}, u32[]{:S(2)}, u32[]{:S(2)}) collective-permute-start(bf16[8,256]{1,0:T(8,128)(2,1)S(1)} %get-tuple-element.18), channel_id=1, source_target_pairs={{0,3},{1,2},{2,1},{3,0},{4,7},{5,6},{6,5},{7,4},{8,11},{9,10},{10,... | collective-permute-start | bytes 12296 | tf_op jit(solution)/shard_map/ppermute | solution.py:217
  13.5 0.0 collective-permute-done.6
  13.5 1.7 %differ.1.refs_8_ = f32[32,128,256]{2,1,0:T(8,128)S(1)} custom-call(bf16[32,128,256]{2,1,0:T(8,128)(2,1)} %bitcast.4, bf16[32,128,256]{2,1,0:T(8,128)(2,1)S(1)} %bitcast.3), custom_call_target="tpu_custom_call" | custom-call | flops 1048576 | bytes 8388608 | tf_op jit(solution)/shard_map/differ/pallas_call | solution.py:160
  15.2 0.0 collective-permute-done.3.refs_0_
  15.2 0.1 collective-permute-done.4.refs_1_
  15.3 0.0 collective-permute-done.5.refs_2_
  15.3 1.0 %solve.1 = bf16[8,16,256]{2,1,0:T(8,128)(2,1)S(1)} custom-call(bf16[8,256]{1,0:T(8,128)(2,1)S(1)} %collective-permute-done.3.refs_0_, bf16[8,256]{1,0:T(8,128)(2,1)S(1)} %collective-permute-done.4.refs_1_, bf16[8,256]{1,0:T(8,128)(2,1)S(1)} %collective-permute-done.5.refs_2_, f32[32,256]{1,0:T(8,128)S(1)} %get-tuple-element.19.refs_3_, ...), custom_call_target="tpu_custom_call" | custom-call | flops 4194304 | bytes 4194304 | tf_op jit(solution)/shard_map/solve/pallas_call | solution.py:160
  16.3 11.1 %all_to_all.5.arrived = bf16[8,16,256]{2,1,0:T(8,128)(2,1)S(1)} all-to-all(bf16[8,16,256]{2,1,0:T(8,128)(2,1)S(1)} %solve.1), channel_id=1, replica_groups=mesh['grp'=2,'arc'=2,'reg'=4,'sat'=2] {'arc','reg'}, dimensions={0} | all-to-all | bytes 131072 | tf_op jit(solution)/shard_map/all_to_all | solution.py:237
  27.5 0.9 %place.1 = f32[120,1,256]{2,1,0:T(1,128)} custom-call(bf16[8,16,256]{2,1,0:T(8,128)(2,1)S(1)} %all_to_all.5.arrived, f32[120,256]{1,0:T(8,128)S(1)} %get-tuple-element.24.damped), custom_call_target="tpu_custom_call" | custom-call | flops 3932160 | bytes 245760 | tf_op jit(solution)/shard_map/place/pallas_call | solution.py:160
Async XLA Ops:
  0.0 13.5 %collective-permute-start.6 = (bf16[4,8,1,128,256]{4,3,2,1,0:T(8,128)(2,1)}, bf16[4,8,1,128,256]{4,3,2,1,0:T(8,128)(2,1)S(1)}, u32[]{:S(2)}, u32[]{:S(2)}) collective-permute-start(bf16[4,8,1,128,256]{4,3,2,1,0:T(8,128)(2,1)} %param.6), channel_id=1, source_target_pairs={{0,1},{1,0},{2,3},{3,2},{4,5},{5,4},{6,7},{7,6},{8,9},{9,8},{10,11... | collective-permute-start | bytes 6291464 | tf_op jit(solution)/shard_map/ppermute | solution.py:188
  0.5 7.0 %collective-permute-start.1 = (s32[4,8]{1,0:T(4,128)}, s32[4,8]{1,0:T(4,128)S(1)}, u32[]{:S(2)}, u32[]{:S(2)}) collective-permute-start(s32[4,8]{1,0:T(4,128)} %refs_0_.1), channel_id=1, source_target_pairs={{0,7},{1,6},{2,5},{3,4},{4,3},{5,2},{6,1},{7,0},{8,15},{9,14},{10,... | collective-permute-start | bytes 392 | tf_op jit(solution)/shard_map/ppermute | solution.py:187
  5.2 4.1 %collective-permute-start = (s32[4,8]{1,0:T(4,128)}, s32[4,8]{1,0:T(4,128)S(1)}, u32[]{:S(2)}, u32[]{:S(2)}) collective-permute-start(s32[4,8]{1,0:T(4,128)} %refs_0_.1), channel_id=1, source_target_pairs={{0,5},{1,4},{2,7},{3,6},{4,1},{5,0},{6,3},{7,2},{8,13},{9,12},{10,... | collective-permute-start | bytes 392 | tf_op jit(solution)/shard_map/ppermute | solution.py:187
  5.2 4.1 %collective-permute-start.2 = (s32[4,8]{1,0:T(4,128)}, s32[4,8]{1,0:T(4,128)S(1)}, u32[]{:S(2)}, u32[]{:S(2)}) collective-permute-start(s32[4,8]{1,0:T(4,128)} %refs_0_.1), channel_id=1, source_target_pairs={{0,3},{1,2},{2,1},{3,0},{4,7},{5,6},{6,5},{7,4},{8,11},{9,10},{10,... | collective-permute-start | bytes 392 | tf_op jit(solution)/shard_map/ppermute | solution.py:187
  9.7 5.5 %collective-permute-start.3 = (bf16[8,256]{1,0:T(8,128)(2,1)S(1)}, bf16[8,256]{1,0:T(8,128)(2,1)S(1)}, u32[]{:S(2)}, u32[]{:S(2)}) collective-permute-start(bf16[8,256]{1,0:T(8,128)(2,1)S(1)} %get-tuple-element.16), channel_id=1, source_target_pairs={{0,7},{1,6},{2,5},{3,4},{4,3},{5,2},{6,1},{7,0},{8,15},{9,14},{10,... | collective-permute-start | bytes 12296 | tf_op jit(solution)/shard_map/ppermute | solution.py:217
  11.4 3.9 %collective-permute-start.4 = (bf16[8,256]{1,0:T(8,128)(2,1)S(1)}, bf16[8,256]{1,0:T(8,128)(2,1)S(1)}, u32[]{:S(2)}, u32[]{:S(2)}) collective-permute-start(bf16[8,256]{1,0:T(8,128)(2,1)S(1)} %get-tuple-element.17), channel_id=1, source_target_pairs={{0,5},{1,4},{2,7},{3,6},{4,1},{5,0},{6,3},{7,2},{8,13},{9,12},{10,... | collective-permute-start | bytes 12296 | tf_op jit(solution)/shard_map/ppermute | solution.py:217
  11.5 3.8 %collective-permute-start.5 = (bf16[8,256]{1,0:T(8,128)(2,1)S(1)}, bf16[8,256]{1,0:T(8,128)(2,1)S(1)}, u32[]{:S(2)}, u32[]{:S(2)}) collective-permute-start(bf16[8,256]{1,0:T(8,128)(2,1)S(1)} %get-tuple-element.18), channel_id=1, source_target_pairs={{0,3},{1,2},{2,1},{3,0},{4,7},{5,6},{6,5},{7,4},{8,11},{9,10},{10,... | collective-permute-start | bytes 12296 | tf_op jit(solution)/shard_map/ppermute | solution.py:217

commit v4 on v3

--- a/solution.py
+++ b/solution.py
@@ -78,7 +78,7 @@
     step = owner ^ me
     spot = iota(near_ref.shape, 1)
     near = valid & (step > 0) & (spot == (owners - 1 - step) * cap + rank)
-    far = (valid & (iota(far_ref.shape, 1) == owner * cap + rank)).astype(F32)
+    far = (valid & (iota(far_ref.shape, 1) == step * cap + rank)).astype(F32)
     width = names_ref.shape[1]
     digit = jnp.where(iota((count, width), 1) < width // 2, local // 16, local % 16)
     near_ref[...] = near.astype(F32) * sign
@@ -107,10 +107,9 @@
             out[i] = held[i].astype(F32) - other[i].astype(F32)
 
 
-def solve_kernel(cap, copies, *refs):
-    n = len(refs) - 7
-    came = refs[:n]
-    own_ref, near_ref, far_ref, names_ref, turned, diff, out = refs[n:]
+def solve_kernel(cap, owners, *refs):
+    came, outs = refs[: owners - 1], refs[-owners:]
+    own_ref, near_ref, far_ref, names_ref, turned, diff = refs[owners - 1 : -owners]
     arcs = turned.shape[1] // 2
     slots = diff.shape[0] // arcs
     came = jnp.concatenate([r[...].astype(F32) for r in came], axis=0).astype(BF16)
@@ -129,24 +128,21 @@
             parts.append(jnp.sum(diff[a * slots + k] * weighted, axis=0, keepdims=True))
     contribution = jnp.concatenate(parts, axis=0).astype(BF16)
     packed = transposed_dot(far_ref[...].astype(BF16), contribution)
-    owners = out.shape[0] // copies
-    for o in range(owners):
-        both = jnp.concatenate(
-            [packed[o * cap : (o + 1) * cap], names_ref[o * cap : (o + 1) * cap]], axis=0
-        ).astype(BF16)
-        for c in range(copies):
-            out[c * owners + o] = both
-
-
-def place_kernel(cap, arrived, damped, out):
-    sources, _, width = arrived.shape
-    share = out.shape[0]
+    for k in range(owners):
+        part = slice(k * cap, (k + 1) * cap)
+        outs[k][...] = jnp.concatenate([packed[part], names_ref[part, :]], axis=0).astype(BF16)
+
+
+def place_kernel(cap, *refs):
+    *arrived, damped, out = refs
+    share, _, width = out.shape
     block = lax.axis_index("arc") * lax.axis_size("sat") + lax.axis_index("sat")
     values, names = [], []
-    for s in range(sources):
-        got = arrived[s].astype(F32)
-        values.append(got[:cap])
-        names.append(got[cap:, : width // 2] * 16.0 + got[cap:, width // 2 :])
+    for ref in arrived:
+        for s in range(ref.shape[0]):
+            got = ref[s].astype(F32)
+            values.append(got[:cap])
+            names.append(got[cap:, : width // 2] * 16.0 + got[cap:, width // 2 :])
     values = jnp.concatenate(values, axis=0).astype(BF16)
     local = jnp.concatenate(names, axis=0).astype(I32)
     local = jnp.concatenate([local] * -(-share // local.shape[1]), axis=1)
@@ -227,19 +223,25 @@
         (0,),
     )
     sent = call(
-        functools.partial(solve_kernel, cap, blocks),
+        functools.partial(solve_kernel, cap, owners),
         "solve",
-        shape((blocks * owners, 2 * cap, width), BF16),
+        [shape((2 * cap, width), BF16)] * owners,
         [*came, own, near, far, named, turned, diff],
         4 * count * epochs * width,
         count * epochs * width * 4,
     )
-    arrived = lax.all_to_all(sent, ("arc", "reg"), split_axis=0, concat_axis=0, tiled=True)
+    mine = [sent[0]] + [lax.ppermute(sent[k], names, crossing(k)) for k in far_first]
+    mine = jnp.stack(mine)
+    if blocks == 2:
+        over = [(a * 2 + s, (1 - a) * 2 + (1 - s)) for a in range(2) for s in range(2)]
+        arrived = [mine, lax.ppermute(mine, ("arc", "sat"), over)]
+    else:
+        arrived = [lax.all_gather(mine, "arc", tiled=True)]
     return call(
         functools.partial(place_kernel, cap),
         "place",
         shape((share, 1, width), F32),
-        [arrived, damped],
+        [*arrived, damped],
         2 * share * width * blocks * count,
         share * width * 8,
     )

time: 28.5 us -> 26.8 us (0.940)
  blocking collectives: 11.1 us -> 0 us
  starting transfers between devices: 9.24 us -> 14.7 us
  waiting for transfers between devices: 1.93 us -> 5.88 us
    all_to_all x1 -> x0, blocking collectives: 11.1 us -> none  [per_device(): lax.all_to_all(sent, ('arc', 'reg'), split_axis=0, concat_axis=0, tiled=T...]
    ppermute x0 -> x4, starting transfers between devices: none -> 5.5 us  [the longest x3 4.23 us: per_device(): lax.ppermute(sent[k], names, crossing(k))]
    ppermute x0 -> x4, waiting for transfers between devices: none -> 3.94 us  [the longest x1 2.2 us: per_device(): arrived = [mine, lax.ppermute(mine, ('arc', 'sat'), over)]]
  transfers between devices with their start and end apart: 7 -> 11, of which waited for: 2 -> 5; matrix products, arithmetic and copies ran while one was open for 0% -> 0% of each run, Pallas kernels for 14% -> 15%
where the time goes in v4:
time: 26.8 us; the launch traced here: 26.7 us
  starting transfers between devices  14.7 us (55%)
  Pallas kernels  6 us (22%)
  waiting for transfers between devices  5.88 us (22%)
    pallas_call x5, Pallas kernels, call(): pl.pallas_call(kernel, out_shape=outs, in_specs=[raw if i in anywhere els...  6 us
    ppermute x3, starting transfers between devices, per_device(): asked = [lax.ppermute(regions, names, crossing(k)) for k in askers]  4.95 us
    ppermute x3, starting transfers between devices, per_device(): lax.ppermute(sent[k], names, crossing(k))  4.23 us
    ppermute x3, starting transfers between devices, per_device(): lax.ppermute(found[askers.index(k)], names, crossing(k))  3.84 us
    ppermute x1, waiting for transfers between devices, per_device(): arrived = [mine, lax.ppermute(mine, ('arc', 'sat'), over)]  2.2 us
    ppermute x3, waiting for transfers between devices, per_device(): asked = [lax.ppermute(regions, names, crossing(k)) for k in askers]  1.84 us
    ppermute x3, waiting for transfers between devices, per_device(): lax.ppermute(sent[k], names, crossing(k))  1.75 us
    ppermute x1, starting transfers between devices, per_device(): arrived = [mine, lax.ppermute(mine, ('arc', 'sat'), over)]  1.27 us
  transfers between devices with their start and end apart: 11, of which 5 were waited for; matrix products, arithmetic and copies ran while one was open for 0% of the time, Pallas kernels for 15%

profile of v4, /device:TPU:0, one launch (start us, length us, event | category | flops | bytes accessed | tf_op | source)
XLA Modules:
  0.0 26.7 jit_solution(10500089357048761898)
XLA Ops:
  0.0 0.5 %collective-permute-start.6 = (bf16[4,8,1,128,256]{4,3,2,1,0:T(8,128)(2,1)}, bf16[4,8,1,128,256]{4,3,2,1,0:T(8,128)(2,1)S(1)}, u32[]{:S(2)}, u32[]{:S(2)}) collective-permute-start(bf16[4,8,1,128,256]{4,3,2,1,0:T(8,128)(2,1)} %param.6), channel_id=1, source_target_pairs={{0,1},{1,0},{2,3},{3,2},{4,5},{5,4},{6,7},{7,6},{8,9},{9,8},{10,11... | collective-permute-start | bytes 6291464 | tf_op jit(solution)/shard_map/ppermute | solution.py:184
  0.5 4.7 %collective-permute-start.1 = (s32[4,8]{1,0:T(4,128)}, s32[4,8]{1,0:T(4,128)S(1)}, u32[]{:S(2)}, u32[]{:S(2)}) collective-permute-start(s32[4,8]{1,0:T(4,128)} %refs_0_.1), channel_id=1, source_target_pairs={{0,7},{1,6},{2,5},{3,4},{4,3},{5,2},{6,1},{7,0},{8,15},{9,14},{10,... | collective-permute-start | bytes 392 | tf_op jit(solution)/shard_map/ppermute | solution.py:183
  5.2 0.0 collective-permute-start
  5.2 0.2 collective-permute-start.2
  5.4 2.0 %plan.1 = (bf16[480,256]{1,0:T(8,128)(2,1)S(1)}, f32[32,256]{1,0:T(8,128)S(1)}, f32[32,24]{1,0:T(8,128)S(1)}, f32[32,32]{1,0:T(8,128)S(1)}, f32[32,256]{1,0:T(8,...) custom-call(s32[4,8]{1,0:T(4,128)} %refs_0_.1, f32[4,128]{1,0:T(4,128)} %refs_1_.1, f32[4,128]{1,0:T(4,128)} %refs_2_.1, ...), custom_call_target="tpu_custom_call" | custom-call | flops 262144 | bytes 491520 | tf_op jit(solution)/shard_map/plan/pallas_call | solution.py:156
  7.4 0.0 collective-permute-done.1.refs_1_
  7.4 1.8 %collective-permute-done.refs_0_ = s32[4,8]{1,0:T(4,128)S(1)} collective-permute-done((s32[4,8]{1,0:T(4,128)}, s32[4,8]{1,0:T(4,128)S(1)}, u32[]{:S(2)}, u32[]{:S(2)}) %collective-permute-start) | collective-permute-done | bytes 160 | tf_op jit(solution)/shard_map/ppermute | solution.py:183
  9.3 0.0 collective-permute-done.2.refs_2_
  9.3 0.4 %lookup.1 = (bf16[8,256]{1,0:T(8,128)(2,1)S(1)}, bf16[8,256]{1,0:T(8,128)(2,1)S(1)}, bf16[8,256]{1,0:T(8,128)(2,1)S(1)}) custom-call(s32[4,8]{1,0:T(4,128)S(1)} %collective-permute-done.refs_0_, s32[4,8]{1,0:T(4,128)S(1)} %collective-permute-done.1.refs_1_, s32[4,8]{1,0:T(4,128)S(1)} %collective-permute-done.2.refs_2_, ...), custom_call_target="tpu_custom_call" | custom-call | flops 31457280 | bytes 491520 | tf_op jit(solution)/shard_map/lookup/pallas_call | solution.py:156
  9.7 1.7 %collective-permute-start.3 = (bf16[8,256]{1,0:T(8,128)(2,1)S(1)}, bf16[8,256]{1,0:T(8,128)(2,1)S(1)}, u32[]{:S(2)}, u32[]{:S(2)}) collective-permute-start(bf16[8,256]{1,0:T(8,128)(2,1)S(1)} %get-tuple-element.20), channel_id=1, source_target_pairs={{0,7},{1,6},{2,5},{3,4},{4,3},{5,2},{6,1},{7,0},{8,15},{9,14},{10,... | collective-permute-start | bytes 12296 | tf_op jit(solution)/shard_map/ppermute | solution.py:213
  11.4 0.1 collective-permute-start.4
  11.5 2.0 %collective-permute-start.5 = (bf16[8,256]{1,0:T(8,128)(2,1)S(1)}, bf16[8,256]{1,0:T(8,128)(2,1)S(1)}, u32[]{:S(2)}, u32[]{:S(2)}) collective-permute-start(bf16[8,256]{1,0:T(8,128)(2,1)S(1)} %get-tuple-element.22), channel_id=1, source_target_pairs={{0,3},{1,2},{2,1},{3,0},{4,7},{5,6},{6,5},{7,4},{8,11},{9,10},{10,... | collective-permute-start | bytes 12296 | tf_op jit(solution)/shard_map/ppermute | solution.py:213
  13.5 0.0 collective-permute-done.6
  13.5 1.7 %differ.1.refs_8_ = f32[32,128,256]{2,1,0:T(8,128)S(1)} custom-call(bf16[32,128,256]{2,1,0:T(8,128)(2,1)} %bitcast.9, bf16[32,128,256]{2,1,0:T(8,128)(2,1)S(1)} %bitcast.7), custom_call_target="tpu_custom_call" | custom-call | flops 1048576 | bytes 8388608 | tf_op jit(solution)/shard_map/differ/pallas_call | solution.py:156
  15.2 0.0 collective-permute-done.3.refs_0_
  15.2 0.1 collective-permute-done.4.refs_1_
  15.3 0.0 collective-permute-done.5.refs_2_
  15.3 1.0 %solve.1 = (bf16[16,256]{1,0:T(8,128)(2,1)S(1)}, bf16[16,256]{1,0:T(8,128)(2,1)S(1)}, bf16[16,256]{1,0:T(8,128)(2,1)S(1)}, bf16[16,256]{1,0:T(8,128)(2,1)S(1)}) custom-call(bf16[8,256]{1,0:T(8,128)(2,1)S(1)} %collective-permute-done.3.refs_0_, bf16[8,256]{1,0:T(8,128)(2,1)S(1)} %collective-permute-done.4.refs_1_, ...), custom_call_target="tpu_custom_call" | custom-call | flops 4194304 | bytes 4194304 | tf_op jit(solution)/shard_map/solve/pallas_call | solution.py:156
  16.3 2.0 %collective-permute-start.7 = (bf16[16,256]{1,0:T(8,128)(2,1)S(1)}, bf16[16,256]{1,0:T(8,128)(2,1)S(1)}, u32[]{:S(2)}, u32[]{:S(2)}) collective-permute-start(bf16[16,256]{1,0:T(8,128)(2,1)S(1)} %get-tuple-element.29), channel_id=1, source_target_pairs={{0,7},{1,6},{2,5},{3,4},{4,3},{5,2},{6,1},{7,0},{8,15},{9,14},{10,... | collective-permute-start | bytes 24584 | tf_op jit(solution)/shard_map/ppermute | solution.py:233
  18.3 0.8 %collective-permute-start.8 = (bf16[16,256]{1,0:T(8,128)(2,1)S(1)}, bf16[16,256]{1,0:T(8,128)(2,1)S(1)}, u32[]{:S(2)}, u32[]{:S(2)}) collective-permute-start(bf16[16,256]{1,0:T(8,128)(2,1)S(1)} %get-tuple-element.30), channel_id=1, source_target_pairs={{0,5},{1,4},{2,7},{3,6},{4,1},{5,0},{6,3},{7,2},{8,13},{9,12},{10,... | collective-permute-start | bytes 24584 | tf_op jit(solution)/shard_map/ppermute | solution.py:233
  19.1 1.4 %collective-permute-start.9 = (bf16[16,256]{1,0:T(8,128)(2,1)S(1)}, bf16[16,256]{1,0:T(8,128)(2,1)S(1)}, u32[]{:S(2)}, u32[]{:S(2)}) collective-permute-start(bf16[16,256]{1,0:T(8,128)(2,1)S(1)} %get-tuple-element.31), channel_id=1, source_target_pairs={{0,3},{1,2},{2,1},{3,0},{4,7},{5,6},{6,5},{7,4},{8,11},{9,10},{10,... | collective-permute-start | bytes 24584 | tf_op jit(solution)/shard_map/ppermute | solution.py:233
  20.6 0.7 %collective-permute-done.7 = bf16[16,256]{1,0:T(8,128)(2,1)S(1)} collective-permute-done((bf16[16,256]{1,0:T(8,128)(2,1)S(1)}, bf16[16,256]{1,0:T(8,128)(2,1)S(1)}, u32[]{:S(2)}, u32[]{:S(2)}) %collective-permute-start.7) | collective-permute-done | bytes 8224 | tf_op jit(solution)/shard_map/ppermute | solution.py:233
  21.2 1.1 %collective-permute-done.8 = bf16[16,256]{1,0:T(8,128)(2,1)S(1)} collective-permute-done((bf16[16,256]{1,0:T(8,128)(2,1)S(1)}, bf16[16,256]{1,0:T(8,128)(2,1)S(1)}, u32[]{:S(2)}, u32[]{:S(2)}) %collective-permute-start.8) | collective-permute-done | bytes 8224 | tf_op jit(solution)/shard_map/ppermute | solution.py:233
  22.3 0.0 collective-permute-done.9
  22.3 1.3 %collective-permute-start.10 = (bf16[4,16,256]{2,1,0:T(8,128)(2,1)S(1)}, bf16[4,16,256]{2,1,0:T(8,128)(2,1)S(1)}, u32[]{:S(2)}, u32[]{:S(2)}) collective-permute-start(bf16[4,16,256]{2,1,0:T(8,128)(2,1)S(1)} %pad_maximum_fusion.refs_0_), channel_id=1, source_target_pairs={{0,9},{1,8},{8,1},{9,0},{2,11},{3,10},{10,3},{11,2},{4,13},{5,12},... | collective-permute-start | bytes 98312 | tf_op jit(solution)/shard_map/ppermute | solution.py:237
  23.6 2.2 %collective-permute-done.10.refs_1_ = bf16[4,16,256]{2,1,0:T(8,128)(2,1)S(1)} collective-permute-done((bf16[4,16,256]{2,1,0:T(8,128)(2,1)S(1)}, bf16[4,16,256]{2,1,0:T(8,128)(2,1)S(1)}, u32[]{:S(2)}, u32[]{:S(2)}) %collective-permute-start.10) | collective-permute-done | bytes 32800 | tf_op jit(solution)/shard_map/ppermute | solution.py:237
  25.8 0.9 %place.1 = f32[120,1,256]{2,1,0:T(1,128)} custom-call(bf16[4,16,256]{2,1,0:T(8,128)(2,1)S(1)} %pad_maximum_fusion.refs_0_, bf16[4,16,256]{2,1,0:T(8,128)(2,1)S(1)} %collective-permute-done.10.refs_1_, f32[120,256]{1,0:T(8,128)S(1)} %get-tuple-element.32.refs_2_), custom_call_target="tpu_custom_call" | custom-call | flops 3932160 | bytes 245760 | tf_op jit(solution)/shard_map/place/pallas_call | solution.py:156
  (1 shorter events, 0.0 us)
Async XLA Ops:
  0.0 13.5 %collective-permute-start.6 = (bf16[4,8,1,128,256]{4,3,2,1,0:T(8,128)(2,1)}, bf16[4,8,1,128,256]{4,3,2,1,0:T(8,128)(2,1)S(1)}, u32[]{:S(2)}, u32[]{:S(2)}) collective-permute-start(bf16[4,8,1,128,256]{4,3,2,1,0:T(8,128)(2,1)} %param.6), channel_id=1, source_target_pairs={{0,1},{1,0},{2,3},{3,2},{4,5},{5,4},{6,7},{7,6},{8,9},{9,8},{10,11... | collective-permute-start | bytes 6291464 | tf_op jit(solution)/shard_map/ppermute | solution.py:184
  0.5 7.0 %collective-permute-start.1 = (s32[4,8]{1,0:T(4,128)}, s32[4,8]{1,0:T(4,128)S(1)}, u32[]{:S(2)}, u32[]{:S(2)}) collective-permute-start(s32[4,8]{1,0:T(4,128)} %refs_0_.1), channel_id=1, source_target_pairs={{0,7},{1,6},{2,5},{3,4},{4,3},{5,2},{6,1},{7,0},{8,15},{9,14},{10,... | collective-permute-start | bytes 392 | tf_op jit(solution)/shard_map/ppermute | solution.py:183
  5.2 4.1 %collective-permute-start = (s32[4,8]{1,0:T(4,128)}, s32[4,8]{1,0:T(4,128)S(1)}, u32[]{:S(2)}, u32[]{:S(2)}) collective-permute-start(s32[4,8]{1,0:T(4,128)} %refs_0_.1), channel_id=1, source_target_pairs={{0,5},{1,4},{2,7},{3,6},{4,1},{5,0},{6,3},{7,2},{8,13},{9,12},{10,... | collective-permute-start | bytes 392 | tf_op jit(solution)/shard_map/ppermute | solution.py:183
  5.2 4.1 %collective-permute-start.2 = (s32[4,8]{1,0:T(4,128)}, s32[4,8]{1,0:T(4,128)S(1)}, u32[]{:S(2)}, u32[]{:S(2)}) collective-permute-start(s32[4,8]{1,0:T(4,128)} %refs_0_.1), channel_id=1, source_target_pairs={{0,3},{1,2},{2,1},{3,0},{4,7},{5,6},{6,5},{7,4},{8,11},{9,10},{10,... | collective-permute-start | bytes 392 | tf_op jit(solution)/shard_map/ppermute | solution.py:183
  9.7 5.5 %collective-permute-start.3 = (bf16[8,256]{1,0:T(8,128)(2,1)S(1)}, bf16[8,256]{1,0:T(8,128)(2,1)S(1)}, u32[]{:S(2)}, u32[]{:S(2)}) collective-permute-start(bf16[8,256]{1,0:T(8,128)(2,1)S(1)} %get-tuple-element.20), channel_id=1, source_target_pairs={{0,7},{1,6},{2,5},{3,4},{4,3},{5,2},{6,1},{7,0},{8,15},{9,14},{10,... | collective-permute-start | bytes 12296 | tf_op jit(solution)/shard_map/ppermute | solution.py:213
  11.4 3.9 %collective-permute-start.4 = (bf16[8,256]{1,0:T(8,128)(2,1)S(1)}, bf16[8,256]{1,0:T(8,128)(2,1)S(1)}, u32[]{:S(2)}, u32[]{:S(2)}) collective-permute-start(bf16[8,256]{1,0:T(8,128)(2,1)S(1)} %get-tuple-element.21), channel_id=1, source_target_pairs={{0,5},{1,4},{2,7},{3,6},{4,1},{5,0},{6,3},{7,2},{8,13},{9,12},{10,... | collective-permute-start | bytes 12296 | tf_op jit(solution)/shard_map/ppermute | solution.py:213
  11.5 3.8 %collective-permute-start.5 = (bf16[8,256]{1,0:T(8,128)(2,1)S(1)}, bf16[8,256]{1,0:T(8,128)(2,1)S(1)}, u32[]{:S(2)}, u32[]{:S(2)}) collective-permute-start(bf16[8,256]{1,0:T(8,128)(2,1)S(1)} %get-tuple-element.22), channel_id=1, source_target_pairs={{0,3},{1,2},{2,1},{3,0},{4,7},{5,6},{6,5},{7,4},{8,11},{9,10},{10,... | collective-permute-start | bytes 12296 | tf_op jit(solution)/shard_map/ppermute | solution.py:213
  16.3 4.9 %collective-permute-start.7 = (bf16[16,256]{1,0:T(8,128)(2,1)S(1)}, bf16[16,256]{1,0:T(8,128)(2,1)S(1)}, u32[]{:S(2)}, u32[]{:S(2)}) collective-permute-start(bf16[16,256]{1,0:T(8,128)(2,1)S(1)} %get-tuple-element.29), channel_id=1, source_target_pairs={{0,7},{1,6},{2,5},{3,4},{4,3},{5,2},{6,1},{7,0},{8,15},{9,14},{10,... | collective-permute-start | bytes 24584 | tf_op jit(solution)/shard_map/ppermute | solution.py:233
  18.3 4.0 %collective-permute-start.8 = (bf16[16,256]{1,0:T(8,128)(2,1)S(1)}, bf16[16,256]{1,0:T(8,128)(2,1)S(1)}, u32[]{:S(2)}, u32[]{:S(2)}) collective-permute-start(bf16[16,256]{1,0:T(8,128)(2,1)S(1)} %get-tuple-element.30), channel_id=1, source_target_pairs={{0,5},{1,4},{2,7},{3,6},{4,1},{5,0},{6,3},{7,2},{8,13},{9,12},{10,... | collective-permute-start | bytes 24584 | tf_op jit(solution)/shard_map/ppermute | solution.py:233
  19.1 3.2 %collective-permute-start.9 = (bf16[16,256]{1,0:T(8,128)(2,1)S(1)}, bf16[16,256]{1,0:T(8,128)(2,1)S(1)}, u32[]{:S(2)}, u32[]{:S(2)}) collective-permute-start(bf16[16,256]{1,0:T(8,128)(2,1)S(1)} %get-tuple-element.31), channel_id=1, source_target_pairs={{0,3},{1,2},{2,1},{3,0},{4,7},{5,6},{6,5},{7,4},{8,11},{9,10},{10,... | collective-permute-start | bytes 24584 | tf_op jit(solution)/shard_map/ppermute | solution.py:233
  22.3 3.5 %collective-permute-start.10 = (bf16[4,16,256]{2,1,0:T(8,128)(2,1)S(1)}, bf16[4,16,256]{2,1,0:T(8,128)(2,1)S(1)}, u32[]{:S(2)}, u32[]{:S(2)}) collective-permute-start(bf16[4,16,256]{2,1,0:T(8,128)(2,1)S(1)} %pad_maximum_fusion.refs_0_), channel_id=1, source_target_pairs={{0,9},{1,8},{8,1},{9,0},{2,11},{3,10},{10,3},{11,2},{4,13},{5,12},... | collective-permute-start | bytes 98312 | tf_op jit(solution)/shard_map/ppermute | solution.py:237

commit v5 on v4

--- a/solution.py
+++ b/solution.py
@@ -9,6 +9,7 @@
 
 F32, BF16, I32 = jnp.float32, jnp.bfloat16, jnp.int32
 VMEM = pltpu.VMEM
+LANES = 128
 
 
 def iota(shape, dim):
@@ -53,23 +54,38 @@
         outs[k][...] = packed[k * cap : (k + 1) * cap].astype(BF16)
 
 
-def plan_kernel(cap, owners, *refs):
-    ins, outs, scratch = refs[:5], refs[5:12], refs[12:]
-    table_ref, own_ref, near_ref, far_ref, names_ref, turned_ref, damped_ref = outs
-    *held, sems = scratch
-    copies = [pltpu.make_async_copy(i, h, sems.at[j]) for j, (i, h) in enumerate(zip(ins, held))]
+def load_kernel(mascons, partials, *refs):
+    n = (len(refs) - 4) // 2
+    smalls, table, own, outs = refs[:n], refs[n], refs[n + 1], refs[n + 2 : 2 * n + 2]
+    held, sems = refs[2 * n + 2 :]
+    parts = sems.shape[0] - n - 1
+    step = table.shape[0] // parts
+    copies = []
+    for p in range(parts):
+        part = pl.ds(p * step, step)
+        copies.append(pltpu.make_async_copy(mascons.at[part], held.at[part], sems.at[p]))
+    for j, (i, o) in enumerate(zip((*smalls, partials), (*outs, own))):
+        copies.append(pltpu.make_async_copy(i, o, sems.at[parts + j]))
     for copy in copies:
         copy.start()
-    ids, observed, weights, prior, mascons = held
-    for copy in copies[:4]:
+    for p in range(parts):
+        copies[p].wait()
+        rows = slice(p * step, (p + 1) * step)
+        table[rows, :] = held[rows, 0, :].astype(BF16)
+    for copy in copies[parts:]:
         copy.wait()
+
+
+def plan_kernel(
+    cap, owners, ids, observed, weights, table, own_ref, near_ref, far_ref, names_ref, turned_ref
+):
     me = lax.axis_index("reg")
     sign = 1.0 - 2.0 * lax.axis_index("sat").astype(F32)
-    group = table_ref.shape[0]
+    group = table.shape[0]
     col = column([ids])
     count = col.shape[0]
+    own_ref[...] = rows_of(col - me * group, table) * sign
     owner = col // group
-    local = col - owner * group
     member = (owner == iota((count, owners), 1)).astype(F32)
     before = (iota((count, count), 1) < iota((count, count), 0)).astype(F32).astype(BF16)
     ahead = jnp.dot(before, member.astype(BF16), preferred_element_type=F32)
@@ -79,32 +95,16 @@
     spot = iota(near_ref.shape, 1)
     near = valid & (step > 0) & (spot == (owners - 1 - step) * cap + rank)
     far = (valid & (iota(far_ref.shape, 1) == step * cap + rank)).astype(F32)
-    width = names_ref.shape[1]
-    digit = jnp.where(iota((count, width), 1) < width // 2, local // 16, local % 16)
+    local = jnp.broadcast_to((col - owner * group - group // 2).astype(F32), (count, names_ref.shape[1]))
     near_ref[...] = near.astype(F32) * sign
     far_ref[...] = far * sign
-    names_ref[...] = transposed_dot(far.astype(BF16), digit.astype(F32).astype(BF16))
+    names_ref[...] = transposed_dot(far.astype(BF16), local.astype(BF16))
     turned_ref[...] = jnp.concatenate([observed[...], weights[...]], axis=0).T
-    copies[4].wait()
-    table_ref[...] = mascons[:, 0, :].astype(BF16)
-    own_ref[...] = rows_of(col - me * group, table_ref) * sign
-    share = damped_ref.shape[0]
-    block = lax.axis_index("arc") * lax.axis_size("sat") + lax.axis_index("sat")
-    damped_ref[...] = prior[...] * mascons[pl.ds(block * share, share), 0, :]
-
-
-def differ_kernel(own, other, out, held, sems):
-    parts = sems.shape[0]
-    step = out.shape[0] // parts
-    copies = []
-    for p in range(parts):
-        part = pl.ds(p * step, step)
-        copies.append(pltpu.make_async_copy(own.at[part], held.at[part], sems.at[p]))
-        copies[-1].start()
-    for p in range(parts):
-        copies[p].wait()
-        for i in range(p * step, (p + 1) * step):
-            out[i] = held[i].astype(F32) - other[i].astype(F32)
+
+
+def differ_kernel(own, other, out):
+    for i in range(out.shape[0]):
+        out[i] = own[i].astype(F32) - other[i].astype(F32)
 
 
 def solve_kernel(cap, owners, *refs):
@@ -130,25 +130,33 @@
     packed = transposed_dot(far_ref[...].astype(BF16), contribution)
     for k in range(owners):
         part = slice(k * cap, (k + 1) * cap)
-        outs[k][...] = jnp.concatenate([packed[part], names_ref[part, :]], axis=0).astype(BF16)
-
-
-def place_kernel(cap, *refs):
-    *arrived, damped, out = refs
+        outs[k][...] = jnp.concatenate([packed[part], names_ref[part, :]], axis=1).astype(BF16)
+
+
+def placed_rows(arrived, group, share, width):
+    block = lax.axis_index("arc") * lax.axis_size("sat") + lax.axis_index("sat")
+    got = jnp.concatenate([r[s].astype(F32) for r in arrived for s in range(r.shape[0])], axis=0)
+    local = got[:, width:].astype(I32) + group // 2 - block * share
+    local = jnp.concatenate([local] * -(-share // local.shape[1]), axis=1)
+    onehot = (local == iota(local.shape, 1)).astype(F32).astype(BF16)
+    return transposed_dot(onehot, got[:, :width].astype(BF16))[:share]
+
+
+def base_kernel(mascons, prior, *refs):
+    *arrived, out, held, sem = refs
+    share, width = out.shape
+    block = lax.axis_index("arc") * lax.axis_size("sat") + lax.axis_index("sat")
+    copy = pltpu.make_async_copy(mascons.at[pl.ds(block * share, share)], held, sem)
+    copy.start()
+    placed = placed_rows(arrived, mascons.shape[0], share, width) if arrived else 0.0
+    copy.wait()
+    out[...] = placed - prior[...] * held[:, 0, :]
+
+
+def place_kernel(group, *refs):
+    *arrived, base, out = refs
     share, _, width = out.shape
-    block = lax.axis_index("arc") * lax.axis_size("sat") + lax.axis_index("sat")
-    values, names = [], []
-    for ref in arrived:
-        for s in range(ref.shape[0]):
-            got = ref[s].astype(F32)
-            values.append(got[:cap])
-            names.append(got[cap:, : width // 2] * 16.0 + got[cap:, width // 2 :])
-    values = jnp.concatenate(values, axis=0).astype(BF16)
-    local = jnp.concatenate(names, axis=0).astype(I32)
-    local = jnp.concatenate([local] * -(-share // local.shape[1]), axis=1)
-    onehot = (local - block * share == iota(local.shape, 1)).astype(F32).astype(BF16)
-    total = transposed_dot(onehot, values)
-    out[:, 0, :] = total[:share] - damped[...]
+    out[:, 0, :] = base[...] + placed_rows(arrived, group, share, width)
 
 
 def call(kernel, name, outs, args, flops, size, scratch=(), anywhere=()):
@@ -178,29 +186,22 @@
         return [(r * 2 + s, (r ^ k) * 2 + (1 - s)) for r in range(owners) for s in range(2)]
 
     names = ("reg", "sat")
+    share = group // (blocks * lax.axis_size("sat"))
+    whole = (count, epochs, width)
+    dma = pltpu.SemaphoreType.DMA
     far_first = list(range(owners - 1, 0, -1))
-    askers = far_first[1:2] + far_first[:1] + far_first[2:]
-    asked = [lax.ppermute(regions, names, crossing(k)) for k in askers]
+    asked = [lax.ppermute(regions, names, crossing(k)) for k in far_first]
     other = lax.ppermute(partials, "sat", [(0, 1), (1, 0)])
-    share = group // (blocks * lax.axis_size("sat"))
-    inputs = [regions, observed, weights, prior.reshape(1, width), mascons]
-    table, own, near, far, named, turned, damped = call(
-        functools.partial(plan_kernel, cap, owners),
-        "plan",
-        [
-            shape((group, width), BF16),
-            shape((count, width), F32),
-            shape((count, (owners - 1) * cap), F32),
-            shape((count, owners * cap), F32),
-            shape((owners * cap, width), F32),
-            shape((epochs, 2 * arcs), F32),
-            shape((share, width), F32),
-        ],
-        inputs,
-        count * count * width,
+    smalls = [regions, observed, weights]
+    table, own_partials, ids, residuals, precisions = call(
+        load_kernel,
+        "load",
+        [shape((group, width), BF16), shape(whole, BF16), *(shape(i.shape, i.dtype) for i in smalls)],
+        [mascons, partials.reshape(whole), *smalls],
+        group * width,
         group * width * 4,
-        [*(VMEM(i.shape, i.dtype) for i in inputs), pltpu.SemaphoreType.DMA((len(inputs),))],
-        range(len(inputs)),
+        [VMEM(mascons.shape, F32), dma((4 + 1 + len(smalls),))],
+        range(2 + len(smalls)),
     )
     found = call(
         functools.partial(lookup_kernel, cap),
@@ -210,22 +211,34 @@
         2 * owners * count * group * width,
         group * width * 4,
     )
-    came = [lax.ppermute(found[askers.index(k)], names, crossing(k)) for k in far_first]
-    whole = (count, epochs, width)
+    came = [lax.ppermute(found[far_first.index(k)], names, crossing(k)) for k in far_first]
+    ids, _ = lax.optimization_barrier((ids, found[-1]))
+    own, near, far, named, turned = call(
+        functools.partial(plan_kernel, cap, owners),
+        "plan",
+        [
+            shape((count, width), F32),
+            shape((count, (owners - 1) * cap), F32),
+            shape((count, owners * cap), F32),
+            shape((owners * cap, LANES), F32),
+            shape((epochs, 2 * arcs), F32),
+        ],
+        [ids, residuals, precisions, table],
+        count * count * width,
+        count * width * 4,
+    )
     diff = call(
         differ_kernel,
         "differ",
         shape(whole, F32),
-        [partials.reshape(whole), other.reshape(whole)],
+        [own_partials, other.reshape(whole)],
         count * epochs * width,
         count * epochs * width * 8,
-        [VMEM(whole, BF16), pltpu.SemaphoreType.DMA((4,))],
-        (0,),
     )
     sent = call(
         functools.partial(solve_kernel, cap, owners),
         "solve",
-        [shape((2 * cap, width), BF16)] * owners,
+        [shape((cap, width + LANES), BF16)] * owners,
         [*came, own, near, far, named, turned, diff],
         4 * count * epochs * width,
         count * epochs * width * 4,
@@ -234,14 +247,24 @@
     mine = jnp.stack(mine)
     if blocks == 2:
         over = [(a * 2 + s, (1 - a) * 2 + (1 - s)) for a in range(2) for s in range(2)]
-        arrived = [mine, lax.ppermute(mine, ("arc", "sat"), over)]
+        early, late = [mine], [lax.ppermute(mine, ("arc", "sat"), over)]
     else:
-        arrived = [lax.all_gather(mine, "arc", tiled=True)]
+        early, late = [], [lax.all_gather(mine, "arc", tiled=True)]
+    base = call(
+        base_kernel,
+        "base",
+        shape((share, width), F32),
+        [mascons, prior.reshape(1, width), *early],
+        2 * share * width * count,
+        share * width * 8,
+        [VMEM((share, 1, width), F32), dma],
+        (0,),
+    )
     return call(
-        functools.partial(place_kernel, cap),
+        functools.partial(place_kernel, group),
         "place",
         shape((share, 1, width), F32),
-        [*arrived, damped],
+        [*late, base],
         2 * share * width * blocks * count,
         share * width * 8,
     )

time: 26.8 us -> 26.5 us (0.989)
  starting transfers between devices: 14.7 us -> 14.3 us
    ppermute x3, starting transfers between devices: 4.23 us -> 3.84 us  [per_device(): lax.ppermute(sent[k], names, crossing(k))]
    pallas_call x5 -> x7, Pallas kernels: 6 us -> 6.15 us  [call(): pl.pallas_call(kernel, out_shape=outs, in_specs=[raw if i in anywhere els...]
  transfers between devices with their start and end apart: 11 -> 11, of which waited for: 5 -> 6; matrix products, arithmetic and copies ran while one was open for 0% -> 0% of each run, Pallas kernels for 15% -> 16%
where the time goes in v5:
time: 26.5 us; the launch traced here: 26.4 us
  starting transfers between devices  14.3 us (54%)
  Pallas kernels  6.15 us (23%)
  waiting for transfers between devices  5.89 us (22%)
    pallas_call x7, Pallas kernels, call(): pl.pallas_call(kernel, out_shape=outs, in_specs=[raw if i in anywhere els...  6.15 us
    ppermute x3, starting transfers between devices, per_device(): asked = [lax.ppermute(regions, names, crossing(k)) for k in far_first]  4.89 us
    ppermute x3, starting transfers between devices, per_device(): lax.ppermute(found[far_first.index(k)], names, crossing(k))  3.84 us
    ppermute x3, starting transfers between devices, per_device(): lax.ppermute(sent[k], names, crossing(k))  3.84 us
    ppermute x3, waiting for transfers between devices, per_device(): lax.ppermute(sent[k], names, crossing(k))  2.01 us
    ppermute x3, waiting for transfers between devices, per_device(): asked = [lax.ppermute(regions, names, crossing(k)) for k in far_first]  1.85 us
    ppermute x1, starting transfers between devices, per_device(): early, late = ([mine], [lax.ppermute(mine, ('arc', 'sat'), over)])  1.25 us
    ppermute x1, waiting for transfers between devices, per_device(): early, late = ([mine], [lax.ppermute(mine, ('arc', 'sat'), over)])  1.09 us
  transfers between devices with their start and end apart: 11, of which 6 were waited for; matrix products, arithmetic and copies ran while one was open for 0% of the time, Pallas kernels for 16%

profile of v5, /device:TPU:0, one launch (start us, length us, event | category | flops | bytes accessed | tf_op | source)
XLA Modules:
  0.0 26.4 jit_solution(11641860152972241375)
XLA Ops:
  0.0 0.5 %collective-permute-start.6 = (bf16[4,8,1,128,256]{4,3,2,1,0:T(8,128)(2,1)}, bf16[4,8,1,128,256]{4,3,2,1,0:T(8,128)(2,1)S(1)}, u32[]{:S(2)}, u32[]{:S(2)}) collective-permute-start(bf16[4,8,1,128,256]{4,3,2,1,0:T(8,128)(2,1)} %param.6), channel_id=1, source_target_pairs={{0,1},{1,0},{2,3},{3,2},{4,5},{5,4},{6,7},{7,6},{8,9},{9,8},{10,11... | collective-permute-start | bytes 6291464 | tf_op jit(solution)/shard_map/ppermute | solution.py:194
  0.5 3.7 %collective-permute-start.1 = (s32[4,8]{1,0:T(4,128)}, s32[4,8]{1,0:T(4,128)S(1)}, u32[]{:S(2)}, u32[]{:S(2)}) collective-permute-start(s32[4,8]{1,0:T(4,128)} %refs_0_.1), channel_id=1, source_target_pairs={{0,5},{1,4},{2,7},{3,6},{4,1},{5,0},{6,3},{7,2},{8,13},{9,12},{10,... | collective-permute-start | bytes 392 | tf_op jit(solution)/shard_map/ppermute | solution.py:193
  4.2 1.0 %collective-permute-start = (s32[4,8]{1,0:T(4,128)}, s32[4,8]{1,0:T(4,128)S(1)}, u32[]{:S(2)}, u32[]{:S(2)}) collective-permute-start(s32[4,8]{1,0:T(4,128)} %refs_0_.1), channel_id=1, source_target_pairs={{0,7},{1,6},{2,5},{3,4},{4,3},{5,2},{6,1},{7,0},{8,15},{9,14},{10,... | collective-permute-start | bytes 392 | tf_op jit(solution)/shard_map/ppermute | solution.py:193
  5.2 0.2 collective-permute-start.2
  5.3 2.0 %load.1 = (bf16[480,256]{1,0:T(8,128)(2,1)S(1)}, bf16[32,128,256]{2,1,0:T(8,128)(2,1)S(1)}, s32[4,8]{1,0:T(4,128)S(1)}, f32[4,128]{1,0:T(4,128)S(1)}, f32[4,128]{1,0:T(4,128)S(1)}) custom-call(f32[480,1,256]{2,1,0:T(1,128)} %mascons.3, bf16[32,128,256]{2,1,0:T(8,128)(2,1)} %bitcast.10, s32[4,8]{1,0:T(4,128)} %refs_0_.1, f32[4,128]{1,0:T(4,128)} %refs_1_.1, ...), custom_call_target="tpu_custom_call" | custom-call | flops 122880 | bytes 491520 | tf_op jit(solution)/shard_map/load/pallas_call | solution.py:164
  7.3 0.0 collective-permute-done.1.refs_1_
  7.3 1.8 %collective-permute-done.refs_0_ = s32[4,8]{1,0:T(4,128)S(1)} collective-permute-done((s32[4,8]{1,0:T(4,128)}, s32[4,8]{1,0:T(4,128)S(1)}, u32[]{:S(2)}, u32[]{:S(2)}) %collective-permute-start) | collective-permute-done | bytes 160 | tf_op jit(solution)/shard_map/ppermute | solution.py:193
  9.2 0.0 collective-permute-done.2.refs_2_
  9.2 0.4 %lookup.1 = (bf16[8,256]{1,0:T(8,128)(2,1)S(1)}, bf16[8,256]{1,0:T(8,128)(2,1)S(1)}, bf16[8,256]{1,0:T(8,128)(2,1)S(1)}) custom-call(s32[4,8]{1,0:T(4,128)S(1)} %collective-permute-done.refs_0_, s32[4,8]{1,0:T(4,128)S(1)} %collective-permute-done.1.refs_1_, s32[4,8]{1,0:T(4,128)S(1)} %collective-permute-done.2.refs_2_, ...), custom_call_target="tpu_custom_call" | custom-call | flops 31457280 | bytes 491520 | tf_op jit(solution)/shard_map/lookup/pallas_call | solution.py:164
  9.6 1.8 %collective-permute-start.3 = (bf16[8,256]{1,0:T(8,128)(2,1)S(1)}, bf16[8,256]{1,0:T(8,128)(2,1)S(1)}, u32[]{:S(2)}, u32[]{:S(2)}) collective-permute-start(bf16[8,256]{1,0:T(8,128)(2,1)S(1)} %get-tuple-element.24), channel_id=1, source_target_pairs={{0,7},{1,6},{2,5},{3,4},{4,3},{5,2},{6,1},{7,0},{8,15},{9,14},{10,... | collective-permute-start | bytes 12296 | tf_op jit(solution)/shard_map/ppermute | solution.py:214
  11.3 0.0 collective-permute-start.4
  11.3 2.1 %collective-permute-start.5 = (bf16[8,256]{1,0:T(8,128)(2,1)S(1)}, bf16[8,256]{1,0:T(8,128)(2,1)S(1)}, u32[]{:S(2)}, u32[]{:S(2)}) collective-permute-start(bf16[8,256]{1,0:T(8,128)(2,1)S(1)} %get-tuple-element.26), channel_id=1, source_target_pairs={{0,3},{1,2},{2,1},{3,0},{4,7},{5,6},{6,5},{7,4},{8,11},{9,10},{10,... | collective-permute-start | bytes 12296 | tf_op jit(solution)/shard_map/ppermute | solution.py:214
  13.4 0.5 %plan.1 = (f32[32,256]{1,0:T(8,128)S(1)}, f32[32,24]{1,0:T(8,128)S(1)}, f32[32,32]{1,0:T(8,128)S(1)}, f32[32,128]{1,0:T(8,128)S(1)}, f32[128,8]{1,0:T(8,128)S(1)}) custom-call(s32[4,8]{1,0:T(4,128)S(1)} %get-tuple-element.28.ids, f32[4,128]{1,0:T(4,128)S(1)} %get-tuple-element.29.observed, f32[4,128]{1,0:T(4,128)S(1)} %get-tuple-element.30.weights, ...), custom_call_target="tpu_custom_call" | custom-call | flops 262144 | bytes 32768 | tf_op jit(solution)/shard_map/plan/pallas_call | solution.py:164
  13.9 0.0 collective-permute-done.6
  13.9 0.4 %differ.1.refs_8_ = f32[32,128,256]{2,1,0:T(8,128)S(1)} custom-call(bf16[32,128,256]{2,1,0:T(8,128)(2,1)S(1)} %get-tuple-element.36.own, bf16[32,128,256]{2,1,0:T(8,128)(2,1)S(1)} %bitcast.7), custom_call_target="tpu_custom_call" | custom-call | flops 1048576 | bytes 8388608 | tf_op jit(solution)/shard_map/differ/pallas_call | solution.py:164
  14.3 0.1 collective-permute-done.3.refs_0_
  14.4 0.8 %collective-permute-done.4.refs_1_ = bf16[8,256]{1,0:T(8,128)(2,1)S(1)} collective-permute-done((bf16[8,256]{1,0:T(8,128)(2,1)S(1)}, bf16[8,256]{1,0:T(8,128)(2,1)S(1)}, u32[]{:S(2)}, u32[]{:S(2)}) %collective-permute-start.4) | collective-permute-done | bytes 4128 | tf_op jit(solution)/shard_map/ppermute | solution.py:214
  15.3 0.0 collective-permute-done.5.refs_2_
  15.3 0.0 copy-start
  15.3 1.0 %solve.1 = (bf16[8,384]{1,0:T(8,128)(2,1)S(1)}, bf16[8,384]{1,0:T(8,128)(2,1)S(1)}, bf16[8,384]{1,0:T(8,128)(2,1)S(1)}, bf16[8,384]{1,0:T(8,128)(2,1)S(1)}) custom-call(bf16[8,256]{1,0:T(8,128)(2,1)S(1)} %collective-permute-done.3.refs_0_, bf16[8,256]{1,0:T(8,128)(2,1)S(1)} %collective-permute-done.4.refs_1_, ...), custom_call_target="tpu_custom_call" | custom-call | flops 4194304 | bytes 4194304 | tf_op jit(solution)/shard_map/solve/pallas_call | solution.py:164
  16.3 1.9 %collective-permute-start.7 = (bf16[8,384]{1,0:T(8,128)(2,1)S(1)}, bf16[8,384]{1,0:T(8,128)(2,1)S(1)}, u32[]{:S(2)}, u32[]{:S(2)}) collective-permute-start(bf16[8,384]{1,0:T(8,128)(2,1)S(1)} %get-tuple-element.38), channel_id=1, source_target_pairs={{0,7},{1,6},{2,5},{3,4},{4,3},{5,2},{6,1},{7,0},{8,15},{9,14},{10,... | collective-permute-start | bytes 18440 | tf_op jit(solution)/shard_map/ppermute | solution.py:246
  18.2 0.9 %collective-permute-start.8 = (bf16[8,384]{1,0:T(8,128)(2,1)S(1)}, bf16[8,384]{1,0:T(8,128)(2,1)S(1)}, u32[]{:S(2)}, u32[]{:S(2)}) collective-permute-start(bf16[8,384]{1,0:T(8,128)(2,1)S(1)} %get-tuple-element.39), channel_id=1, source_target_pairs={{0,5},{1,4},{2,7},{3,6},{4,1},{5,0},{6,3},{7,2},{8,13},{9,12},{10,... | collective-permute-start | bytes 18440 | tf_op jit(solution)/shard_map/ppermute | solution.py:246
  19.0 1.1 %collective-permute-start.9 = (bf16[8,384]{1,0:T(8,128)(2,1)S(1)}, bf16[8,384]{1,0:T(8,128)(2,1)S(1)}, u32[]{:S(2)}, u32[]{:S(2)}) collective-permute-start(bf16[8,384]{1,0:T(8,128)(2,1)S(1)} %get-tuple-element.40), channel_id=1, source_target_pairs={{0,3},{1,2},{2,1},{3,0},{4,7},{5,6},{6,5},{7,4},{8,11},{9,10},{10,... | collective-permute-start | bytes 18440 | tf_op jit(solution)/shard_map/ppermute | solution.py:246
  20.2 1.0 %collective-permute-done.7 = bf16[8,384]{1,0:T(8,128)(2,1)S(1)} collective-permute-done((bf16[8,384]{1,0:T(8,128)(2,1)S(1)}, bf16[8,384]{1,0:T(8,128)(2,1)S(1)}, u32[]{:S(2)}, u32[]{:S(2)}) %collective-permute-start.7) | collective-permute-done | bytes 6176 | tf_op jit(solution)/shard_map/ppermute | solution.py:246
  21.2 1.0 %collective-permute-done.8 = bf16[8,384]{1,0:T(8,128)(2,1)S(1)} collective-permute-done((bf16[8,384]{1,0:T(8,128)(2,1)S(1)}, bf16[8,384]{1,0:T(8,128)(2,1)S(1)}, u32[]{:S(2)}, u32[]{:S(2)}) %collective-permute-start.8) | collective-permute-done | bytes 6176 | tf_op jit(solution)/shard_map/ppermute | solution.py:246
  22.2 0.0 collective-permute-done.9
  22.2 1.2 %collective-permute-start.10 = (bf16[4,8,384]{2,1,0:T(8,128)(2,1)S(1)}, bf16[4,8,384]{2,1,0:T(8,128)(2,1)S(1)}, u32[]{:S(2)}, u32[]{:S(2)}) collective-permute-start(bf16[4,8,384]{2,1,0:T(8,128)(2,1)S(1)} %pad_maximum_fusion.refs_0_), channel_id=1, source_target_pairs={{0,9},{1,8},{8,1},{9,0},{2,11},{3,10},{10,3},{11,2},{4,13},{5,12},... | collective-permute-start | bytes 73736 | tf_op jit(solution)/shard_map/ppermute | solution.py:250
  23.4 0.0 copy-done
  23.4 1.0 %base.1.refs_1_ = f32[120,256]{1,0:T(8,128)S(1)} custom-call(f32[480,1,256]{2,1,0:T(1,128)} %mascons.3, f32[1,256]{1,0:T(1,128)S(1)} %bitcast.9, bf16[4,8,384]{2,1,0:T(8,128)(2,1)S(1)} %pad_maximum_fusion.refs_0_), custom_call_target="tpu_custom_call" | custom-call | flops 1966080 | bytes 245760 | tf_op jit(solution)/shard_map/base/pallas_call | solution.py:164
  24.4 1.1 %collective-permute-done.10.refs_0_ = bf16[4,8,384]{2,1,0:T(8,128)(2,1)S(1)} collective-permute-done((bf16[4,8,384]{2,1,0:T(8,128)(2,1)S(1)}, bf16[4,8,384]{2,1,0:T(8,128)(2,1)S(1)}, u32[]{:S(2)}, u32[]{:S(2)}) %collective-permute-start.10) | collective-permute-done | bytes 24608 | tf_op jit(solution)/shard_map/ppermute | solution.py:250
  25.5 0.9 %place.1 = f32[120,1,256]{2,1,0:T(1,128)} custom-call(bf16[4,8,384]{2,1,0:T(8,128)(2,1)S(1)} %collective-permute-done.10.refs_0_, f32[120,256]{1,0:T(8,128)S(1)} %base.1.refs_1_), custom_call_target="tpu_custom_call" | custom-call | flops 3932160 | bytes 245760 | tf_op jit(solution)/shard_map/place/pallas_call | solution.py:164
  (1 shorter events, 0.0 us)
Async XLA Ops:
  0.0 13.9 %collective-permute-start.6 = (bf16[4,8,1,128,256]{4,3,2,1,0:T(8,128)(2,1)}, bf16[4,8,1,128,256]{4,3,2,1,0:T(8,128)(2,1)S(1)}, u32[]{:S(2)}, u32[]{:S(2)}) collective-permute-start(bf16[4,8,1,128,256]{4,3,2,1,0:T(8,128)(2,1)} %param.6), channel_id=1, source_target_pairs={{0,1},{1,0},{2,3},{3,2},{4,5},{5,4},{6,7},{7,6},{8,9},{9,8},{10,11... | collective-permute-start | bytes 6291464 | tf_op jit(solution)/shard_map/ppermute | solution.py:194
  0.5 6.9 %collective-permute-start.1 = (s32[4,8]{1,0:T(4,128)}, s32[4,8]{1,0:T(4,128)S(1)}, u32[]{:S(2)}, u32[]{:S(2)}) collective-permute-start(s32[4,8]{1,0:T(4,128)} %refs_0_.1), channel_id=1, source_target_pairs={{0,5},{1,4},{2,7},{3,6},{4,1},{5,0},{6,3},{7,2},{8,13},{9,12},{10,... | collective-permute-start | bytes 392 | tf_op jit(solution)/shard_map/ppermute | solution.py:193
  4.2 5.0 %collective-permute-start = (s32[4,8]{1,0:T(4,128)}, s32[4,8]{1,0:T(4,128)S(1)}, u32[]{:S(2)}, u32[]{:S(2)}) collective-permute-start(s32[4,8]{1,0:T(4,128)} %refs_0_.1), channel_id=1, source_target_pairs={{0,7},{1,6},{2,5},{3,4},{4,3},{5,2},{6,1},{7,0},{8,15},{9,14},{10,... | collective-permute-start | bytes 392 | tf_op jit(solution)/shard_map/ppermute | solution.py:193
  5.2 4.0 %collective-permute-start.2 = (s32[4,8]{1,0:T(4,128)}, s32[4,8]{1,0:T(4,128)S(1)}, u32[]{:S(2)}, u32[]{:S(2)}) collective-permute-start(s32[4,8]{1,0:T(4,128)} %refs_0_.1), channel_id=1, source_target_pairs={{0,3},{1,2},{2,1},{3,0},{4,7},{5,6},{6,5},{7,4},{8,11},{9,10},{10,... | collective-permute-start | bytes 392 | tf_op jit(solution)/shard_map/ppermute | solution.py:193
  9.6 4.8 %collective-permute-start.3 = (bf16[8,256]{1,0:T(8,128)(2,1)S(1)}, bf16[8,256]{1,0:T(8,128)(2,1)S(1)}, u32[]{:S(2)}, u32[]{:S(2)}) collective-permute-start(bf16[8,256]{1,0:T(8,128)(2,1)S(1)} %get-tuple-element.24), channel_id=1, source_target_pairs={{0,7},{1,6},{2,5},{3,4},{4,3},{5,2},{6,1},{7,0},{8,15},{9,14},{10,... | collective-permute-start | bytes 12296 | tf_op jit(solution)/shard_map/ppermute | solution.py:214
  11.3 3.9 %collective-permute-start.4 = (bf16[8,256]{1,0:T(8,128)(2,1)S(1)}, bf16[8,256]{1,0:T(8,128)(2,1)S(1)}, u32[]{:S(2)}, u32[]{:S(2)}) collective-permute-start(bf16[8,256]{1,0:T(8,128)(2,1)S(1)} %get-tuple-element.25), channel_id=1, source_target_pairs={{0,5},{1,4},{2,7},{3,6},{4,1},{5,0},{6,3},{7,2},{8,13},{9,12},{10,... | collective-permute-start | bytes 12296 | tf_op jit(solution)/shard_map/ppermute | solution.py:214
  11.3 3.9 %collective-permute-start.5 = (bf16[8,256]{1,0:T(8,128)(2,1)S(1)}, bf16[8,256]{1,0:T(8,128)(2,1)S(1)}, u32[]{:S(2)}, u32[]{:S(2)}) collective-permute-start(bf16[8,256]{1,0:T(8,128)(2,1)S(1)} %get-tuple-element.26), channel_id=1, source_target_pairs={{0,3},{1,2},{2,1},{3,0},{4,7},{5,6},{6,5},{7,4},{8,11},{9,10},{10,... | collective-permute-start | bytes 12296 | tf_op jit(solution)/shard_map/ppermute | solution.py:214
  15.3 8.1 %copy-start = (f32[256]{0:T(256)S(1)}, f32[256]{0:T(256)}, u32[]{:S(2)}) copy-start(f32[256]{0:T(256)} %param.11) | copy-start | bytes 3076
  16.3 4.9 %collective-permute-start.7 = (bf16[8,384]{1,0:T(8,128)(2,1)S(1)}, bf16[8,384]{1,0:T(8,128)(2,1)S(1)}, u32[]{:S(2)}, u32[]{:S(2)}) collective-permute-start(bf16[8,384]{1,0:T(8,128)(2,1)S(1)} %get-tuple-element.38), channel_id=1, source_target_pairs={{0,7},{1,6},{2,5},{3,4},{4,3},{5,2},{6,1},{7,0},{8,15},{9,14},{10,... | collective-permute-start | bytes 18440 | tf_op jit(solution)/shard_map/ppermute | solution.py:246
  18.2 4.0 %collective-permute-start.8 = (bf16[8,384]{1,0:T(8,128)(2,1)S(1)}, bf16[8,384]{1,0:T(8,128)(2,1)S(1)}, u32[]{:S(2)}, u32[]{:S(2)}) collective-permute-start(bf16[8,384]{1,0:T(8,128)(2,1)S(1)} %get-tuple-element.39), channel_id=1, source_target_pairs={{0,5},{1,4},{2,7},{3,6},{4,1},{5,0},{6,3},{7,2},{8,13},{9,12},{10,... | collective-permute-start | bytes 18440 | tf_op jit(solution)/shard_map/ppermute | solution.py:246
  19.0 3.1 %collective-permute-start.9 = (bf16[8,384]{1,0:T(8,128)(2,1)S(1)}, bf16[8,384]{1,0:T(8,128)(2,1)S(1)}, u32[]{:S(2)}, u32[]{:S(2)}) collective-permute-start(bf16[8,384]{1,0:T(8,128)(2,1)S(1)} %get-tuple-element.40), channel_id=1, source_target_pairs={{0,3},{1,2},{2,1},{3,0},{4,7},{5,6},{6,5},{7,4},{8,11},{9,10},{10,... | collective-permute-start | bytes 18440 | tf_op jit(solution)/shard_map/ppermute | solution.py:246
  22.2 3.3 %collective-permute-start.10 = (bf16[4,8,384]{2,1,0:T(8,128)(2,1)S(1)}, bf16[4,8,384]{2,1,0:T(8,128)(2,1)S(1)}, u32[]{:S(2)}, u32[]{:S(2)}) collective-permute-start(bf16[4,8,384]{2,1,0:T(8,128)(2,1)S(1)} %pad_maximum_fusion.refs_0_), channel_id=1, source_target_pairs={{0,9},{1,8},{8,1},{9,0},{2,11},{3,10},{10,3},{11,2},{4,13},{5,12},... | collective-permute-start | bytes 73736 | tf_op jit(solution)/shard_map/ppermute | solution.py:250

commit v6 on v5

--- a/solution.py
+++ b/solution.py
@@ -54,17 +54,17 @@
         outs[k][...] = packed[k * cap : (k + 1) * cap].astype(BF16)
 
 
-def load_kernel(mascons, partials, *refs):
-    n = (len(refs) - 4) // 2
-    smalls, table, own, outs = refs[:n], refs[n], refs[n + 1], refs[n + 2 : 2 * n + 2]
-    held, sems = refs[2 * n + 2 :]
-    parts = sems.shape[0] - n - 1
+def load_kernel(mascons, *refs):
+    n = (len(refs) - 3) // 2
+    smalls, table, outs = refs[:n], refs[n], refs[n + 1 : 2 * n + 1]
+    held, sems = refs[2 * n + 1 :]
+    parts = sems.shape[0] - n
     step = table.shape[0] // parts
     copies = []
     for p in range(parts):
         part = pl.ds(p * step, step)
         copies.append(pltpu.make_async_copy(mascons.at[part], held.at[part], sems.at[p]))
-    for j, (i, o) in enumerate(zip((*smalls, partials), (*outs, own))):
+    for j, (i, o) in enumerate(zip(smalls, outs)):
         copies.append(pltpu.make_async_copy(i, o, sems.at[parts + j]))
     for copy in copies:
         copy.start()
@@ -76,9 +76,15 @@
         copy.wait()
 
 
-def plan_kernel(
-    cap, owners, ids, observed, weights, table, own_ref, near_ref, far_ref, names_ref, turned_ref
-):
+def plan_kernel(cap, owners, order, ids, observed, weights, table, mine, other, *refs):
+    own_ref, near_ref, far_ref, names_ref, turned_ref, diff, held, sems = refs
+    parts = sems.shape[0]
+    size = diff.shape[0] // parts
+    copies = []
+    for p in range(parts):
+        part = pl.ds(p * size, size)
+        copies.append(pltpu.make_async_copy(mine.at[part], held.at[part], sems.at[p]))
+        copies[-1].start()
     me = lax.axis_index("reg")
     sign = 1.0 - 2.0 * lax.axis_index("sat").astype(F32)
     group = table.shape[0]
@@ -93,18 +99,18 @@
     valid = owner < owners
     step = owner ^ me
     spot = iota(near_ref.shape, 1)
-    near = valid & (step > 0) & (spot == (owners - 1 - step) * cap + rank)
+    turn = sum(jnp.where(step == k, j * cap, 0) for j, k in enumerate(order))
+    near = valid & (step > 0) & (spot == turn + rank)
     far = (valid & (iota(far_ref.shape, 1) == step * cap + rank)).astype(F32)
     local = jnp.broadcast_to((col - owner * group - group // 2).astype(F32), (count, names_ref.shape[1]))
     near_ref[...] = near.astype(F32) * sign
     far_ref[...] = far * sign
     names_ref[...] = transposed_dot(far.astype(BF16), local.astype(BF16))
     turned_ref[...] = jnp.concatenate([observed[...], weights[...]], axis=0).T
-
-
-def differ_kernel(own, other, out):
-    for i in range(out.shape[0]):
-        out[i] = own[i].astype(F32) - other[i].astype(F32)
+    for p in range(parts):
+        copies[p].wait()
+        for i in range(p * size, (p + 1) * size):
+            diff[i] = held[i].astype(F32) - other[i].astype(F32)
 
 
 def solve_kernel(cap, owners, *refs):
@@ -190,31 +196,37 @@
     whole = (count, epochs, width)
     dma = pltpu.SemaphoreType.DMA
     far_first = list(range(owners - 1, 0, -1))
-    asked = [lax.ppermute(regions, names, crossing(k)) for k in far_first]
+    order = far_first[::-1]
+    asked = {k: lax.ppermute(regions, names, crossing(k)) for k in far_first}
     other = lax.ppermute(partials, "sat", [(0, 1), (1, 0)])
     smalls = [regions, observed, weights]
-    table, own_partials, ids, residuals, precisions = call(
+    table, ids, residuals, precisions = call(
         load_kernel,
         "load",
-        [shape((group, width), BF16), shape(whole, BF16), *(shape(i.shape, i.dtype) for i in smalls)],
-        [mascons, partials.reshape(whole), *smalls],
+        [shape((group, width), BF16), *(shape(i.shape, i.dtype) for i in smalls)],
+        [mascons, *smalls],
         group * width,
         group * width * 4,
-        [VMEM(mascons.shape, F32), dma((4 + 1 + len(smalls),))],
-        range(2 + len(smalls)),
-    )
-    found = call(
-        functools.partial(lookup_kernel, cap),
-        "lookup",
-        [shape((cap, width), BF16)] * (owners - 1),
-        [*asked, table],
-        2 * owners * count * group * width,
-        group * width * 4,
-    )
-    came = [lax.ppermute(found[far_first.index(k)], names, crossing(k)) for k in far_first]
-    ids, _ = lax.optimization_barrier((ids, found[-1]))
-    own, near, far, named, turned = call(
-        functools.partial(plan_kernel, cap, owners),
+        [VMEM(mascons.shape, F32), dma((4 + len(smalls),))],
+        range(1 + len(smalls)),
+    )
+    found = {}
+    for some in filter(None, (far_first[1:2], far_first[:1] + far_first[2:])):
+        found |= zip(
+            some,
+            call(
+                functools.partial(lookup_kernel, cap),
+                "lookup",
+                [shape((cap, width), BF16)] * len(some),
+                [*(asked[k] for k in some), table],
+                2 * len(some) * count * group * width,
+                group * width * 4,
+            ),
+        )
+    came = [lax.ppermute(found[k], names, crossing(k)) for k in order]
+    ids, _ = lax.optimization_barrier((ids, found[order[0]]))
+    own, near, far, named, turned, diff = call(
+        functools.partial(plan_kernel, cap, owners, order),
         "plan",
         [
             shape((count, width), F32),
@@ -222,18 +234,13 @@
             shape((count, owners * cap), F32),
             shape((owners * cap, LANES), F32),
             shape((epochs, 2 * arcs), F32),
+            shape(whole, F32),
         ],
-        [ids, residuals, precisions, table],
-        count * count * width,
-        count * width * 4,
-    )
-    diff = call(
-        differ_kernel,
-        "differ",
-        shape(whole, F32),
-        [own_partials, other.reshape(whole)],
+        [ids, residuals, precisions, table, partials.reshape(whole), other.reshape(whole)],
         count * epochs * width,
         count * epochs * width * 8,
+        [VMEM(whole, BF16), dma((4,))],
+        (4,),
     )
     sent = call(
         functools.partial(solve_kernel, cap, owners),

time: 26.5 us -> 26.2 us (0.989)
  Pallas kernels: 6.15 us -> 7.1 us
  waiting for transfers between devices: 5.89 us -> 5.04 us
  starting transfers between devices: 14.3 us -> 13.8 us
    pallas_call x7, Pallas kernels: 6.15 us -> 7.1 us  [call(): pl.pallas_call(kernel, out_shape=outs, in_specs=[raw if i in anywhere els...]
    ppermute x6, starting transfers between devices: 8.72 us -> 7.9 us  [the longest x3 4.95 us: per_device(): asked = {k: lax.ppermute(regions, names, crossing(k)) for k in far_first}]
    ppermute x3, waiting for transfers between devices: 2.01 us -> 1.39 us  [per_device(): lax.ppermute(sent[k], names, crossing(k))]
    ppermute x3, starting transfers between devices: 3.84 us -> 4.26 us  [per_device(): lax.ppermute(sent[k], names, crossing(k))]
    ppermute x6, waiting for transfers between devices: 2.79 us -> 2.5 us  [the longest x3 1.5 us: per_device(): asked = {k: lax.ppermute(regions, names, crossing(k)) for k in far_first}]
  transfers between devices with their start and end apart: 11 -> 11, of which waited for: 6 -> 5; matrix products, arithmetic and copies ran while one was open for 0% -> 0% of each run, Pallas kernels for 16% -> 20%
where the time goes in v6:
time: 26.2 us; the launch traced here: 26 us
  starting transfers between devices  13.8 us (53%)
  Pallas kernels  7.1 us (27%)
  waiting for transfers between devices  5.04 us (19%)
    pallas_call x7, Pallas kernels, call(): pl.pallas_call(kernel, out_shape=outs, in_specs=[raw if i in anywhere els...  7.1 us
    ppermute x3, starting transfers between devices, per_device(): asked = {k: lax.ppermute(regions, names, crossing(k)) for k in far_first}  4.95 us
    ppermute x3, starting transfers between devices, per_device(): lax.ppermute(sent[k], names, crossing(k))  4.26 us
    ppermute x3, starting transfers between devices, per_device(): came = [lax.ppermute(found[k], names, crossing(k)) for k in order]  2.94 us
    ppermute x3, waiting for transfers between devices, per_device(): asked = {k: lax.ppermute(regions, names, crossing(k)) for k in far_first}  1.5 us
    ppermute x3, waiting for transfers between devices, per_device(): lax.ppermute(sent[k], names, crossing(k))  1.39 us
    ppermute x1, starting transfers between devices, per_device(): early, late = ([mine], [lax.ppermute(mine, ('arc', 'sat'), over)])  1.22 us
    ppermute x1, waiting for transfers between devices, per_device(): early, late = ([mine], [lax.ppermute(mine, ('arc', 'sat'), over)])  1.15 us
  transfers between devices with their start and end apart: 11, of which 5 were waited for; matrix products, arithmetic and copies ran while one was open for 0% of the time, Pallas kernels for 20%

profile of v6, /device:TPU:0, one launch (start us, length us, event | category | flops | bytes accessed | tf_op | source)
XLA Modules:
  0.0 26.0 jit_solution(630961838402484829)
XLA Ops:
  0.0 0.5 %collective-permute-start.6 = (bf16[4,8,1,128,256]{4,3,2,1,0:T(8,128)(2,1)}, bf16[4,8,1,128,256]{4,3,2,1,0:T(8,128)(2,1)S(1)}, u32[]{:S(2)}, u32[]{:S(2)}) collective-permute-start(bf16[4,8,1,128,256]{4,3,2,1,0:T(8,128)(2,1)} %param.6), channel_id=1, source_target_pairs={{0,1},{1,0},{2,3},{3,2},{4,5},{5,4},{6,7},{7,6},{8,9},{9,8},{10,11... | collective-permute-start | bytes 6291464 | tf_op jit(solution)/shard_map/ppermute | solution.py:201
  0.5 4.7 %collective-permute-start = (s32[4,8]{1,0:T(4,128)}, s32[4,8]{1,0:T(4,128)S(1)}, u32[]{:S(2)}, u32[]{:S(2)}) collective-permute-start(s32[4,8]{1,0:T(4,128)} %refs_0_.1), channel_id=1, source_target_pairs={{0,7},{1,6},{2,5},{3,4},{4,3},{5,2},{6,1},{7,0},{8,15},{9,14},{10,... | collective-permute-start | bytes 392 | tf_op jit(solution)/shard_map/ppermute | solution.py:200
  5.2 0.0 collective-permute-start.1
  5.2 0.2 collective-permute-start.3
  5.4 1.5 %load.1 = (bf16[480,256]{1,0:T(8,128)(2,1)S(1)}, s32[4,8]{1,0:T(4,128)S(1)}, f32[4,128]{1,0:T(4,128)S(1)}, f32[4,128]{1,0:T(4,128)S(1)}) custom-call(f32[480,1,256]{2,1,0:T(1,128)} %mascons.3, s32[4,8]{1,0:T(4,128)} %refs_0_.1, f32[4,128]{1,0:T(4,128)} %refs_1_.1, f32[4,128]{1,0:T(4,128)} %refs_2_.1), custom_call_target="tpu_custom_call" | custom-call | flops 122880 | bytes 491520 | tf_op jit(solution)/shard_map/load/pallas_call | solution.py:170
  6.9 0.0 collective-permute-done.refs_0_
  6.9 1.5 %collective-permute-done.1.refs_1_ = s32[4,8]{1,0:T(4,128)S(1)} collective-permute-done((s32[4,8]{1,0:T(4,128)}, s32[4,8]{1,0:T(4,128)S(1)}, u32[]{:S(2)}, u32[]{:S(2)}) %collective-permute-start.1) | collective-permute-done | bytes 160 | tf_op jit(solution)/shard_map/ppermute | solution.py:200
  8.4 0.4 %lookup.2 = (bf16[8,256]{1,0:T(8,128)(2,1)S(1)}, bf16[8,256]{1,0:T(8,128)(2,1)S(1)}) custom-call(s32[4,8]{1,0:T(4,128)S(1)} %collective-permute-done.refs_0_, s32[4,8]{1,0:T(4,128)S(1)} %collective-permute-done.1.refs_1_, bf16[480,256]{1,0:T(8,128)(2,1)S(1)} %get-tuple-element.22.refs_2_.refs_1_.table), custom_call_target="tpu_custom_call" | custom-call | flops 15728640 | bytes 491520 | tf_op jit(solution)/shard_map/lookup/pallas_call | solution.py:170
  8.8 0.0 collective-permute-start.2
  8.8 2.0 %collective-permute-start.5 = (bf16[8,256]{1,0:T(8,128)(2,1)S(1)}, bf16[8,256]{1,0:T(8,128)(2,1)S(1)}, u32[]{:S(2)}, u32[]{:S(2)}) collective-permute-start(bf16[8,256]{1,0:T(8,128)(2,1)S(1)} %get-tuple-element.24), channel_id=1, source_target_pairs={{0,7},{1,6},{2,5},{3,4},{4,3},{5,2},{6,1},{7,0},{8,15},{9,14},{10,... | collective-permute-start | bytes 12296 | tf_op jit(solution)/shard_map/ppermute | solution.py:226
  10.8 0.0 collective-permute-done.3.refs_0_
  10.8 0.4 %lookup.3 = bf16[8,256]{1,0:T(8,128)(2,1)S(1)} custom-call(s32[4,8]{1,0:T(4,128)S(1)} %collective-permute-done.3.refs_0_, bf16[480,256]{1,0:T(8,128)(2,1)S(1)} %get-tuple-element.22.refs_2_.refs_1_.table), custom_call_target="tpu_custom_call" | custom-call | flops 7864320 | bytes 491520 | tf_op jit(solution)/shard_map/lookup/pallas_call | solution.py:170
  11.2 0.9 %collective-permute-start.4 = (bf16[8,256]{1,0:T(8,128)(2,1)S(1)}, bf16[8,256]{1,0:T(8,128)(2,1)S(1)}, u32[]{:S(2)}, u32[]{:S(2)}) collective-permute-start(bf16[8,256]{1,0:T(8,128)(2,1)S(1)} %lookup.3), channel_id=1, source_target_pairs={{0,5},{1,4},{2,7},{3,6},{4,1},{5,0},{6,3},{7,2},{8,13},{9,12},{10,... | collective-permute-start | bytes 12296 | tf_op jit(solution)/shard_map/ppermute | solution.py:226
  12.1 0.0 collective-permute-done.6
  12.1 2.0 %plan.1 = (f32[32,256]{1,0:T(8,128)S(1)}, f32[32,24]{1,0:T(8,128)S(1)}, f32[32,32]{1,0:T(8,128)S(1)}, f32[32,128]{1,0:T(8,128)S(1)}, f32[128,8]{1,0:T(8,128)S(1)}, /*index=5*/f32[32,128,256]{2,1,0:T(8,128)S(1)}) custom-call(s32[4,8]{1,0:T(4,128)S(1)} %get-tuple-element.26.ids, f32[4,128]{1,0:T(4,128)S(1)} %get-tuple-element.27.observed, ...), custom_call_target="tpu_custom_call" | custom-call | flops 1048576 | bytes 8388608 | tf_op jit(solution)/shard_map/plan/pallas_call | solution.py:170
  14.1 0.0 collective-permute-done.2.refs_0_
  14.1 0.0 collective-permute-done.5.refs_2_
  14.1 1.0 %collective-permute-done.4.refs_1_ = bf16[8,256]{1,0:T(8,128)(2,1)S(1)} collective-permute-done((bf16[8,256]{1,0:T(8,128)(2,1)S(1)}, bf16[8,256]{1,0:T(8,128)(2,1)S(1)}, u32[]{:S(2)}, u32[]{:S(2)}) %collective-permute-start.4) | collective-permute-done | bytes 4128 | tf_op jit(solution)/shard_map/ppermute | solution.py:226
  15.1 0.0 copy-start
  15.1 1.0 %solve.1 = (bf16[8,384]{1,0:T(8,128)(2,1)S(1)}, bf16[8,384]{1,0:T(8,128)(2,1)S(1)}, bf16[8,384]{1,0:T(8,128)(2,1)S(1)}, bf16[8,384]{1,0:T(8,128)(2,1)S(1)}) custom-call(bf16[8,256]{1,0:T(8,128)(2,1)S(1)} %collective-permute-done.2.refs_0_, bf16[8,256]{1,0:T(8,128)(2,1)S(1)} %collective-permute-done.4.refs_1_, ...), custom_call_target="tpu_custom_call" | custom-call | flops 4194304 | bytes 4194304 | tf_op jit(solution)/shard_map/solve/pallas_call | solution.py:170
  16.2 1.6 %collective-permute-start.7 = (bf16[8,384]{1,0:T(8,128)(2,1)S(1)}, bf16[8,384]{1,0:T(8,128)(2,1)S(1)}, u32[]{:S(2)}, u32[]{:S(2)}) collective-permute-start(bf16[8,384]{1,0:T(8,128)(2,1)S(1)} %get-tuple-element.36), channel_id=1, source_target_pairs={{0,7},{1,6},{2,5},{3,4},{4,3},{5,2},{6,1},{7,0},{8,15},{9,14},{10,... | collective-permute-start | bytes 18440 | tf_op jit(solution)/shard_map/ppermute | solution.py:253
  17.8 0.8 %collective-permute-start.8 = (bf16[8,384]{1,0:T(8,128)(2,1)S(1)}, bf16[8,384]{1,0:T(8,128)(2,1)S(1)}, u32[]{:S(2)}, u32[]{:S(2)}) collective-permute-start(bf16[8,384]{1,0:T(8,128)(2,1)S(1)} %get-tuple-element.37), channel_id=1, source_target_pairs={{0,5},{1,4},{2,7},{3,6},{4,1},{5,0},{6,3},{7,2},{8,13},{9,12},{10,... | collective-permute-start | bytes 18440 | tf_op jit(solution)/shard_map/ppermute | solution.py:253
  18.6 1.8 %collective-permute-start.9 = (bf16[8,384]{1,0:T(8,128)(2,1)S(1)}, bf16[8,384]{1,0:T(8,128)(2,1)S(1)}, u32[]{:S(2)}, u32[]{:S(2)}) collective-permute-start(bf16[8,384]{1,0:T(8,128)(2,1)S(1)} %get-tuple-element.38), channel_id=1, source_target_pairs={{0,3},{1,2},{2,1},{3,0},{4,7},{5,6},{6,5},{7,4},{8,11},{9,10},{10,... | collective-permute-start | bytes 18440 | tf_op jit(solution)/shard_map/ppermute | solution.py:253
  20.4 0.6 %collective-permute-done.7 = bf16[8,384]{1,0:T(8,128)(2,1)S(1)} collective-permute-done((bf16[8,384]{1,0:T(8,128)(2,1)S(1)}, bf16[8,384]{1,0:T(8,128)(2,1)S(1)}, u32[]{:S(2)}, u32[]{:S(2)}) %collective-permute-start.7) | collective-permute-done | bytes 6176 | tf_op jit(solution)/shard_map/ppermute | solution.py:253
  21.0 0.8 %collective-permute-done.8 = bf16[8,384]{1,0:T(8,128)(2,1)S(1)} collective-permute-done((bf16[8,384]{1,0:T(8,128)(2,1)S(1)}, bf16[8,384]{1,0:T(8,128)(2,1)S(1)}, u32[]{:S(2)}, u32[]{:S(2)}) %collective-permute-start.8) | collective-permute-done | bytes 6176 | tf_op jit(solution)/shard_map/ppermute | solution.py:253
  21.8 0.0 collective-permute-done.9
  21.8 1.2 %collective-permute-start.10 = (bf16[4,8,384]{2,1,0:T(8,128)(2,1)S(1)}, bf16[4,8,384]{2,1,0:T(8,128)(2,1)S(1)}, u32[]{:S(2)}, u32[]{:S(2)}) collective-permute-start(bf16[4,8,384]{2,1,0:T(8,128)(2,1)S(1)} %pad_maximum_fusion.refs_0_), channel_id=1, source_target_pairs={{0,9},{1,8},{8,1},{9,0},{2,11},{3,10},{10,3},{11,2},{4,13},{5,12},... | collective-permute-start | bytes 73736 | tf_op jit(solution)/shard_map/ppermute | solution.py:257
  23.0 0.0 copy-done
  23.0 1.0 %base.1.refs_1_ = f32[120,256]{1,0:T(8,128)S(1)} custom-call(f32[480,1,256]{2,1,0:T(1,128)} %mascons.3, f32[1,256]{1,0:T(1,128)S(1)} %bitcast.9, bf16[4,8,384]{2,1,0:T(8,128)(2,1)S(1)} %pad_maximum_fusion.refs_0_), custom_call_target="tpu_custom_call" | custom-call | flops 1966080 | bytes 245760 | tf_op jit(solution)/shard_map/base/pallas_call | solution.py:170
  24.0 1.2 %collective-permute-done.10.refs_0_ = bf16[4,8,384]{2,1,0:T(8,128)(2,1)S(1)} collective-permute-done((bf16[4,8,384]{2,1,0:T(8,128)(2,1)S(1)}, bf16[4,8,384]{2,1,0:T(8,128)(2,1)S(1)}, u32[]{:S(2)}, u32[]{:S(2)}) %collective-permute-start.10) | collective-permute-done | bytes 24608 | tf_op jit(solution)/shard_map/ppermute | solution.py:257
  25.2 0.9 %place.1 = f32[120,1,256]{2,1,0:T(1,128)} custom-call(bf16[4,8,384]{2,1,0:T(8,128)(2,1)S(1)} %collective-permute-done.10.refs_0_, f32[120,256]{1,0:T(8,128)S(1)} %base.1.refs_1_), custom_call_target="tpu_custom_call" | custom-call | flops 3932160 | bytes 245760 | tf_op jit(solution)/shard_map/place/pallas_call | solution.py:170
  (1 shorter events, 0.0 us)
Async XLA Ops:
  0.0 12.1 %collective-permute-start.6 = (bf16[4,8,1,128,256]{4,3,2,1,0:T(8,128)(2,1)}, bf16[4,8,1,128,256]{4,3,2,1,0:T(8,128)(2,1)S(1)}, u32[]{:S(2)}, u32[]{:S(2)}) collective-permute-start(bf16[4,8,1,128,256]{4,3,2,1,0:T(8,128)(2,1)} %param.6), channel_id=1, source_target_pairs={{0,1},{1,0},{2,3},{3,2},{4,5},{5,4},{6,7},{7,6},{8,9},{9,8},{10,11... | collective-permute-start | bytes 6291464 | tf_op jit(solution)/shard_map/ppermute | solution.py:201
  0.5 6.4 %collective-permute-start = (s32[4,8]{1,0:T(4,128)}, s32[4,8]{1,0:T(4,128)S(1)}, u32[]{:S(2)}, u32[]{:S(2)}) collective-permute-start(s32[4,8]{1,0:T(4,128)} %refs_0_.1), channel_id=1, source_target_pairs={{0,7},{1,6},{2,5},{3,4},{4,3},{5,2},{6,1},{7,0},{8,15},{9,14},{10,... | collective-permute-start | bytes 392 | tf_op jit(solution)/shard_map/ppermute | solution.py:200
  5.2 3.2 %collective-permute-start.1 = (s32[4,8]{1,0:T(4,128)}, s32[4,8]{1,0:T(4,128)S(1)}, u32[]{:S(2)}, u32[]{:S(2)}) collective-permute-start(s32[4,8]{1,0:T(4,128)} %refs_0_.1), channel_id=1, source_target_pairs={{0,3},{1,2},{2,1},{3,0},{4,7},{5,6},{6,5},{7,4},{8,11},{9,10},{10,... | collective-permute-start | bytes 392 | tf_op jit(solution)/shard_map/ppermute | solution.py:200
  5.2 5.6 %collective-permute-start.3 = (s32[4,8]{1,0:T(4,128)}, s32[4,8]{1,0:T(4,128)S(1)}, u32[]{:S(2)}, u32[]{:S(2)}) collective-permute-start(s32[4,8]{1,0:T(4,128)} %refs_0_.1), channel_id=1, source_target_pairs={{0,5},{1,4},{2,7},{3,6},{4,1},{5,0},{6,3},{7,2},{8,13},{9,12},{10,... | collective-permute-start | bytes 392 | tf_op jit(solution)/shard_map/ppermute | solution.py:200
  8.8 5.3 %collective-permute-start.2 = (bf16[8,256]{1,0:T(8,128)(2,1)S(1)}, bf16[8,256]{1,0:T(8,128)(2,1)S(1)}, u32[]{:S(2)}, u32[]{:S(2)}) collective-permute-start(bf16[8,256]{1,0:T(8,128)(2,1)S(1)} %get-tuple-element.23), channel_id=1, source_target_pairs={{0,3},{1,2},{2,1},{3,0},{4,7},{5,6},{6,5},{7,4},{8,11},{9,10},{10,... | collective-permute-start | bytes 12296 | tf_op jit(solution)/shard_map/ppermute | solution.py:226
  8.8 5.3 %collective-permute-start.5 = (bf16[8,256]{1,0:T(8,128)(2,1)S(1)}, bf16[8,256]{1,0:T(8,128)(2,1)S(1)}, u32[]{:S(2)}, u32[]{:S(2)}) collective-permute-start(bf16[8,256]{1,0:T(8,128)(2,1)S(1)} %get-tuple-element.24), channel_id=1, source_target_pairs={{0,7},{1,6},{2,5},{3,4},{4,3},{5,2},{6,1},{7,0},{8,15},{9,14},{10,... | collective-permute-start | bytes 12296 | tf_op jit(solution)/shard_map/ppermute | solution.py:226
  11.2 3.9 %collective-permute-start.4 = (bf16[8,256]{1,0:T(8,128)(2,1)S(1)}, bf16[8,256]{1,0:T(8,128)(2,1)S(1)}, u32[]{:S(2)}, u32[]{:S(2)}) collective-permute-start(bf16[8,256]{1,0:T(8,128)(2,1)S(1)} %lookup.3), channel_id=1, source_target_pairs={{0,5},{1,4},{2,7},{3,6},{4,1},{5,0},{6,3},{7,2},{8,13},{9,12},{10,... | collective-permute-start | bytes 12296 | tf_op jit(solution)/shard_map/ppermute | solution.py:226
  15.1 7.9 %copy-start = (f32[256]{0:T(256)S(1)}, f32[256]{0:T(256)}, u32[]{:S(2)}) copy-start(f32[256]{0:T(256)} %param.11) | copy-start | bytes 3076
  16.2 4.9 %collective-permute-start.7 = (bf16[8,384]{1,0:T(8,128)(2,1)S(1)}, bf16[8,384]{1,0:T(8,128)(2,1)S(1)}, u32[]{:S(2)}, u32[]{:S(2)}) collective-permute-start(bf16[8,384]{1,0:T(8,128)(2,1)S(1)} %get-tuple-element.36), channel_id=1, source_target_pairs={{0,7},{1,6},{2,5},{3,4},{4,3},{5,2},{6,1},{7,0},{8,15},{9,14},{10,... | collective-permute-start | bytes 18440 | tf_op jit(solution)/shard_map/ppermute | solution.py:253
  17.8 4.0 %collective-permute-start.8 = (bf16[8,384]{1,0:T(8,128)(2,1)S(1)}, bf16[8,384]{1,0:T(8,128)(2,1)S(1)}, u32[]{:S(2)}, u32[]{:S(2)}) collective-permute-start(bf16[8,384]{1,0:T(8,128)(2,1)S(1)} %get-tuple-element.37), channel_id=1, source_target_pairs={{0,5},{1,4},{2,7},{3,6},{4,1},{5,0},{6,3},{7,2},{8,13},{9,12},{10,... | collective-permute-start | bytes 18440 | tf_op jit(solution)/shard_map/ppermute | solution.py:253
  18.6 3.2 %collective-permute-start.9 = (bf16[8,384]{1,0:T(8,128)(2,1)S(1)}, bf16[8,384]{1,0:T(8,128)(2,1)S(1)}, u32[]{:S(2)}, u32[]{:S(2)}) collective-permute-start(bf16[8,384]{1,0:T(8,128)(2,1)S(1)} %get-tuple-element.38), channel_id=1, source_target_pairs={{0,3},{1,2},{2,1},{3,0},{4,7},{5,6},{6,5},{7,4},{8,11},{9,10},{10,... | collective-permute-start | bytes 18440 | tf_op jit(solution)/shard_map/ppermute | solution.py:253
  21.8 3.3 %collective-permute-start.10 = (bf16[4,8,384]{2,1,0:T(8,128)(2,1)S(1)}, bf16[4,8,384]{2,1,0:T(8,128)(2,1)S(1)}, u32[]{:S(2)}, u32[]{:S(2)}) collective-permute-start(bf16[4,8,384]{2,1,0:T(8,128)(2,1)S(1)} %pad_maximum_fusion.refs_0_), channel_id=1, source_target_pairs={{0,9},{1,8},{8,1},{9,0},{2,11},{3,10},{10,3},{11,2},{4,13},{5,12},... | collective-permute-start | bytes 73736 | tf_op jit(solution)/shard_map/ppermute | solution.py:257

commit v7 on v6

--- a/solution.py
+++ b/solution.py
@@ -63,7 +63,7 @@
     copies = []
     for p in range(parts):
         part = pl.ds(p * step, step)
-        copies.append(pltpu.make_async_copy(mascons.at[part], held.at[part], sems.at[p]))
+        copies.append(pltpu.make_async_copy(mascons.at[part, 0, :], held.at[part], sems.at[p]))
     for j, (i, o) in enumerate(zip(smalls, outs)):
         copies.append(pltpu.make_async_copy(i, o, sems.at[parts + j]))
     for copy in copies:
@@ -71,12 +71,12 @@
     for p in range(parts):
         copies[p].wait()
         rows = slice(p * step, (p + 1) * step)
-        table[rows, :] = held[rows, 0, :].astype(BF16)
+        table[rows, :] = held[rows, :].astype(BF16)
     for copy in copies[parts:]:
         copy.wait()
 
 
-def plan_kernel(cap, owners, order, ids, observed, weights, table, mine, other, *refs):
+def plan_kernel(cap, owners, pairs, ids, observed, weights, table, mine, other, *refs):
     own_ref, near_ref, far_ref, names_ref, turned_ref, diff, held, sems = refs
     parts = sems.shape[0]
     size = diff.shape[0] // parts
@@ -99,7 +99,11 @@
     valid = owner < owners
     step = owner ^ me
     spot = iota(near_ref.shape, 1)
-    turn = sum(jnp.where(step == k, j * cap, 0) for j, k in enumerate(order))
+    sat = lax.axis_index("sat")
+    turn = jnp.where(step == 1, 2 * len(pairs) * cap, 0)
+    for j, (high, low) in enumerate(pairs):
+        turn += jnp.where(step == high, (2 * j + sat) * cap, 0)
+        turn += jnp.where(step == low, (2 * j + 1 - sat) * cap, 0)
     near = valid & (step > 0) & (spot == turn + rank)
     far = (valid & (iota(far_ref.shape, 1) == step * cap + rank)).astype(F32)
     local = jnp.broadcast_to((col - owner * group - group // 2).astype(F32), (count, names_ref.shape[1]))
@@ -188,16 +192,19 @@
     cap = count // owners
     shape = jax.ShapeDtypeStruct
 
-    def crossing(k):
-        return [(r * 2 + s, (r ^ k) * 2 + (1 - s)) for r in range(owners) for s in range(2)]
+    def crossing(even, odd):
+        return [
+            (r * 2 + s, (r ^ (odd if s else even)) * 2 + (1 - s)) for r in range(owners) for s in range(2)
+        ]
 
     names = ("reg", "sat")
     share = group // (blocks * lax.axis_size("sat"))
     whole = (count, epochs, width)
     dma = pltpu.SemaphoreType.DMA
     far_first = list(range(owners - 1, 0, -1))
-    order = far_first[::-1]
-    asked = {k: lax.ppermute(regions, names, crossing(k)) for k in far_first}
+    pairs = [(k + 1, k) for k in range(owners - 2, 0, -2)]
+    hands = [(1, 1), *pairs]
+    asked = {h: lax.ppermute(regions, names, crossing(*h)) for h in hands}
     other = lax.ppermute(partials, "sat", [(0, 1), (1, 0)])
     smalls = [regions, observed, weights]
     table, ids, residuals, precisions = call(
@@ -207,26 +214,22 @@
         [mascons, *smalls],
         group * width,
         group * width * 4,
-        [VMEM(mascons.shape, F32), dma((4 + len(smalls),))],
+        [VMEM((group, width), F32), dma((4 + len(smalls),))],
         range(1 + len(smalls)),
     )
-    found = {}
-    for some in filter(None, (far_first[1:2], far_first[:1] + far_first[2:])):
-        found |= zip(
-            some,
-            call(
-                functools.partial(lookup_kernel, cap),
-                "lookup",
-                [shape((cap, width), BF16)] * len(some),
-                [*(asked[k] for k in some), table],
-                2 * len(some) * count * group * width,
-                group * width * 4,
-            ),
-        )
-    came = [lax.ppermute(found[k], names, crossing(k)) for k in order]
-    ids, _ = lax.optimization_barrier((ids, found[order[0]]))
+    found = call(
+        functools.partial(lookup_kernel, cap),
+        "lookup",
+        [shape((cap, width), BF16)] * len(hands),
+        [*(asked[h] for h in hands), table],
+        2 * len(hands) * count * group * width,
+        group * width * 4,
+    )
+    found = dict(zip(hands, found))
+    came = {h: lax.ppermute(found[h], names, crossing(*h[::-1])) for h in hands}
+    ids, _ = lax.optimization_barrier((ids, found[(1, 1)]))
     own, near, far, named, turned, diff = call(
-        functools.partial(plan_kernel, cap, owners, order),
+        functools.partial(plan_kernel, cap, owners, pairs),
         "plan",
         [
             shape((count, width), F32),
@@ -242,15 +245,20 @@
         [VMEM(whole, BF16), dma((4,))],
         (4,),
     )
+    arrived = []
+    for h in pairs:
+        rows, _ = lax.optimization_barrier((came[h], turned))
+        arrived += [came[h], lax.ppermute(rows, "sat", [(0, 1), (1, 0)])]
+    arrived.append(came[1, 1])
     sent = call(
         functools.partial(solve_kernel, cap, owners),
         "solve",
         [shape((cap, width + LANES), BF16)] * owners,
-        [*came, own, near, far, named, turned, diff],
+        [*arrived, own, near, far, named, turned, diff],
         4 * count * epochs * width,
         count * epochs * width * 4,
     )
-    mine = [sent[0]] + [lax.ppermute(sent[k], names, crossing(k)) for k in far_first]
+    mine = [sent[0]] + [lax.ppermute(sent[k], names, crossing(k, k)) for k in far_first]
     mine = jnp.stack(mine)
     if blocks == 2:
         over = [(a * 2 + s, (1 - a) * 2 + (1 - s)) for a in range(2) for s in range(2)]

time: 26.2 us -> 25.3 us (0.966)
  waiting for transfers between devices: 5.04 us -> 4.13 us
  Pallas kernels: 7.1 us -> 6.4 us
  starting transfers between devices: 13.8 us -> 14.5 us
    pallas_call x7 -> x6, Pallas kernels: 7.1 us -> 6.4 us  [call(): pl.pallas_call(kernel, out_shape=outs, in_specs=[raw if i in anywhere els...]
    ppermute x9 -> x8, waiting for transfers between devices: 3.89 us -> 3.3 us  [the longest x3 1.6 us: per_device(): lax.ppermute(sent[k], names, crossing(k, k))]
    ppermute x9 -> x8, starting transfers between devices: 12.2 us -> 12.6 us  [the longest x2 4.77 us: per_device(): asked = {h: lax.ppermute(regions, names, crossing(*h)) for h in hands}]
    ppermute x1, waiting for transfers between devices: 1.15 us -> 0.83 us  [per_device(): early, late = ([mine], [lax.ppermute(mine, ('arc', 'sat'), over)])]
    ppermute x1, starting transfers between devices: 1.22 us -> 1.51 us  [per_device(): early, late = ([mine], [lax.ppermute(mine, ('arc', 'sat'), over)])]
  transfers between devices with their start and end apart: 11 -> 10, of which waited for: 5 -> 5; matrix products, arithmetic and copies ran while one was open for 0% -> 0% of each run, Pallas kernels for 20% -> 18%
where the time goes in v7:
time: 25.3 us; the launch traced here: 25.1 us
  starting transfers between devices  14.5 us (57%)
  Pallas kernels  6.4 us (25%)
  waiting for transfers between devices  4.13 us (16%)
    pallas_call x6, Pallas kernels, call(): pl.pallas_call(kernel, out_shape=outs, in_specs=[raw if i in anywhere els...  6.4 us
    ppermute x2, starting transfers between devices, per_device(): asked = {h: lax.ppermute(regions, names, crossing(*h)) for h in hands}  4.77 us
    ppermute x3, starting transfers between devices, per_device(): lax.ppermute(sent[k], names, crossing(k, k))  4.07 us
    ppermute x2, starting transfers between devices, per_device(): came = {h: lax.ppermute(found[h], names, crossing(*h[::-1])) for h in hands}  2.88 us
    ppermute x3, waiting for transfers between devices, per_device(): lax.ppermute(sent[k], names, crossing(k, k))  1.6 us
    ppermute x1, starting transfers between devices, per_device(): early, late = ([mine], [lax.ppermute(mine, ('arc', 'sat'), over)])  1.51 us
    ppermute x2, waiting for transfers between devices, per_device(): asked = {h: lax.ppermute(regions, names, crossing(*h)) for h in hands}  0.87 us
    ppermute x1, starting transfers between devices, per_device(): arrived += [came[h], lax.ppermute(rows, 'sat', [(0, 1), (1, 0)])]  0.85 us
  transfers between devices with their start and end apart: 10, of which 5 were waited for; matrix products, arithmetic and copies ran while one was open for 0% of the time, Pallas kernels for 18%

profile of v7, /device:TPU:0, one launch (start us, length us, event | category | flops | bytes accessed | tf_op | source)
XLA Modules:
  0.0 25.1 jit_solution(4726173405517697068)
XLA Ops:
  0.0 0.5 %collective-permute-start.3 = (bf16[4,8,1,128,256]{4,3,2,1,0:T(8,128)(2,1)}, bf16[4,8,1,128,256]{4,3,2,1,0:T(8,128)(2,1)S(1)}, u32[]{:S(2)}, u32[]{:S(2)}) collective-permute-start(bf16[4,8,1,128,256]{4,3,2,1,0:T(8,128)(2,1)} %param.6), channel_id=1, source_target_pairs={{0,1},{1,0},{2,3},{3,2},{4,5},{5,4},{6,7},{7,6},{8,9},{9,8},{10,11... | collective-permute-start | bytes 6291464 | tf_op jit(solution)/shard_map/ppermute | solution.py:208
  0.5 2.7 %collective-permute-start = (s32[4,8]{1,0:T(4,128)}, s32[4,8]{1,0:T(4,128)S(1)}, u32[]{:S(2)}, u32[]{:S(2)}) collective-permute-start(s32[4,8]{1,0:T(4,128)} %refs_0_.1), channel_id=1, source_target_pairs={{0,3},{1,2},{2,1},{3,0},{4,7},{5,6},{6,5},{7,4},{8,11},{9,10},{10,... | collective-permute-start | bytes 392 | tf_op jit(solution)/shard_map/ppermute | solution.py:207
  3.1 2.1 %collective-permute-start.1 = (s32[4,8]{1,0:T(4,128)}, s32[4,8]{1,0:T(4,128)S(1)}, u32[]{:S(2)}, u32[]{:S(2)}) collective-permute-start(s32[4,8]{1,0:T(4,128)} %refs_0_.1), channel_id=1, source_target_pairs={{0,7},{1,4},{2,5},{3,6},{4,3},{5,0},{6,1},{7,2},{8,15},{9,12},{10,... | collective-permute-start | bytes 392 | tf_op jit(solution)/shard_map/ppermute | solution.py:207
  5.2 1.1 %load.1 = (bf16[480,256]{1,0:T(8,128)(2,1)S(1)}, s32[4,8]{1,0:T(4,128)S(1)}, f32[4,128]{1,0:T(4,128)S(1)}, f32[4,128]{1,0:T(4,128)S(1)}) custom-call(f32[480,1,256]{2,1,0:T(1,128)} %mascons.3, s32[4,8]{1,0:T(4,128)} %refs_0_.1, f32[4,128]{1,0:T(4,128)} %refs_1_.1, f32[4,128]{1,0:T(4,128)} %refs_2_.1), custom_call_target="tpu_custom_call" | custom-call | flops 122880 | bytes 491520 | tf_op jit(solution)/shard_map/load/pallas_call | solution.py:174
  6.4 0.0 collective-permute-done.refs_0_
  6.4 0.9 %collective-permute-done.1.refs_1_ = s32[4,8]{1,0:T(4,128)S(1)} collective-permute-done((s32[4,8]{1,0:T(4,128)}, s32[4,8]{1,0:T(4,128)S(1)}, u32[]{:S(2)}, u32[]{:S(2)}) %collective-permute-start.1) | collective-permute-done | bytes 160 | tf_op jit(solution)/shard_map/ppermute | solution.py:207
  7.3 0.4 %lookup.1 = (bf16[8,256]{1,0:T(8,128)(2,1)S(1)}, bf16[8,256]{1,0:T(8,128)(2,1)S(1)}) custom-call(s32[4,8]{1,0:T(4,128)S(1)} %collective-permute-done.refs_0_, s32[4,8]{1,0:T(4,128)S(1)} %collective-permute-done.1.refs_1_, bf16[480,256]{1,0:T(8,128)(2,1)S(1)} %get-tuple-element.23.refs_2_.table), custom_call_target="tpu_custom_call" | custom-call | flops 15728640 | bytes 491520 | tf_op jit(solution)/shard_map/lookup/pallas_call | solution.py:174
  7.7 1.3 %collective-permute-start.2 = (bf16[8,256]{1,0:T(8,128)(2,1)S(1)}, bf16[8,256]{1,0:T(8,128)(2,1)S(1)}, u32[]{:S(2)}, u32[]{:S(2)}) collective-permute-start(bf16[8,256]{1,0:T(8,128)(2,1)S(1)} %get-tuple-element.24), channel_id=1, source_target_pairs={{0,5},{1,6},{2,7},{3,4},{4,1},{5,2},{6,3},{7,0},{8,13},{9,14},{10,... | collective-permute-start | bytes 12296 | tf_op jit(solution)/shard_map/ppermute | solution.py:229
  9.0 1.6 %collective-permute-start.5 = (bf16[8,256]{1,0:T(8,128)(2,1)S(1)}, bf16[8,256]{1,0:T(8,128)(2,1)S(1)}, u32[]{:S(2)}, u32[]{:S(2)}) collective-permute-start(bf16[8,256]{1,0:T(8,128)(2,1)S(1)} %get-tuple-element.26), channel_id=1, source_target_pairs={{0,3},{1,2},{2,1},{3,0},{4,7},{5,6},{6,5},{7,4},{8,11},{9,10},{10,... | collective-permute-start | bytes 12296 | tf_op jit(solution)/shard_map/ppermute | solution.py:229
  10.5 0.0 collective-permute-done.3
  10.5 2.0 %plan.1 = (f32[32,256]{1,0:T(8,128)S(1)}, f32[32,24]{1,0:T(8,128)S(1)}, f32[32,32]{1,0:T(8,128)S(1)}, f32[32,128]{1,0:T(8,128)S(1)}, f32[128,8]{1,0:T(8,128)S(1)}, /*index=5*/f32[32,128,256]{2,1,0:T(8,128)S(1)}) custom-call(s32[4,8]{1,0:T(4,128)S(1)} %get-tuple-element.27.ids, f32[4,128]{1,0:T(4,128)S(1)} %get-tuple-element.28.observed, ...), custom_call_target="tpu_custom_call" | custom-call | flops 1048576 | bytes 8388608 | tf_op jit(solution)/shard_map/plan/pallas_call | solution.py:174
  12.5 0.0 collective-permute-done.2.refs_0_
  12.5 0.9 %collective-permute-start.4 = (bf16[8,256]{1,0:T(8,128)(2,1)S(1)}, bf16[8,256]{1,0:T(8,128)(2,1)S(1)}, u32[]{:S(2)}, u32[]{:S(2)}) collective-permute-start(bf16[8,256]{1,0:T(8,128)(2,1)S(1)} %collective-permute-done.2.refs_0_), channel_id=1, source_target_pairs={{0,1},{1,0},{2,3},{3,2},{4,5},{5,4},{6,7},{7,6},{8,9},{9,8},{10,11... | collective-permute-start | bytes 12296 | tf_op jit(solution)/shard_map/ppermute | solution.py:251
  13.4 0.0 collective-permute-done.5.refs_2_
  13.4 0.8 %collective-permute-done.4.refs_1_ = bf16[8,256]{1,0:T(8,128)(2,1)S(1)} collective-permute-done((bf16[8,256]{1,0:T(8,128)(2,1)S(1)}, bf16[8,256]{1,0:T(8,128)(2,1)S(1)}, u32[]{:S(2)}, u32[]{:S(2)}) %collective-permute-start.4) | collective-permute-done | bytes 4128 | tf_op jit(solution)/shard_map/ppermute | solution.py:251
  14.2 0.0 copy-start
  14.2 1.0 %solve.1 = (bf16[8,384]{1,0:T(8,128)(2,1)S(1)}, bf16[8,384]{1,0:T(8,128)(2,1)S(1)}, bf16[8,384]{1,0:T(8,128)(2,1)S(1)}, bf16[8,384]{1,0:T(8,128)(2,1)S(1)}) custom-call(bf16[8,256]{1,0:T(8,128)(2,1)S(1)} %collective-permute-done.2.refs_0_, bf16[8,256]{1,0:T(8,128)(2,1)S(1)} %collective-permute-done.4.refs_1_, ...), custom_call_target="tpu_custom_call" | custom-call | flops 4194304 | bytes 4194304 | tf_op jit(solution)/shard_map/solve/pallas_call | solution.py:174
  15.2 1.7 %collective-permute-start.6 = (bf16[8,384]{1,0:T(8,128)(2,1)S(1)}, bf16[8,384]{1,0:T(8,128)(2,1)S(1)}, u32[]{:S(2)}, u32[]{:S(2)}) collective-permute-start(bf16[8,384]{1,0:T(8,128)(2,1)S(1)} %get-tuple-element.38), channel_id=1, source_target_pairs={{0,7},{1,6},{2,5},{3,4},{4,3},{5,2},{6,1},{7,0},{8,15},{9,14},{10,... | collective-permute-start | bytes 18440 | tf_op jit(solution)/shard_map/ppermute | solution.py:261
  17.0 0.4 %collective-permute-start.7 = (bf16[8,384]{1,0:T(8,128)(2,1)S(1)}, bf16[8,384]{1,0:T(8,128)(2,1)S(1)}, u32[]{:S(2)}, u32[]{:S(2)}) collective-permute-start(bf16[8,384]{1,0:T(8,128)(2,1)S(1)} %get-tuple-element.39), channel_id=1, source_target_pairs={{0,5},{1,4},{2,7},{3,6},{4,1},{5,0},{6,3},{7,2},{8,13},{9,12},{10,... | collective-permute-start | bytes 18440 | tf_op jit(solution)/shard_map/ppermute | solution.py:261
  17.3 2.0 %collective-permute-start.8 = (bf16[8,384]{1,0:T(8,128)(2,1)S(1)}, bf16[8,384]{1,0:T(8,128)(2,1)S(1)}, u32[]{:S(2)}, u32[]{:S(2)}) collective-permute-start(bf16[8,384]{1,0:T(8,128)(2,1)S(1)} %get-tuple-element.40), channel_id=1, source_target_pairs={{0,3},{1,2},{2,1},{3,0},{4,7},{5,6},{6,5},{7,4},{8,11},{9,10},{10,... | collective-permute-start | bytes 18440 | tf_op jit(solution)/shard_map/ppermute | solution.py:261
  19.3 0.8 %collective-permute-done.6 = bf16[8,384]{1,0:T(8,128)(2,1)S(1)} collective-permute-done((bf16[8,384]{1,0:T(8,128)(2,1)S(1)}, bf16[8,384]{1,0:T(8,128)(2,1)S(1)}, u32[]{:S(2)}, u32[]{:S(2)}) %collective-permute-start.6) | collective-permute-done | bytes 6176 | tf_op jit(solution)/shard_map/ppermute | solution.py:261
  20.1 0.8 %collective-permute-done.7 = bf16[8,384]{1,0:T(8,128)(2,1)S(1)} collective-permute-done((bf16[8,384]{1,0:T(8,128)(2,1)S(1)}, bf16[8,384]{1,0:T(8,128)(2,1)S(1)}, u32[]{:S(2)}, u32[]{:S(2)}) %collective-permute-start.7) | collective-permute-done | bytes 6176 | tf_op jit(solution)/shard_map/ppermute | solution.py:261
  20.9 0.0 collective-permute-done.8
  20.9 1.5 %collective-permute-start.9 = (bf16[4,8,384]{2,1,0:T(8,128)(2,1)S(1)}, bf16[4,8,384]{2,1,0:T(8,128)(2,1)S(1)}, u32[]{:S(2)}, u32[]{:S(2)}) collective-permute-start(bf16[4,8,384]{2,1,0:T(8,128)(2,1)S(1)} %pad_maximum_fusion.refs_0_), channel_id=1, source_target_pairs={{0,9},{1,8},{8,1},{9,0},{2,11},{3,10},{10,3},{11,2},{4,13},{5,12},... | collective-permute-start | bytes 73736 | tf_op jit(solution)/shard_map/ppermute | solution.py:265
  22.4 0.0 copy-done
  22.4 1.0 %base.1.refs_1_ = f32[120,256]{1,0:T(8,128)S(1)} custom-call(f32[480,1,256]{2,1,0:T(1,128)} %mascons.3, f32[1,256]{1,0:T(1,128)S(1)} %bitcast.9, bf16[4,8,384]{2,1,0:T(8,128)(2,1)S(1)} %pad_maximum_fusion.refs_0_), custom_call_target="tpu_custom_call" | custom-call | flops 1966080 | bytes 245760 | tf_op jit(solution)/shard_map/base/pallas_call | solution.py:174
  23.4 0.8 %collective-permute-done.9.refs_0_ = bf16[4,8,384]{2,1,0:T(8,128)(2,1)S(1)} collective-permute-done((bf16[4,8,384]{2,1,0:T(8,128)(2,1)S(1)}, bf16[4,8,384]{2,1,0:T(8,128)(2,1)S(1)}, u32[]{:S(2)}, u32[]{:S(2)}) %collective-permute-start.9) | collective-permute-done | bytes 24608 | tf_op jit(solution)/shard_map/ppermute | solution.py:265
  24.2 0.9 %place.1 = f32[120,1,256]{2,1,0:T(1,128)} custom-call(bf16[4,8,384]{2,1,0:T(8,128)(2,1)S(1)} %collective-permute-done.9.refs_0_, f32[120,256]{1,0:T(8,128)S(1)} %base.1.refs_1_), custom_call_target="tpu_custom_call" | custom-call | flops 3932160 | bytes 245760 | tf_op jit(solution)/shard_map/place/pallas_call | solution.py:174
  (1 shorter events, 0.0 us)
Async XLA Ops:
  0.0 10.5 %collective-permute-start.3 = (bf16[4,8,1,128,256]{4,3,2,1,0:T(8,128)(2,1)}, bf16[4,8,1,128,256]{4,3,2,1,0:T(8,128)(2,1)S(1)}, u32[]{:S(2)}, u32[]{:S(2)}) collective-permute-start(bf16[4,8,1,128,256]{4,3,2,1,0:T(8,128)(2,1)} %param.6), channel_id=1, source_target_pairs={{0,1},{1,0},{2,3},{3,2},{4,5},{5,4},{6,7},{7,6},{8,9},{9,8},{10,11... | collective-permute-start | bytes 6291464 | tf_op jit(solution)/shard_map/ppermute | solution.py:208
  0.5 5.9 %collective-permute-start = (s32[4,8]{1,0:T(4,128)}, s32[4,8]{1,0:T(4,128)S(1)}, u32[]{:S(2)}, u32[]{:S(2)}) collective-permute-start(s32[4,8]{1,0:T(4,128)} %refs_0_.1), channel_id=1, source_target_pairs={{0,3},{1,2},{2,1},{3,0},{4,7},{5,6},{6,5},{7,4},{8,11},{9,10},{10,... | collective-permute-start | bytes 392 | tf_op jit(solution)/shard_map/ppermute | solution.py:207
  3.1 4.1 %collective-permute-start.1 = (s32[4,8]{1,0:T(4,128)}, s32[4,8]{1,0:T(4,128)S(1)}, u32[]{:S(2)}, u32[]{:S(2)}) collective-permute-start(s32[4,8]{1,0:T(4,128)} %refs_0_.1), channel_id=1, source_target_pairs={{0,7},{1,4},{2,5},{3,6},{4,3},{5,0},{6,1},{7,2},{8,15},{9,12},{10,... | collective-permute-start | bytes 392 | tf_op jit(solution)/shard_map/ppermute | solution.py:207
  7.7 4.9 %collective-permute-start.2 = (bf16[8,256]{1,0:T(8,128)(2,1)S(1)}, bf16[8,256]{1,0:T(8,128)(2,1)S(1)}, u32[]{:S(2)}, u32[]{:S(2)}) collective-permute-start(bf16[8,256]{1,0:T(8,128)(2,1)S(1)} %get-tuple-element.24), channel_id=1, source_target_pairs={{0,5},{1,6},{2,7},{3,4},{4,1},{5,2},{6,3},{7,0},{8,13},{9,14},{10,... | collective-permute-start | bytes 12296 | tf_op jit(solution)/shard_map/ppermute | solution.py:229
  9.0 4.4 %collective-permute-start.5 = (bf16[8,256]{1,0:T(8,128)(2,1)S(1)}, bf16[8,256]{1,0:T(8,128)(2,1)S(1)}, u32[]{:S(2)}, u32[]{:S(2)}) collective-permute-start(bf16[8,256]{1,0:T(8,128)(2,1)S(1)} %get-tuple-element.26), channel_id=1, source_target_pairs={{0,3},{1,2},{2,1},{3,0},{4,7},{5,6},{6,5},{7,4},{8,11},{9,10},{10,... | collective-permute-start | bytes 12296 | tf_op jit(solution)/shard_map/ppermute | solution.py:229
  12.5 1.7 %collective-permute-start.4 = (bf16[8,256]{1,0:T(8,128)(2,1)S(1)}, bf16[8,256]{1,0:T(8,128)(2,1)S(1)}, u32[]{:S(2)}, u32[]{:S(2)}) collective-permute-start(bf16[8,256]{1,0:T(8,128)(2,1)S(1)} %collective-permute-done.2.refs_0_), channel_id=1, source_target_pairs={{0,1},{1,0},{2,3},{3,2},{4,5},{5,4},{6,7},{7,6},{8,9},{9,8},{10,11... | collective-permute-start | bytes 12296 | tf_op jit(solution)/shard_map/ppermute | solution.py:251
  14.2 8.2 %copy-start = (f32[256]{0:T(256)S(1)}, f32[256]{0:T(256)}, u32[]{:S(2)}) copy-start(f32[256]{0:T(256)} %param.11) | copy-start | bytes 3076
  15.2 4.9 %collective-permute-start.6 = (bf16[8,384]{1,0:T(8,128)(2,1)S(1)}, bf16[8,384]{1,0:T(8,128)(2,1)S(1)}, u32[]{:S(2)}, u32[]{:S(2)}) collective-permute-start(bf16[8,384]{1,0:T(8,128)(2,1)S(1)} %get-tuple-element.38), channel_id=1, source_target_pairs={{0,7},{1,6},{2,5},{3,4},{4,3},{5,2},{6,1},{7,0},{8,15},{9,14},{10,... | collective-permute-start | bytes 18440 | tf_op jit(solution)/shard_map/ppermute | solution.py:261
  17.0 4.0 %collective-permute-start.7 = (bf16[8,384]{1,0:T(8,128)(2,1)S(1)}, bf16[8,384]{1,0:T(8,128)(2,1)S(1)}, u32[]{:S(2)}, u32[]{:S(2)}) collective-permute-start(bf16[8,384]{1,0:T(8,128)(2,1)S(1)} %get-tuple-element.39), channel_id=1, source_target_pairs={{0,5},{1,4},{2,7},{3,6},{4,1},{5,0},{6,3},{7,2},{8,13},{9,12},{10,... | collective-permute-start | bytes 18440 | tf_op jit(solution)/shard_map/ppermute | solution.py:261
  17.3 3.6 %collective-permute-start.8 = (bf16[8,384]{1,0:T(8,128)(2,1)S(1)}, bf16[8,384]{1,0:T(8,128)(2,1)S(1)}, u32[]{:S(2)}, u32[]{:S(2)}) collective-permute-start(bf16[8,384]{1,0:T(8,128)(2,1)S(1)} %get-tuple-element.40), channel_id=1, source_target_pairs={{0,3},{1,2},{2,1},{3,0},{4,7},{5,6},{6,5},{7,4},{8,11},{9,10},{10,... | collective-permute-start | bytes 18440 | tf_op jit(solution)/shard_map/ppermute | solution.py:261
  20.9 3.3 %collective-permute-start.9 = (bf16[4,8,384]{2,1,0:T(8,128)(2,1)S(1)}, bf16[4,8,384]{2,1,0:T(8,128)(2,1)S(1)}, u32[]{:S(2)}, u32[]{:S(2)}) collective-permute-start(bf16[4,8,384]{2,1,0:T(8,128)(2,1)S(1)} %pad_maximum_fusion.refs_0_), channel_id=1, source_target_pairs={{0,9},{1,8},{8,1},{9,0},{2,11},{3,10},{10,3},{11,2},{4,13},{5,12},... | collective-permute-start | bytes 73736 | tf_op jit(solution)/shard_map/ppermute | solution.py:265

commit v8 on v7

--- a/solution.py
+++ b/solution.py
@@ -56,7 +56,7 @@
 
 def load_kernel(mascons, *refs):
     n = (len(refs) - 3) // 2
-    smalls, table, outs = refs[:n], refs[n], refs[n + 1 : 2 * n + 1]
+    others, table, outs = refs[:n], refs[n], refs[n + 1 : 2 * n + 1]
     held, sems = refs[2 * n + 1 :]
     parts = sems.shape[0] - n
     step = table.shape[0] // parts
@@ -64,7 +64,7 @@
     for p in range(parts):
         part = pl.ds(p * step, step)
         copies.append(pltpu.make_async_copy(mascons.at[part, 0, :], held.at[part], sems.at[p]))
-    for j, (i, o) in enumerate(zip(smalls, outs)):
+    for j, (i, o) in enumerate(zip(others, outs)):
         copies.append(pltpu.make_async_copy(i, o, sems.at[parts + j]))
     for copy in copies:
         copy.start()
@@ -76,15 +76,8 @@
         copy.wait()
 
 
-def plan_kernel(cap, owners, pairs, ids, observed, weights, table, mine, other, *refs):
-    own_ref, near_ref, far_ref, names_ref, turned_ref, diff, held, sems = refs
-    parts = sems.shape[0]
-    size = diff.shape[0] // parts
-    copies = []
-    for p in range(parts):
-        part = pl.ds(p * size, size)
-        copies.append(pltpu.make_async_copy(mine.at[part], held.at[part], sems.at[p]))
-        copies[-1].start()
+def plan_kernel(cap, owners, pairs, ids, observed, weights, table, *refs):
+    own_ref, near_ref, far_ref, names_ref, turned_ref = refs
     me = lax.axis_index("reg")
     sign = 1.0 - 2.0 * lax.axis_index("sat").astype(F32)
     group = table.shape[0]
@@ -111,10 +104,11 @@
     far_ref[...] = far * sign
     names_ref[...] = transposed_dot(far.astype(BF16), local.astype(BF16))
     turned_ref[...] = jnp.concatenate([observed[...], weights[...]], axis=0).T
-    for p in range(parts):
-        copies[p].wait()
-        for i in range(p * size, (p + 1) * size):
-            diff[i] = held[i].astype(F32) - other[i].astype(F32)
+
+
+def differ_kernel(mine, other, diff):
+    for i in range(diff.shape[0]):
+        diff[i] = mine[i].astype(F32) - other[i].astype(F32)
 
 
 def solve_kernel(cap, owners, *refs):
@@ -203,32 +197,37 @@
     dma = pltpu.SemaphoreType.DMA
     far_first = list(range(owners - 1, 0, -1))
     pairs = [(k + 1, k) for k in range(owners - 2, 0, -2)]
-    hands = [(1, 1), *pairs]
+    hands = [*pairs, (1, 1)]
     asked = {h: lax.ppermute(regions, names, crossing(*h)) for h in hands}
     other = lax.ppermute(partials, "sat", [(0, 1), (1, 0)])
-    smalls = [regions, observed, weights]
-    table, ids, residuals, precisions = call(
+    loads = [regions, observed, weights, partials.reshape(whole)]
+    table, ids, residuals, precisions, own_partials = call(
         load_kernel,
         "load",
-        [shape((group, width), BF16), *(shape(i.shape, i.dtype) for i in smalls)],
-        [mascons, *smalls],
+        [shape((group, width), BF16), *(shape(i.shape, i.dtype) for i in loads)],
+        [mascons, *loads],
         group * width,
         group * width * 4,
-        [VMEM((group, width), F32), dma((4 + len(smalls),))],
-        range(1 + len(smalls)),
-    )
-    found = call(
-        functools.partial(lookup_kernel, cap),
-        "lookup",
-        [shape((cap, width), BF16)] * len(hands),
-        [*(asked[h] for h in hands), table],
-        2 * len(hands) * count * group * width,
-        group * width * 4,
-    )
-    found = dict(zip(hands, found))
-    came = {h: lax.ppermute(found[h], names, crossing(*h[::-1])) for h in hands}
-    ids, _ = lax.optimization_barrier((ids, found[(1, 1)]))
-    own, near, far, named, turned, diff = call(
+        [VMEM((group, width), F32), dma((4 + len(loads),))],
+        range(1 + len(loads)),
+    )
+    found, came = {}, {}
+    for h in hands:
+        [found[h]] = call(
+            functools.partial(lookup_kernel, cap),
+            "lookup",
+            [shape((cap, width), BF16)],
+            [asked[h], table],
+            2 * count * group * width,
+            group * width * 4,
+        )
+    for h in hands:
+        rows = found[h]
+        if h in pairs:
+            rows, _ = lax.optimization_barrier((rows, asked[1, 1]))
+        came[h] = lax.ppermute(rows, names, crossing(*h[::-1]))
+    ids, _ = lax.optimization_barrier((ids, found[pairs[0]]))
+    own, near, far, named, turned = call(
         functools.partial(plan_kernel, cap, owners, pairs),
         "plan",
         [
@@ -237,13 +236,18 @@
             shape((count, owners * cap), F32),
             shape((owners * cap, LANES), F32),
             shape((epochs, 2 * arcs), F32),
-            shape(whole, F32),
         ],
-        [ids, residuals, precisions, table, partials.reshape(whole), other.reshape(whole)],
+        [ids, residuals, precisions, table],
+        count * count * width,
+        count * width * 4,
+    )
+    diff = call(
+        differ_kernel,
+        "differ",
+        shape(whole, F32),
+        [own_partials, other.reshape(whole)],
         count * epochs * width,
         count * epochs * width * 8,
-        [VMEM(whole, BF16), dma((4,))],
-        (4,),
     )
     arrived = []
     for h in pairs:

time: 25.3 us -> 25.2 us (level)
  starting transfers between devices: 14.5 us -> 11.5 us
  waiting for transfers between devices: 4.13 us -> 6.91 us
    ppermute x2, waiting for transfers between devices: 0.01 us -> 3.06 us  [per_device(): came[h] = lax.ppermute(rows, names, crossing(*h[::-1]))]
    ppermute x2, starting transfers between devices: 2.88 us -> 0.92 us  [per_device(): came[h] = lax.ppermute(rows, names, crossing(*h[::-1]))]
    ppermute x1, starting transfers between devices: 0.85 us -> 0.01 us  [per_device(): arrived += [came[h], lax.ppermute(rows, 'sat', [(0, 1), (1, 0)])]]
    pallas_call x6 -> x8, Pallas kernels: 6.4 us -> 6.5 us  [call(): pl.pallas_call(kernel, out_shape=outs, in_specs=[raw if i in anywhere els...]
  transfers between devices with their start and end apart: 10 -> 10, of which waited for: 5 -> 6; matrix products, arithmetic and copies ran while one was open for 0% -> 0% of each run, Pallas kernels for 18% -> 18%
where the time goes in v8:
time: 25.2 us; the launch traced here: 25 us
  starting transfers between devices  11.5 us (46%)
  waiting for transfers between devices  6.91 us (27%)
  Pallas kernels  6.5 us (26%)
    pallas_call x8, Pallas kernels, call(): pl.pallas_call(kernel, out_shape=outs, in_specs=[raw if i in anywhere els...  6.5 us
    ppermute x2, starting transfers between devices, per_device(): asked = {h: lax.ppermute(regions, names, crossing(*h)) for h in hands}  4.88 us
    ppermute x3, starting transfers between devices, per_device(): lax.ppermute(sent[k], names, crossing(k, k))  3.89 us
    ppermute x2, waiting for transfers between devices, per_device(): came[h] = lax.ppermute(rows, names, crossing(*h[::-1]))  3.06 us
    ppermute x3, waiting for transfers between devices, per_device(): lax.ppermute(sent[k], names, crossing(k, k))  1.45 us
    ppermute x1, starting transfers between devices, per_device(): early, late = ([mine], [lax.ppermute(mine, ('arc', 'sat'), over)])  1.36 us
    ppermute x1, waiting for transfers between devices, per_device(): early, late = ([mine], [lax.ppermute(mine, ('arc', 'sat'), over)])  0.98 us
    ppermute x2, starting transfers between devices, per_device(): came[h] = lax.ppermute(rows, names, crossing(*h[::-1]))  0.92 us
  transfers between devices with their start and end apart: 10, of which 6 were waited for; matrix products, arithmetic and copies ran while one was open for 0% of the time, Pallas kernels for 18%

profile of v8, /device:TPU:0, one launch (start us, length us, event | category | flops | bytes accessed | tf_op | source)
XLA Modules:
  0.0 25.0 jit_solution(8808663121589783263)
XLA Ops:
  0.0 0.5 %collective-permute-start.5 = (bf16[4,8,1,128,256]{4,3,2,1,0:T(8,128)(2,1)}, bf16[4,8,1,128,256]{4,3,2,1,0:T(8,128)(2,1)S(1)}, u32[]{:S(2)}, u32[]{:S(2)}) collective-permute-start(bf16[4,8,1,128,256]{4,3,2,1,0:T(8,128)(2,1)} %param.6), channel_id=1, source_target_pairs={{0,1},{1,0},{2,3},{3,2},{4,5},{5,4},{6,7},{7,6},{8,9},{9,8},{10,11... | collective-permute-start | bytes 6291464 | tf_op jit(solution)/shard_map/ppermute | solution.py:202
  0.5 4.7 %collective-permute-start = (s32[4,8]{1,0:T(4,128)}, s32[4,8]{1,0:T(4,128)S(1)}, u32[]{:S(2)}, u32[]{:S(2)}) collective-permute-start(s32[4,8]{1,0:T(4,128)} %refs_0_.1), channel_id=1, source_target_pairs={{0,7},{1,4},{2,5},{3,6},{4,3},{5,0},{6,1},{7,2},{8,15},{9,12},{10,... | collective-permute-start | bytes 392 | tf_op jit(solution)/shard_map/ppermute | solution.py:201
  5.2 0.2 collective-permute-start.1
  5.3 2.0 %load.1 = (bf16[480,256]{1,0:T(8,128)(2,1)S(1)}, s32[4,8]{1,0:T(4,128)S(1)}, f32[4,128]{1,0:T(4,128)S(1)}, f32[4,128]{1,0:T(4,128)S(1)}, bf16[32,128,256]{2,1,0:T(8,128)(2,1)S(1)}) custom-call(f32[480,1,256]{2,1,0:T(1,128)} %mascons.3, s32[4,8]{1,0:T(4,128)} %refs_0_.1, f32[4,128]{1,0:T(4,128)} %refs_1_.1, f32[4,128]{1,0:T(4,128)} %refs_2_.1, ...), custom_call_target="tpu_custom_call" | custom-call | flops 122880 | bytes 491520 | tf_op jit(solution)/shard_map/load/pallas_call | solution.py:168
  7.3 0.0 collective-permute-done.refs_0_
  7.3 0.4 %lookup.2 = bf16[8,256]{1,0:T(8,128)(2,1)S(1)} custom-call(s32[4,8]{1,0:T(4,128)S(1)} %collective-permute-done.refs_0_, bf16[480,256]{1,0:T(8,128)(2,1)S(1)} %get-tuple-element.22.refs_1_.table), custom_call_target="tpu_custom_call" | custom-call | flops 7864320 | bytes 491520 | tf_op jit(solution)/shard_map/lookup/pallas_call | solution.py:168
  7.7 0.7 %collective-permute-done.1.refs_0_ = s32[4,8]{1,0:T(4,128)S(1)} collective-permute-done((s32[4,8]{1,0:T(4,128)}, s32[4,8]{1,0:T(4,128)S(1)}, u32[]{:S(2)}, u32[]{:S(2)}) %collective-permute-start.1) | collective-permute-done | bytes 160 | tf_op jit(solution)/shard_map/ppermute | solution.py:201
  8.4 0.0 collective-permute-start.2
  8.4 0.4 %lookup.3 = bf16[8,256]{1,0:T(8,128)(2,1)S(1)} custom-call(s32[4,8]{1,0:T(4,128)S(1)} %collective-permute-done.1.refs_0_, bf16[480,256]{1,0:T(8,128)(2,1)S(1)} %get-tuple-element.22.refs_1_.table), custom_call_target="tpu_custom_call" | custom-call | flops 7864320 | bytes 491520 | tf_op jit(solution)/shard_map/lookup/pallas_call | solution.py:168
  8.8 0.9 %collective-permute-start.4 = (bf16[8,256]{1,0:T(8,128)(2,1)S(1)}, bf16[8,256]{1,0:T(8,128)(2,1)S(1)}, u32[]{:S(2)}, u32[]{:S(2)}) collective-permute-start(bf16[8,256]{1,0:T(8,128)(2,1)S(1)} %lookup.3), channel_id=1, source_target_pairs={{0,3},{1,2},{2,1},{3,0},{4,7},{5,6},{6,5},{7,4},{8,11},{9,10},{10,... | collective-permute-start | bytes 12296 | tf_op jit(solution)/shard_map/ppermute | solution.py:228
  9.7 0.5 %plan.1 = (f32[32,256]{1,0:T(8,128)S(1)}, f32[32,24]{1,0:T(8,128)S(1)}, f32[32,32]{1,0:T(8,128)S(1)}, f32[32,128]{1,0:T(8,128)S(1)}, f32[128,8]{1,0:T(8,128)S(1)}) custom-call(s32[4,8]{1,0:T(4,128)S(1)} %get-tuple-element.25.ids, f32[4,128]{1,0:T(4,128)S(1)} %get-tuple-element.26.observed, f32[4,128]{1,0:T(4,128)S(1)} %get-tuple-element.27.weights, ...), custom_call_target="tpu_custom_call" | custom-call | flops 262144 | bytes 32768 | tf_op jit(solution)/shard_map/plan/pallas_call | solution.py:168
  10.2 3.1 %collective-permute-done.2.refs_0_ = bf16[8,256]{1,0:T(8,128)(2,1)S(1)} collective-permute-done((bf16[8,256]{1,0:T(8,128)(2,1)S(1)}, bf16[8,256]{1,0:T(8,128)(2,1)S(1)}, u32[]{:S(2)}, u32[]{:S(2)}) %collective-permute-start.2) | collective-permute-done | bytes 4128 | tf_op jit(solution)/shard_map/ppermute | solution.py:228
  13.2 0.0 collective-permute-start.3
  13.2 0.0 collective-permute-done.5
  13.2 0.4 %differ.1.refs_8_ = f32[32,128,256]{2,1,0:T(8,128)S(1)} custom-call(bf16[32,128,256]{2,1,0:T(8,128)(2,1)S(1)} %get-tuple-element.34.mine, bf16[32,128,256]{2,1,0:T(8,128)(2,1)S(1)} %bitcast.7), custom_call_target="tpu_custom_call" | custom-call | flops 1048576 | bytes 8388608 | tf_op jit(solution)/shard_map/differ/pallas_call | solution.py:168
  13.7 0.0 collective-permute-done.4.refs_2_
  13.7 0.7 %collective-permute-done.3.refs_1_ = bf16[8,256]{1,0:T(8,128)(2,1)S(1)} collective-permute-done((bf16[8,256]{1,0:T(8,128)(2,1)S(1)}, bf16[8,256]{1,0:T(8,128)(2,1)S(1)}, u32[]{:S(2)}, u32[]{:S(2)}) %collective-permute-start.3) | collective-permute-done | bytes 4128 | tf_op jit(solution)/shard_map/ppermute | solution.py:255
  14.4 0.0 copy-start
  14.4 1.0 %solve.1 = (bf16[8,384]{1,0:T(8,128)(2,1)S(1)}, bf16[8,384]{1,0:T(8,128)(2,1)S(1)}, bf16[8,384]{1,0:T(8,128)(2,1)S(1)}, bf16[8,384]{1,0:T(8,128)(2,1)S(1)}) custom-call(bf16[8,256]{1,0:T(8,128)(2,1)S(1)} %collective-permute-done.2.refs_0_, bf16[8,256]{1,0:T(8,128)(2,1)S(1)} %collective-permute-done.3.refs_1_, ...), custom_call_target="tpu_custom_call" | custom-call | flops 4194304 | bytes 4194304 | tf_op jit(solution)/shard_map/solve/pallas_call | solution.py:168
  15.4 1.3 %collective-permute-start.6 = (bf16[8,384]{1,0:T(8,128)(2,1)S(1)}, bf16[8,384]{1,0:T(8,128)(2,1)S(1)}, u32[]{:S(2)}, u32[]{:S(2)}) collective-permute-start(bf16[8,384]{1,0:T(8,128)(2,1)S(1)} %get-tuple-element.36), channel_id=1, source_target_pairs={{0,7},{1,6},{2,5},{3,4},{4,3},{5,2},{6,1},{7,0},{8,15},{9,14},{10,... | collective-permute-start | bytes 18440 | tf_op jit(solution)/shard_map/ppermute | solution.py:265
  16.8 0.0 collective-permute-start.7
  16.8 2.5 %collective-permute-start.8 = (bf16[8,384]{1,0:T(8,128)(2,1)S(1)}, bf16[8,384]{1,0:T(8,128)(2,1)S(1)}, u32[]{:S(2)}, u32[]{:S(2)}) collective-permute-start(bf16[8,384]{1,0:T(8,128)(2,1)S(1)} %get-tuple-element.38), channel_id=1, source_target_pairs={{0,3},{1,2},{2,1},{3,0},{4,7},{5,6},{6,5},{7,4},{8,11},{9,10},{10,... | collective-permute-start | bytes 18440 | tf_op jit(solution)/shard_map/ppermute | solution.py:265
  19.3 1.0 %collective-permute-done.6 = bf16[8,384]{1,0:T(8,128)(2,1)S(1)} collective-permute-done((bf16[8,384]{1,0:T(8,128)(2,1)S(1)}, bf16[8,384]{1,0:T(8,128)(2,1)S(1)}, u32[]{:S(2)}, u32[]{:S(2)}) %collective-permute-start.6) | collective-permute-done | bytes 6176 | tf_op jit(solution)/shard_map/ppermute | solution.py:265
  20.3 0.5 %collective-permute-done.7 = bf16[8,384]{1,0:T(8,128)(2,1)S(1)} collective-permute-done((bf16[8,384]{1,0:T(8,128)(2,1)S(1)}, bf16[8,384]{1,0:T(8,128)(2,1)S(1)}, u32[]{:S(2)}, u32[]{:S(2)}) %collective-permute-start.7) | collective-permute-done | bytes 6176 | tf_op jit(solution)/shard_map/ppermute | solution.py:265
  20.8 0.0 collective-permute-done.8
  20.8 1.4 %collective-permute-start.9 = (bf16[4,8,384]{2,1,0:T(8,128)(2,1)S(1)}, bf16[4,8,384]{2,1,0:T(8,128)(2,1)S(1)}, u32[]{:S(2)}, u32[]{:S(2)}) collective-permute-start(bf16[4,8,384]{2,1,0:T(8,128)(2,1)S(1)} %pad_maximum_fusion.refs_0_), channel_id=1, source_target_pairs={{0,9},{1,8},{8,1},{9,0},{2,11},{3,10},{10,3},{11,2},{4,13},{5,12},... | collective-permute-start | bytes 73736 | tf_op jit(solution)/shard_map/ppermute | solution.py:269
  22.2 0.0 copy-done
  22.2 1.0 %base.1.refs_1_ = f32[120,256]{1,0:T(8,128)S(1)} custom-call(f32[480,1,256]{2,1,0:T(1,128)} %mascons.3, f32[1,256]{1,0:T(1,128)S(1)} %bitcast.9, bf16[4,8,384]{2,1,0:T(8,128)(2,1)S(1)} %pad_maximum_fusion.refs_0_), custom_call_target="tpu_custom_call" | custom-call | flops 1966080 | bytes 245760 | tf_op jit(solution)/shard_map/base/pallas_call | solution.py:168
  23.1 1.0 %collective-permute-done.9.refs_0_ = bf16[4,8,384]{2,1,0:T(8,128)(2,1)S(1)} collective-permute-done((bf16[4,8,384]{2,1,0:T(8,128)(2,1)S(1)}, bf16[4,8,384]{2,1,0:T(8,128)(2,1)S(1)}, u32[]{:S(2)}, u32[]{:S(2)}) %collective-permute-start.9) | collective-permute-done | bytes 24608 | tf_op jit(solution)/shard_map/ppermute | solution.py:269
  24.1 0.9 %place.1 = f32[120,1,256]{2,1,0:T(1,128)} custom-call(bf16[4,8,384]{2,1,0:T(8,128)(2,1)S(1)} %collective-permute-done.9.refs_0_, f32[120,256]{1,0:T(8,128)S(1)} %base.1.refs_1_), custom_call_target="tpu_custom_call" | custom-call | flops 3932160 | bytes 245760 | tf_op jit(solution)/shard_map/place/pallas_call | solution.py:168
  (1 shorter events, 0.0 us)
Async XLA Ops:
  0.0 13.2 %collective-permute-start.5 = (bf16[4,8,1,128,256]{4,3,2,1,0:T(8,128)(2,1)}, bf16[4,8,1,128,256]{4,3,2,1,0:T(8,128)(2,1)S(1)}, u32[]{:S(2)}, u32[]{:S(2)}) collective-permute-start(bf16[4,8,1,128,256]{4,3,2,1,0:T(8,128)(2,1)} %param.6), channel_id=1, source_target_pairs={{0,1},{1,0},{2,3},{3,2},{4,5},{5,4},{6,7},{7,6},{8,9},{9,8},{10,11... | collective-permute-start | bytes 6291464 | tf_op jit(solution)/shard_map/ppermute | solution.py:202
  0.5 6.9 %collective-permute-start = (s32[4,8]{1,0:T(4,128)}, s32[4,8]{1,0:T(4,128)S(1)}, u32[]{:S(2)}, u32[]{:S(2)}) collective-permute-start(s32[4,8]{1,0:T(4,128)} %refs_0_.1), channel_id=1, source_target_pairs={{0,7},{1,4},{2,5},{3,6},{4,3},{5,0},{6,1},{7,2},{8,15},{9,12},{10,... | collective-permute-start | bytes 392 | tf_op jit(solution)/shard_map/ppermute | solution.py:201
  5.2 3.2 %collective-permute-start.1 = (s32[4,8]{1,0:T(4,128)}, s32[4,8]{1,0:T(4,128)S(1)}, u32[]{:S(2)}, u32[]{:S(2)}) collective-permute-start(s32[4,8]{1,0:T(4,128)} %refs_0_.1), channel_id=1, source_target_pairs={{0,3},{1,2},{2,1},{3,0},{4,7},{5,6},{6,5},{7,4},{8,11},{9,10},{10,... | collective-permute-start | bytes 392 | tf_op jit(solution)/shard_map/ppermute | solution.py:201
  8.4 4.8 %collective-permute-start.2 = (bf16[8,256]{1,0:T(8,128)(2,1)S(1)}, bf16[8,256]{1,0:T(8,128)(2,1)S(1)}, u32[]{:S(2)}, u32[]{:S(2)}) collective-permute-start(bf16[8,256]{1,0:T(8,128)(2,1)S(1)} %lookup.2), channel_id=1, source_target_pairs={{0,5},{1,6},{2,7},{3,4},{4,1},{5,2},{6,3},{7,0},{8,13},{9,14},{10,... | collective-permute-start | bytes 12296 | tf_op jit(solution)/shard_map/ppermute | solution.py:228
  8.8 4.9 %collective-permute-start.4 = (bf16[8,256]{1,0:T(8,128)(2,1)S(1)}, bf16[8,256]{1,0:T(8,128)(2,1)S(1)}, u32[]{:S(2)}, u32[]{:S(2)}) collective-permute-start(bf16[8,256]{1,0:T(8,128)(2,1)S(1)} %lookup.3), channel_id=1, source_target_pairs={{0,3},{1,2},{2,1},{3,0},{4,7},{5,6},{6,5},{7,4},{8,11},{9,10},{10,... | collective-permute-start | bytes 12296 | tf_op jit(solution)/shard_map/ppermute | solution.py:228
  13.2 1.2 %collective-permute-start.3 = (bf16[8,256]{1,0:T(8,128)(2,1)S(1)}, bf16[8,256]{1,0:T(8,128)(2,1)S(1)}, u32[]{:S(2)}, u32[]{:S(2)}) collective-permute-start(bf16[8,256]{1,0:T(8,128)(2,1)S(1)} %collective-permute-done.2.refs_0_), channel_id=1, source_target_pairs={{0,1},{1,0},{2,3},{3,2},{4,5},{5,4},{6,7},{7,6},{8,9},{9,8},{10,11... | collective-permute-start | bytes 12296 | tf_op jit(solution)/shard_map/ppermute | solution.py:255
  14.4 7.8 %copy-start = (f32[256]{0:T(256)S(1)}, f32[256]{0:T(256)}, u32[]{:S(2)}) copy-start(f32[256]{0:T(256)} %param.11) | copy-start | bytes 3076
  15.4 4.9 %collective-permute-start.6 = (bf16[8,384]{1,0:T(8,128)(2,1)S(1)}, bf16[8,384]{1,0:T(8,128)(2,1)S(1)}, u32[]{:S(2)}, u32[]{:S(2)}) collective-permute-start(bf16[8,384]{1,0:T(8,128)(2,1)S(1)} %get-tuple-element.36), channel_id=1, source_target_pairs={{0,7},{1,6},{2,5},{3,4},{4,3},{5,2},{6,1},{7,0},{8,15},{9,14},{10,... | collective-permute-start | bytes 18440 | tf_op jit(solution)/shard_map/ppermute | solution.py:265
  16.8 4.0 %collective-permute-start.7 = (bf16[8,384]{1,0:T(8,128)(2,1)S(1)}, bf16[8,384]{1,0:T(8,128)(2,1)S(1)}, u32[]{:S(2)}, u32[]{:S(2)}) collective-permute-start(bf16[8,384]{1,0:T(8,128)(2,1)S(1)} %get-tuple-element.37), channel_id=1, source_target_pairs={{0,5},{1,4},{2,7},{3,6},{4,1},{5,0},{6,3},{7,2},{8,13},{9,12},{10,... | collective-permute-start | bytes 18440 | tf_op jit(solution)/shard_map/ppermute | solution.py:265
  16.8 4.0 %collective-permute-start.8 = (bf16[8,384]{1,0:T(8,128)(2,1)S(1)}, bf16[8,384]{1,0:T(8,128)(2,1)S(1)}, u32[]{:S(2)}, u32[]{:S(2)}) collective-permute-start(bf16[8,384]{1,0:T(8,128)(2,1)S(1)} %get-tuple-element.38), channel_id=1, source_target_pairs={{0,3},{1,2},{2,1},{3,0},{4,7},{5,6},{6,5},{7,4},{8,11},{9,10},{10,... | collective-permute-start | bytes 18440 | tf_op jit(solution)/shard_map/ppermute | solution.py:265
  20.8 3.3 %collective-permute-start.9 = (bf16[4,8,384]{2,1,0:T(8,128)(2,1)S(1)}, bf16[4,8,384]{2,1,0:T(8,128)(2,1)S(1)}, u32[]{:S(2)}, u32[]{:S(2)}) collective-permute-start(bf16[4,8,384]{2,1,0:T(8,128)(2,1)S(1)} %pad_maximum_fusion.refs_0_), channel_id=1, source_target_pairs={{0,9},{1,8},{8,1},{9,0},{2,11},{3,10},{10,3},{11,2},{4,13},{5,12},... | collective-permute-start | bytes 73736 | tf_op jit(solution)/shard_map/ppermute | solution.py:269

commit v9 on v8

--- a/solution.py
+++ b/solution.py
@@ -58,21 +58,14 @@
     n = (len(refs) - 3) // 2
     others, table, outs = refs[:n], refs[n], refs[n + 1 : 2 * n + 1]
     held, sems = refs[2 * n + 1 :]
-    parts = sems.shape[0] - n
-    step = table.shape[0] // parts
-    copies = []
-    for p in range(parts):
-        part = pl.ds(p * step, step)
-        copies.append(pltpu.make_async_copy(mascons.at[part, 0, :], held.at[part], sems.at[p]))
+    copies = [pltpu.make_async_copy(mascons.at[:, 0, :], held, sems.at[n])]
     for j, (i, o) in enumerate(zip(others, outs)):
-        copies.append(pltpu.make_async_copy(i, o, sems.at[parts + j]))
+        copies.append(pltpu.make_async_copy(i, o, sems.at[j]))
     for copy in copies:
         copy.start()
-    for p in range(parts):
-        copies[p].wait()
-        rows = slice(p * step, (p + 1) * step)
-        table[rows, :] = held[rows, :].astype(BF16)
-    for copy in copies[parts:]:
+    copies[0].wait()
+    table[...] = held[...].astype(BF16)
+    for copy in copies[1:]:
         copy.wait()
 
 
@@ -208,7 +201,7 @@
         [mascons, *loads],
         group * width,
         group * width * 4,
-        [VMEM((group, width), F32), dma((4 + len(loads),))],
+        [VMEM((group, width), F32), dma((1 + len(loads),))],
         range(1 + len(loads)),
     )
     found, came = {}, {}

time: 25.2 us -> 25.1 us (level)
  no operation moved by 1% of the time
where the time goes in v9:
time: 25.1 us; the launch traced here: 25 us
  starting transfers between devices  11.4 us (45%)
  waiting for transfers between devices  7.14 us (28%)
  Pallas kernels  6.38 us (25%)
    pallas_call x8, Pallas kernels, call(): pl.pallas_call(kernel, out_shape=outs, in_specs=[raw if i in anywhere els...  6.38 us
    ppermute x2, starting transfers between devices, per_device(): asked = {h: lax.ppermute(regions, names, crossing(*h)) for h in hands}  4.88 us
    ppermute x3, starting transfers between devices, per_device(): lax.ppermute(sent[k], names, crossing(k, k))  3.89 us
    ppermute x2, waiting for transfers between devices, per_device(): came[h] = lax.ppermute(rows, names, crossing(*h[::-1]))  3.17 us
    ppermute x3, waiting for transfers between devices, per_device(): lax.ppermute(sent[k], names, crossing(k, k))  1.45 us
    ppermute x1, starting transfers between devices, per_device(): early, late = ([mine], [lax.ppermute(mine, ('arc', 'sat'), over)])  1.36 us
    ppermute x1, waiting for transfers between devices, per_device(): early, late = ([mine], [lax.ppermute(mine, ('arc', 'sat'), over)])  0.98 us
    ppermute x2, waiting for transfers between devices, per_device(): asked = {h: lax.ppermute(regions, names, crossing(*h)) for h in hands}  0.8 us
  transfers between devices with their start and end apart: 10, of which 6 were waited for; matrix products, arithmetic and copies ran while one was open for 0% of the time, Pallas kernels for 18%

profile of v9, /device:TPU:0, one launch (start us, length us, event | category | flops | bytes accessed | tf_op | source)
XLA Modules:
  0.0 25.0 jit_solution(9176909277517518305)
XLA Ops:
  0.0 0.5 %collective-permute-start.5 = (bf16[4,8,1,128,256]{4,3,2,1,0:T(8,128)(2,1)}, bf16[4,8,1,128,256]{4,3,2,1,0:T(8,128)(2,1)S(1)}, u32[]{:S(2)}, u32[]{:S(2)}) collective-permute-start(bf16[4,8,1,128,256]{4,3,2,1,0:T(8,128)(2,1)} %param.6), channel_id=1, source_target_pairs={{0,1},{1,0},{2,3},{3,2},{4,5},{5,4},{6,7},{7,6},{8,9},{9,8},{10,11... | collective-permute-start | bytes 6291464 | tf_op jit(solution)/shard_map/ppermute | solution.py:195
  0.5 4.7 %collective-permute-start = (s32[4,8]{1,0:T(4,128)}, s32[4,8]{1,0:T(4,128)S(1)}, u32[]{:S(2)}, u32[]{:S(2)}) collective-permute-start(s32[4,8]{1,0:T(4,128)} %refs_0_.1), channel_id=1, source_target_pairs={{0,7},{1,4},{2,5},{3,6},{4,3},{5,0},{6,1},{7,2},{8,15},{9,12},{10,... | collective-permute-start | bytes 392 | tf_op jit(solution)/shard_map/ppermute | solution.py:194
  5.2 0.2 collective-permute-start.1
  5.3 1.8 %load.1 = (bf16[480,256]{1,0:T(8,128)(2,1)S(1)}, s32[4,8]{1,0:T(4,128)S(1)}, f32[4,128]{1,0:T(4,128)S(1)}, f32[4,128]{1,0:T(4,128)S(1)}, bf16[32,128,256]{2,1,0:T(8,128)(2,1)S(1)}) custom-call(f32[480,1,256]{2,1,0:T(1,128)} %mascons.3, s32[4,8]{1,0:T(4,128)} %refs_0_.1, f32[4,128]{1,0:T(4,128)} %refs_1_.1, f32[4,128]{1,0:T(4,128)} %refs_2_.1, ...), custom_call_target="tpu_custom_call" | custom-call | flops 122880 | bytes 491520 | tf_op jit(solution)/shard_map/load/pallas_call | solution.py:161
  7.2 0.0 collective-permute-done.refs_0_
  7.2 0.4 %lookup.2 = bf16[8,256]{1,0:T(8,128)(2,1)S(1)} custom-call(s32[4,8]{1,0:T(4,128)S(1)} %collective-permute-done.refs_0_, bf16[480,256]{1,0:T(8,128)(2,1)S(1)} %get-tuple-element.22.refs_1_.table), custom_call_target="tpu_custom_call" | custom-call | flops 7864320 | bytes 491520 | tf_op jit(solution)/shard_map/lookup/pallas_call | solution.py:161
  7.6 0.8 %collective-permute-done.1.refs_0_ = s32[4,8]{1,0:T(4,128)S(1)} collective-permute-done((s32[4,8]{1,0:T(4,128)}, s32[4,8]{1,0:T(4,128)S(1)}, u32[]{:S(2)}, u32[]{:S(2)}) %collective-permute-start.1) | collective-permute-done | bytes 160 | tf_op jit(solution)/shard_map/ppermute | solution.py:194
  8.4 0.0 collective-permute-start.2
  8.4 0.4 %lookup.3 = bf16[8,256]{1,0:T(8,128)(2,1)S(1)} custom-call(s32[4,8]{1,0:T(4,128)S(1)} %collective-permute-done.1.refs_0_, bf16[480,256]{1,0:T(8,128)(2,1)S(1)} %get-tuple-element.22.refs_1_.table), custom_call_target="tpu_custom_call" | custom-call | flops 7864320 | bytes 491520 | tf_op jit(solution)/shard_map/lookup/pallas_call | solution.py:161
  8.8 0.8 %collective-permute-start.4 = (bf16[8,256]{1,0:T(8,128)(2,1)S(1)}, bf16[8,256]{1,0:T(8,128)(2,1)S(1)}, u32[]{:S(2)}, u32[]{:S(2)}) collective-permute-start(bf16[8,256]{1,0:T(8,128)(2,1)S(1)} %lookup.3), channel_id=1, source_target_pairs={{0,3},{1,2},{2,1},{3,0},{4,7},{5,6},{6,5},{7,4},{8,11},{9,10},{10,... | collective-permute-start | bytes 12296 | tf_op jit(solution)/shard_map/ppermute | solution.py:221
  9.6 0.5 %plan.1 = (f32[32,256]{1,0:T(8,128)S(1)}, f32[32,24]{1,0:T(8,128)S(1)}, f32[32,32]{1,0:T(8,128)S(1)}, f32[32,128]{1,0:T(8,128)S(1)}, f32[128,8]{1,0:T(8,128)S(1)}) custom-call(s32[4,8]{1,0:T(4,128)S(1)} %get-tuple-element.25.ids, f32[4,128]{1,0:T(4,128)S(1)} %get-tuple-element.26.observed, f32[4,128]{1,0:T(4,128)S(1)} %get-tuple-element.27.weights, ...), custom_call_target="tpu_custom_call" | custom-call | flops 262144 | bytes 32768 | tf_op jit(solution)/shard_map/plan/pallas_call | solution.py:161
  10.1 3.2 %collective-permute-done.2.refs_0_ = bf16[8,256]{1,0:T(8,128)(2,1)S(1)} collective-permute-done((bf16[8,256]{1,0:T(8,128)(2,1)S(1)}, bf16[8,256]{1,0:T(8,128)(2,1)S(1)}, u32[]{:S(2)}, u32[]{:S(2)}) %collective-permute-start.2) | collective-permute-done | bytes 4128 | tf_op jit(solution)/shard_map/ppermute | solution.py:221
  13.2 0.0 collective-permute-start.3
  13.2 0.0 collective-permute-done.5
  13.2 0.4 %differ.1.refs_8_ = f32[32,128,256]{2,1,0:T(8,128)S(1)} custom-call(bf16[32,128,256]{2,1,0:T(8,128)(2,1)S(1)} %get-tuple-element.34.mine, bf16[32,128,256]{2,1,0:T(8,128)(2,1)S(1)} %bitcast.7), custom_call_target="tpu_custom_call" | custom-call | flops 1048576 | bytes 8388608 | tf_op jit(solution)/shard_map/differ/pallas_call | solution.py:161
  13.6 0.0 collective-permute-done.4.refs_2_
  13.6 0.7 %collective-permute-done.3.refs_1_ = bf16[8,256]{1,0:T(8,128)(2,1)S(1)} collective-permute-done((bf16[8,256]{1,0:T(8,128)(2,1)S(1)}, bf16[8,256]{1,0:T(8,128)(2,1)S(1)}, u32[]{:S(2)}, u32[]{:S(2)}) %collective-permute-start.3) | collective-permute-done | bytes 4128 | tf_op jit(solution)/shard_map/ppermute | solution.py:248
  14.4 0.0 copy-start
  14.4 1.0 %solve.1 = (bf16[8,384]{1,0:T(8,128)(2,1)S(1)}, bf16[8,384]{1,0:T(8,128)(2,1)S(1)}, bf16[8,384]{1,0:T(8,128)(2,1)S(1)}, bf16[8,384]{1,0:T(8,128)(2,1)S(1)}) custom-call(bf16[8,256]{1,0:T(8,128)(2,1)S(1)} %collective-permute-done.2.refs_0_, bf16[8,256]{1,0:T(8,128)(2,1)S(1)} %collective-permute-done.3.refs_1_, ...), custom_call_target="tpu_custom_call" | custom-call | flops 4194304 | bytes 4194304 | tf_op jit(solution)/shard_map/solve/pallas_call | solution.py:161
  15.4 1.3 %collective-permute-start.6 = (bf16[8,384]{1,0:T(8,128)(2,1)S(1)}, bf16[8,384]{1,0:T(8,128)(2,1)S(1)}, u32[]{:S(2)}, u32[]{:S(2)}) collective-permute-start(bf16[8,384]{1,0:T(8,128)(2,1)S(1)} %get-tuple-element.36), channel_id=1, source_target_pairs={{0,7},{1,6},{2,5},{3,4},{4,3},{5,2},{6,1},{7,0},{8,15},{9,14},{10,... | collective-permute-start | bytes 18440 | tf_op jit(solution)/shard_map/ppermute | solution.py:258
  16.7 0.1 collective-permute-start.7
  16.8 2.5 %collective-permute-start.8 = (bf16[8,384]{1,0:T(8,128)(2,1)S(1)}, bf16[8,384]{1,0:T(8,128)(2,1)S(1)}, u32[]{:S(2)}, u32[]{:S(2)}) collective-permute-start(bf16[8,384]{1,0:T(8,128)(2,1)S(1)} %get-tuple-element.38), channel_id=1, source_target_pairs={{0,3},{1,2},{2,1},{3,0},{4,7},{5,6},{6,5},{7,4},{8,11},{9,10},{10,... | collective-permute-start | bytes 18440 | tf_op jit(solution)/shard_map/ppermute | solution.py:258
  19.3 1.0 %collective-permute-done.6 = bf16[8,384]{1,0:T(8,128)(2,1)S(1)} collective-permute-done((bf16[8,384]{1,0:T(8,128)(2,1)S(1)}, bf16[8,384]{1,0:T(8,128)(2,1)S(1)}, u32[]{:S(2)}, u32[]{:S(2)}) %collective-permute-start.6) | collective-permute-done | bytes 6176 | tf_op jit(solution)/shard_map/ppermute | solution.py:258
  20.3 0.5 %collective-permute-done.7 = bf16[8,384]{1,0:T(8,128)(2,1)S(1)} collective-permute-done((bf16[8,384]{1,0:T(8,128)(2,1)S(1)}, bf16[8,384]{1,0:T(8,128)(2,1)S(1)}, u32[]{:S(2)}, u32[]{:S(2)}) %collective-permute-start.7) | collective-permute-done | bytes 6176 | tf_op jit(solution)/shard_map/ppermute | solution.py:258
  20.8 0.0 collective-permute-done.8
  20.8 1.4 %collective-permute-start.9 = (bf16[4,8,384]{2,1,0:T(8,128)(2,1)S(1)}, bf16[4,8,384]{2,1,0:T(8,128)(2,1)S(1)}, u32[]{:S(2)}, u32[]{:S(2)}) collective-permute-start(bf16[4,8,384]{2,1,0:T(8,128)(2,1)S(1)} %pad_maximum_fusion.refs_0_), channel_id=1, source_target_pairs={{0,9},{1,8},{8,1},{9,0},{2,11},{3,10},{10,3},{11,2},{4,13},{5,12},... | collective-permute-start | bytes 73736 | tf_op jit(solution)/shard_map/ppermute | solution.py:262
  22.1 0.0 copy-done
  22.1 1.0 %base.1.refs_1_ = f32[120,256]{1,0:T(8,128)S(1)} custom-call(f32[480,1,256]{2,1,0:T(1,128)} %mascons.3, f32[1,256]{1,0:T(1,128)S(1)} %bitcast.9, bf16[4,8,384]{2,1,0:T(8,128)(2,1)S(1)} %pad_maximum_fusion.refs_0_), custom_call_target="tpu_custom_call" | custom-call | flops 1966080 | bytes 245760 | tf_op jit(solution)/shard_map/base/pallas_call | solution.py:161
  23.1 1.0 %collective-permute-done.9.refs_0_ = bf16[4,8,384]{2,1,0:T(8,128)(2,1)S(1)} collective-permute-done((bf16[4,8,384]{2,1,0:T(8,128)(2,1)S(1)}, bf16[4,8,384]{2,1,0:T(8,128)(2,1)S(1)}, u32[]{:S(2)}, u32[]{:S(2)}) %collective-permute-start.9) | collective-permute-done | bytes 24608 | tf_op jit(solution)/shard_map/ppermute | solution.py:262
  24.1 0.9 %place.1 = f32[120,1,256]{2,1,0:T(1,128)} custom-call(bf16[4,8,384]{2,1,0:T(8,128)(2,1)S(1)} %collective-permute-done.9.refs_0_, f32[120,256]{1,0:T(8,128)S(1)} %base.1.refs_1_), custom_call_target="tpu_custom_call" | custom-call | flops 3932160 | bytes 245760 | tf_op jit(solution)/shard_map/place/pallas_call | solution.py:161
  (1 shorter events, 0.0 us)
Async XLA Ops:
  0.0 13.2 %collective-permute-start.5 = (bf16[4,8,1,128,256]{4,3,2,1,0:T(8,128)(2,1)}, bf16[4,8,1,128,256]{4,3,2,1,0:T(8,128)(2,1)S(1)}, u32[]{:S(2)}, u32[]{:S(2)}) collective-permute-start(bf16[4,8,1,128,256]{4,3,2,1,0:T(8,128)(2,1)} %param.6), channel_id=1, source_target_pairs={{0,1},{1,0},{2,3},{3,2},{4,5},{5,4},{6,7},{7,6},{8,9},{9,8},{10,11... | collective-permute-start | bytes 6291464 | tf_op jit(solution)/shard_map/ppermute | solution.py:195
  0.5 6.7 %collective-permute-start = (s32[4,8]{1,0:T(4,128)}, s32[4,8]{1,0:T(4,128)S(1)}, u32[]{:S(2)}, u32[]{:S(2)}) collective-permute-start(s32[4,8]{1,0:T(4,128)} %refs_0_.1), channel_id=1, source_target_pairs={{0,7},{1,4},{2,5},{3,6},{4,3},{5,0},{6,1},{7,2},{8,15},{9,12},{10,... | collective-permute-start | bytes 392 | tf_op jit(solution)/shard_map/ppermute | solution.py:194
  5.2 3.2 %collective-permute-start.1 = (s32[4,8]{1,0:T(4,128)}, s32[4,8]{1,0:T(4,128)S(1)}, u32[]{:S(2)}, u32[]{:S(2)}) collective-permute-start(s32[4,8]{1,0:T(4,128)} %refs_0_.1), channel_id=1, source_target_pairs={{0,3},{1,2},{2,1},{3,0},{4,7},{5,6},{6,5},{7,4},{8,11},{9,10},{10,... | collective-permute-start | bytes 392 | tf_op jit(solution)/shard_map/ppermute | solution.py:194
  8.4 4.8 %collective-permute-start.2 = (bf16[8,256]{1,0:T(8,128)(2,1)S(1)}, bf16[8,256]{1,0:T(8,128)(2,1)S(1)}, u32[]{:S(2)}, u32[]{:S(2)}) collective-permute-start(bf16[8,256]{1,0:T(8,128)(2,1)S(1)} %lookup.2), channel_id=1, source_target_pairs={{0,5},{1,6},{2,7},{3,4},{4,1},{5,2},{6,3},{7,0},{8,13},{9,14},{10,... | collective-permute-start | bytes 12296 | tf_op jit(solution)/shard_map/ppermute | solution.py:221
  8.8 4.9 %collective-permute-start.4 = (bf16[8,256]{1,0:T(8,128)(2,1)S(1)}, bf16[8,256]{1,0:T(8,128)(2,1)S(1)}, u32[]{:S(2)}, u32[]{:S(2)}) collective-permute-start(bf16[8,256]{1,0:T(8,128)(2,1)S(1)} %lookup.3), channel_id=1, source_target_pairs={{0,3},{1,2},{2,1},{3,0},{4,7},{5,6},{6,5},{7,4},{8,11},{9,10},{10,... | collective-permute-start | bytes 12296 | tf_op jit(solution)/shard_map/ppermute | solution.py:221
  13.2 1.2 %collective-permute-start.3 = (bf16[8,256]{1,0:T(8,128)(2,1)S(1)}, bf16[8,256]{1,0:T(8,128)(2,1)S(1)}, u32[]{:S(2)}, u32[]{:S(2)}) collective-permute-start(bf16[8,256]{1,0:T(8,128)(2,1)S(1)} %collective-permute-done.2.refs_0_), channel_id=1, source_target_pairs={{0,1},{1,0},{2,3},{3,2},{4,5},{5,4},{6,7},{7,6},{8,9},{9,8},{10,11... | collective-permute-start | bytes 12296 | tf_op jit(solution)/shard_map/ppermute | solution.py:248
  14.4 7.8 %copy-start = (f32[256]{0:T(256)S(1)}, f32[256]{0:T(256)}, u32[]{:S(2)}) copy-start(f32[256]{0:T(256)} %param.11) | copy-start | bytes 3076
  15.4 4.9 %collective-permute-start.6 = (bf16[8,384]{1,0:T(8,128)(2,1)S(1)}, bf16[8,384]{1,0:T(8,128)(2,1)S(1)}, u32[]{:S(2)}, u32[]{:S(2)}) collective-permute-start(bf16[8,384]{1,0:T(8,128)(2,1)S(1)} %get-tuple-element.36), channel_id=1, source_target_pairs={{0,7},{1,6},{2,5},{3,4},{4,3},{5,2},{6,1},{7,0},{8,15},{9,14},{10,... | collective-permute-start | bytes 18440 | tf_op jit(solution)/shard_map/ppermute | solution.py:258
  16.7 4.0 %collective-permute-start.7 = (bf16[8,384]{1,0:T(8,128)(2,1)S(1)}, bf16[8,384]{1,0:T(8,128)(2,1)S(1)}, u32[]{:S(2)}, u32[]{:S(2)}) collective-permute-start(bf16[8,384]{1,0:T(8,128)(2,1)S(1)} %get-tuple-element.37), channel_id=1, source_target_pairs={{0,5},{1,4},{2,7},{3,6},{4,1},{5,0},{6,3},{7,2},{8,13},{9,12},{10,... | collective-permute-start | bytes 18440 | tf_op jit(solution)/shard_map/ppermute | solution.py:258
  16.8 3.9 %collective-permute-start.8 = (bf16[8,384]{1,0:T(8,128)(2,1)S(1)}, bf16[8,384]{1,0:T(8,128)(2,1)S(1)}, u32[]{:S(2)}, u32[]{:S(2)}) collective-permute-start(bf16[8,384]{1,0:T(8,128)(2,1)S(1)} %get-tuple-element.38), channel_id=1, source_target_pairs={{0,3},{1,2},{2,1},{3,0},{4,7},{5,6},{6,5},{7,4},{8,11},{9,10},{10,... | collective-permute-start | bytes 18440 | tf_op jit(solution)/shard_map/ppermute | solution.py:258
  20.8 3.3 %collective-permute-start.9 = (bf16[4,8,384]{2,1,0:T(8,128)(2,1)S(1)}, bf16[4,8,384]{2,1,0:T(8,128)(2,1)S(1)}, u32[]{:S(2)}, u32[]{:S(2)}) collective-permute-start(bf16[4,8,384]{2,1,0:T(8,128)(2,1)S(1)} %pad_maximum_fusion.refs_0_), channel_id=1, source_target_pairs={{0,9},{1,8},{8,1},{9,0},{2,11},{3,10},{10,3},{11,2},{4,13},{5,12},... | collective-permute-start | bytes 73736 | tf_op jit(solution)/shard_map/ppermute | solution.py:262

commit v10 on v9

--- a/solution.py
+++ b/solution.py
@@ -91,10 +91,10 @@
         turn += jnp.where(step == high, (2 * j + sat) * cap, 0)
         turn += jnp.where(step == low, (2 * j + 1 - sat) * cap, 0)
     near = valid & (step > 0) & (spot == turn + rank)
-    far = (valid & (iota(far_ref.shape, 1) == step * cap + rank)).astype(F32)
+    far = (valid & (iota((count, far_ref.shape[0]), 1) == step * cap + rank)).astype(F32)
     local = jnp.broadcast_to((col - owner * group - group // 2).astype(F32), (count, names_ref.shape[1]))
     near_ref[...] = near.astype(F32) * sign
-    far_ref[...] = far * sign
+    far_ref[...] = (far * sign).T
     names_ref[...] = transposed_dot(far.astype(BF16), local.astype(BF16))
     turned_ref[...] = jnp.concatenate([observed[...], weights[...]], axis=0).T
 
@@ -124,7 +124,7 @@
         for k in range(slots):
             parts.append(jnp.sum(diff[a * slots + k] * weighted, axis=0, keepdims=True))
     contribution = jnp.concatenate(parts, axis=0).astype(BF16)
-    packed = transposed_dot(far_ref[...].astype(BF16), contribution)
+    packed = jnp.dot(far_ref[...].astype(BF16), contribution, preferred_element_type=F32)
     for k in range(owners):
         part = slice(k * cap, (k + 1) * cap)
         outs[k][...] = jnp.concatenate([packed[part], names_ref[part, :]], axis=1).astype(BF16)
@@ -226,7 +226,7 @@
         [
             shape((count, width), F32),
             shape((count, (owners - 1) * cap), F32),
-            shape((count, owners * cap), F32),
+            shape((owners * cap, count), F32),
             shape((owners * cap, LANES), F32),
             shape((epochs, 2 * arcs), F32),
         ],

time: 25.1 us -> 25.1 us (level)
  no operation moved by 1% of the time
where the time goes in v10:
time: 25.1 us; the launch traced here: 25 us
  starting transfers between devices  11.4 us (45%)
  waiting for transfers between devices  7.14 us (28%)
  Pallas kernels  6.38 us (25%)
    pallas_call x8, Pallas kernels, call(): pl.pallas_call(kernel, out_shape=outs, in_specs=[raw if i in anywhere els...  6.38 us
    ppermute x2, starting transfers between devices, per_device(): asked = {h: lax.ppermute(regions, names, crossing(*h)) for h in hands}  4.88 us
    ppermute x3, starting transfers between devices, per_device(): lax.ppermute(sent[k], names, crossing(k, k))  3.89 us
    ppermute x2, waiting for transfers between devices, per_device(): came[h] = lax.ppermute(rows, names, crossing(*h[::-1]))  3.17 us
    ppermute x3, waiting for transfers between devices, per_device(): lax.ppermute(sent[k], names, crossing(k, k))  1.45 us
    ppermute x1, starting transfers between devices, per_device(): early, late = ([mine], [lax.ppermute(mine, ('arc', 'sat'), over)])  1.36 us
    ppermute x1, waiting for transfers between devices, per_device(): early, late = ([mine], [lax.ppermute(mine, ('arc', 'sat'), over)])  0.98 us
    ppermute x2, waiting for transfers between devices, per_device(): asked = {h: lax.ppermute(regions, names, crossing(*h)) for h in hands}  0.8 us
  transfers between devices with their start and end apart: 10, of which 6 were waited for; matrix products, arithmetic and copies ran while one was open for 0% of the time, Pallas kernels for 18%

profile of v10, /device:TPU:0, one launch (start us, length us, event | category | flops | bytes accessed | tf_op | source)
XLA Modules:
  0.0 25.0 jit_solution(8286026570737804801)
XLA Ops:
  0.0 0.5 %collective-permute-start.5 = (bf16[4,8,1,128,256]{4,3,2,1,0:T(8,128)(2,1)}, bf16[4,8,1,128,256]{4,3,2,1,0:T(8,128)(2,1)S(1)}, u32[]{:S(2)}, u32[]{:S(2)}) collective-permute-start(bf16[4,8,1,128,256]{4,3,2,1,0:T(8,128)(2,1)} %param.6), channel_id=1, source_target_pairs={{0,1},{1,0},{2,3},{3,2},{4,5},{5,4},{6,7},{7,6},{8,9},{9,8},{10,11... | collective-permute-start | bytes 6291464 | tf_op jit(solution)/shard_map/ppermute | solution.py:195
  0.5 4.7 %collective-permute-start = (s32[4,8]{1,0:T(4,128)}, s32[4,8]{1,0:T(4,128)S(1)}, u32[]{:S(2)}, u32[]{:S(2)}) collective-permute-start(s32[4,8]{1,0:T(4,128)} %refs_0_.1), channel_id=1, source_target_pairs={{0,7},{1,4},{2,5},{3,6},{4,3},{5,0},{6,1},{7,2},{8,15},{9,12},{10,... | collective-permute-start | bytes 392 | tf_op jit(solution)/shard_map/ppermute | solution.py:194
  5.2 0.2 collective-permute-start.1
  5.3 1.8 %load.1 = (bf16[480,256]{1,0:T(8,128)(2,1)S(1)}, s32[4,8]{1,0:T(4,128)S(1)}, f32[4,128]{1,0:T(4,128)S(1)}, f32[4,128]{1,0:T(4,128)S(1)}, bf16[32,128,256]{2,1,0:T(8,128)(2,1)S(1)}) custom-call(f32[480,1,256]{2,1,0:T(1,128)} %mascons.3, s32[4,8]{1,0:T(4,128)} %refs_0_.1, f32[4,128]{1,0:T(4,128)} %refs_1_.1, f32[4,128]{1,0:T(4,128)} %refs_2_.1, ...), custom_call_target="tpu_custom_call" | custom-call | flops 122880 | bytes 491520 | tf_op jit(solution)/shard_map/load/pallas_call | solution.py:161
  7.2 0.0 collective-permute-done.refs_0_
  7.2 0.4 %lookup.2 = bf16[8,256]{1,0:T(8,128)(2,1)S(1)} custom-call(s32[4,8]{1,0:T(4,128)S(1)} %collective-permute-done.refs_0_, bf16[480,256]{1,0:T(8,128)(2,1)S(1)} %get-tuple-element.22.refs_1_.table), custom_call_target="tpu_custom_call" | custom-call | flops 7864320 | bytes 491520 | tf_op jit(solution)/shard_map/lookup/pallas_call | solution.py:161
  7.6 0.8 %collective-permute-done.1.refs_0_ = s32[4,8]{1,0:T(4,128)S(1)} collective-permute-done((s32[4,8]{1,0:T(4,128)}, s32[4,8]{1,0:T(4,128)S(1)}, u32[]{:S(2)}, u32[]{:S(2)}) %collective-permute-start.1) | collective-permute-done | bytes 160 | tf_op jit(solution)/shard_map/ppermute | solution.py:194
  8.4 0.0 collective-permute-start.2
  8.4 0.4 %lookup.3 = bf16[8,256]{1,0:T(8,128)(2,1)S(1)} custom-call(s32[4,8]{1,0:T(4,128)S(1)} %collective-permute-done.1.refs_0_, bf16[480,256]{1,0:T(8,128)(2,1)S(1)} %get-tuple-element.22.refs_1_.table), custom_call_target="tpu_custom_call" | custom-call | flops 7864320 | bytes 491520 | tf_op jit(solution)/shard_map/lookup/pallas_call | solution.py:161
  8.8 0.8 %collective-permute-start.4 = (bf16[8,256]{1,0:T(8,128)(2,1)S(1)}, bf16[8,256]{1,0:T(8,128)(2,1)S(1)}, u32[]{:S(2)}, u32[]{:S(2)}) collective-permute-start(bf16[8,256]{1,0:T(8,128)(2,1)S(1)} %lookup.3), channel_id=1, source_target_pairs={{0,3},{1,2},{2,1},{3,0},{4,7},{5,6},{6,5},{7,4},{8,11},{9,10},{10,... | collective-permute-start | bytes 12296 | tf_op jit(solution)/shard_map/ppermute | solution.py:221
  9.6 0.5 %plan.1 = (f32[32,256]{1,0:T(8,128)S(1)}, f32[32,24]{1,0:T(8,128)S(1)}, f32[32,32]{1,0:T(8,128)S(1)}, f32[32,128]{1,0:T(8,128)S(1)}, f32[128,8]{1,0:T(8,128)S(1)}) custom-call(s32[4,8]{1,0:T(4,128)S(1)} %get-tuple-element.25.ids, f32[4,128]{1,0:T(4,128)S(1)} %get-tuple-element.26.observed, f32[4,128]{1,0:T(4,128)S(1)} %get-tuple-element.27.weights, ...), custom_call_target="tpu_custom_call" | custom-call | flops 262144 | bytes 32768 | tf_op jit(solution)/shard_map/plan/pallas_call | solution.py:161
  10.0 3.2 %collective-permute-done.2.refs_0_ = bf16[8,256]{1,0:T(8,128)(2,1)S(1)} collective-permute-done((bf16[8,256]{1,0:T(8,128)(2,1)S(1)}, bf16[8,256]{1,0:T(8,128)(2,1)S(1)}, u32[]{:S(2)}, u32[]{:S(2)}) %collective-permute-start.2) | collective-permute-done | bytes 4128 | tf_op jit(solution)/shard_map/ppermute | solution.py:221
  13.2 0.0 collective-permute-start.3
  13.2 0.0 collective-permute-done.5
  13.2 0.4 %differ.1.refs_8_ = f32[32,128,256]{2,1,0:T(8,128)S(1)} custom-call(bf16[32,128,256]{2,1,0:T(8,128)(2,1)S(1)} %get-tuple-element.34.mine, bf16[32,128,256]{2,1,0:T(8,128)(2,1)S(1)} %bitcast.7), custom_call_target="tpu_custom_call" | custom-call | flops 1048576 | bytes 8388608 | tf_op jit(solution)/shard_map/differ/pallas_call | solution.py:161
  13.6 0.0 collective-permute-done.4.refs_2_
  13.6 0.7 %collective-permute-done.3.refs_1_ = bf16[8,256]{1,0:T(8,128)(2,1)S(1)} collective-permute-done((bf16[8,256]{1,0:T(8,128)(2,1)S(1)}, bf16[8,256]{1,0:T(8,128)(2,1)S(1)}, u32[]{:S(2)}, u32[]{:S(2)}) %collective-permute-start.3) | collective-permute-done | bytes 4128 | tf_op jit(solution)/shard_map/ppermute | solution.py:248
  14.4 0.0 copy-start
  14.4 1.0 %solve.1 = (bf16[8,384]{1,0:T(8,128)(2,1)S(1)}, bf16[8,384]{1,0:T(8,128)(2,1)S(1)}, bf16[8,384]{1,0:T(8,128)(2,1)S(1)}, bf16[8,384]{1,0:T(8,128)(2,1)S(1)}) custom-call(bf16[8,256]{1,0:T(8,128)(2,1)S(1)} %collective-permute-done.2.refs_0_, bf16[8,256]{1,0:T(8,128)(2,1)S(1)} %collective-permute-done.3.refs_1_, ...), custom_call_target="tpu_custom_call" | custom-call | flops 4194304 | bytes 4194304 | tf_op jit(solution)/shard_map/solve/pallas_call | solution.py:161
  15.4 1.3 %collective-permute-start.6 = (bf16[8,384]{1,0:T(8,128)(2,1)S(1)}, bf16[8,384]{1,0:T(8,128)(2,1)S(1)}, u32[]{:S(2)}, u32[]{:S(2)}) collective-permute-start(bf16[8,384]{1,0:T(8,128)(2,1)S(1)} %get-tuple-element.36), channel_id=1, source_target_pairs={{0,7},{1,6},{2,5},{3,4},{4,3},{5,2},{6,1},{7,0},{8,15},{9,14},{10,... | collective-permute-start | bytes 18440 | tf_op jit(solution)/shard_map/ppermute | solution.py:258
  16.7 0.1 collective-permute-start.7
  16.8 2.5 %collective-permute-start.8 = (bf16[8,384]{1,0:T(8,128)(2,1)S(1)}, bf16[8,384]{1,0:T(8,128)(2,1)S(1)}, u32[]{:S(2)}, u32[]{:S(2)}) collective-permute-start(bf16[8,384]{1,0:T(8,128)(2,1)S(1)} %get-tuple-element.38), channel_id=1, source_target_pairs={{0,3},{1,2},{2,1},{3,0},{4,7},{5,6},{6,5},{7,4},{8,11},{9,10},{10,... | collective-permute-start | bytes 18440 | tf_op jit(solution)/shard_map/ppermute | solution.py:258
  19.3 1.0 %collective-permute-done.6 = bf16[8,384]{1,0:T(8,128)(2,1)S(1)} collective-permute-done((bf16[8,384]{1,0:T(8,128)(2,1)S(1)}, bf16[8,384]{1,0:T(8,128)(2,1)S(1)}, u32[]{:S(2)}, u32[]{:S(2)}) %collective-permute-start.6) | collective-permute-done | bytes 6176 | tf_op jit(solution)/shard_map/ppermute | solution.py:258
  20.3 0.5 %collective-permute-done.7 = bf16[8,384]{1,0:T(8,128)(2,1)S(1)} collective-permute-done((bf16[8,384]{1,0:T(8,128)(2,1)S(1)}, bf16[8,384]{1,0:T(8,128)(2,1)S(1)}, u32[]{:S(2)}, u32[]{:S(2)}) %collective-permute-start.7) | collective-permute-done | bytes 6176 | tf_op jit(solution)/shard_map/ppermute | solution.py:258
  20.8 0.0 collective-permute-done.8
  20.8 1.4 %collective-permute-start.9 = (bf16[4,8,384]{2,1,0:T(8,128)(2,1)S(1)}, bf16[4,8,384]{2,1,0:T(8,128)(2,1)S(1)}, u32[]{:S(2)}, u32[]{:S(2)}) collective-permute-start(bf16[4,8,384]{2,1,0:T(8,128)(2,1)S(1)} %pad_maximum_fusion.refs_0_), channel_id=1, source_target_pairs={{0,9},{1,8},{8,1},{9,0},{2,11},{3,10},{10,3},{11,2},{4,13},{5,12},... | collective-permute-start | bytes 73736 | tf_op jit(solution)/shard_map/ppermute | solution.py:262
  22.1 0.0 copy-done
  22.1 1.0 %base.1.refs_1_ = f32[120,256]{1,0:T(8,128)S(1)} custom-call(f32[480,1,256]{2,1,0:T(1,128)} %mascons.3, f32[1,256]{1,0:T(1,128)S(1)} %bitcast.9, bf16[4,8,384]{2,1,0:T(8,128)(2,1)S(1)} %pad_maximum_fusion.refs_0_), custom_call_target="tpu_custom_call" | custom-call | flops 1966080 | bytes 245760 | tf_op jit(solution)/shard_map/base/pallas_call | solution.py:161
  23.1 1.0 %collective-permute-done.9.refs_0_ = bf16[4,8,384]{2,1,0:T(8,128)(2,1)S(1)} collective-permute-done((bf16[4,8,384]{2,1,0:T(8,128)(2,1)S(1)}, bf16[4,8,384]{2,1,0:T(8,128)(2,1)S(1)}, u32[]{:S(2)}, u32[]{:S(2)}) %collective-permute-start.9) | collective-permute-done | bytes 24608 | tf_op jit(solution)/shard_map/ppermute | solution.py:262
  24.1 0.9 %place.1 = f32[120,1,256]{2,1,0:T(1,128)} custom-call(bf16[4,8,384]{2,1,0:T(8,128)(2,1)S(1)} %collective-permute-done.9.refs_0_, f32[120,256]{1,0:T(8,128)S(1)} %base.1.refs_1_), custom_call_target="tpu_custom_call" | custom-call | flops 3932160 | bytes 245760 | tf_op jit(solution)/shard_map/place/pallas_call | solution.py:161
  (1 shorter events, 0.0 us)
Async XLA Ops:
  0.0 13.2 %collective-permute-start.5 = (bf16[4,8,1,128,256]{4,3,2,1,0:T(8,128)(2,1)}, bf16[4,8,1,128,256]{4,3,2,1,0:T(8,128)(2,1)S(1)}, u32[]{:S(2)}, u32[]{:S(2)}) collective-permute-start(bf16[4,8,1,128,256]{4,3,2,1,0:T(8,128)(2,1)} %param.6), channel_id=1, source_target_pairs={{0,1},{1,0},{2,3},{3,2},{4,5},{5,4},{6,7},{7,6},{8,9},{9,8},{10,11... | collective-permute-start | bytes 6291464 | tf_op jit(solution)/shard_map/ppermute | solution.py:195
  0.5 6.7 %collective-permute-start = (s32[4,8]{1,0:T(4,128)}, s32[4,8]{1,0:T(4,128)S(1)}, u32[]{:S(2)}, u32[]{:S(2)}) collective-permute-start(s32[4,8]{1,0:T(4,128)} %refs_0_.1), channel_id=1, source_target_pairs={{0,7},{1,4},{2,5},{3,6},{4,3},{5,0},{6,1},{7,2},{8,15},{9,12},{10,... | collective-permute-start | bytes 392 | tf_op jit(solution)/shard_map/ppermute | solution.py:194
  5.2 3.2 %collective-permute-start.1 = (s32[4,8]{1,0:T(4,128)}, s32[4,8]{1,0:T(4,128)S(1)}, u32[]{:S(2)}, u32[]{:S(2)}) collective-permute-start(s32[4,8]{1,0:T(4,128)} %refs_0_.1), channel_id=1, source_target_pairs={{0,3},{1,2},{2,1},{3,0},{4,7},{5,6},{6,5},{7,4},{8,11},{9,10},{10,... | collective-permute-start | bytes 392 | tf_op jit(solution)/shard_map/ppermute | solution.py:194
  8.4 4.8 %collective-permute-start.2 = (bf16[8,256]{1,0:T(8,128)(2,1)S(1)}, bf16[8,256]{1,0:T(8,128)(2,1)S(1)}, u32[]{:S(2)}, u32[]{:S(2)}) collective-permute-start(bf16[8,256]{1,0:T(8,128)(2,1)S(1)} %lookup.2), channel_id=1, source_target_pairs={{0,5},{1,6},{2,7},{3,4},{4,1},{5,2},{6,3},{7,0},{8,13},{9,14},{10,... | collective-permute-start | bytes 12296 | tf_op jit(solution)/shard_map/ppermute | solution.py:221
  8.8 4.9 %collective-permute-start.4 = (bf16[8,256]{1,0:T(8,128)(2,1)S(1)}, bf16[8,256]{1,0:T(8,128)(2,1)S(1)}, u32[]{:S(2)}, u32[]{:S(2)}) collective-permute-start(bf16[8,256]{1,0:T(8,128)(2,1)S(1)} %lookup.3), channel_id=1, source_target_pairs={{0,3},{1,2},{2,1},{3,0},{4,7},{5,6},{6,5},{7,4},{8,11},{9,10},{10,... | collective-permute-start | bytes 12296 | tf_op jit(solution)/shard_map/ppermute | solution.py:221
  13.2 1.2 %collective-permute-start.3 = (bf16[8,256]{1,0:T(8,128)(2,1)S(1)}, bf16[8,256]{1,0:T(8,128)(2,1)S(1)}, u32[]{:S(2)}, u32[]{:S(2)}) collective-permute-start(bf16[8,256]{1,0:T(8,128)(2,1)S(1)} %collective-permute-done.2.refs_0_), channel_id=1, source_target_pairs={{0,1},{1,0},{2,3},{3,2},{4,5},{5,4},{6,7},{7,6},{8,9},{9,8},{10,11... | collective-permute-start | bytes 12296 | tf_op jit(solution)/shard_map/ppermute | solution.py:248
  14.4 7.8 %copy-start = (f32[256]{0:T(256)S(1)}, f32[256]{0:T(256)}, u32[]{:S(2)}) copy-start(f32[256]{0:T(256)} %param.11) | copy-start | bytes 3076
  15.4 4.9 %collective-permute-start.6 = (bf16[8,384]{1,0:T(8,128)(2,1)S(1)}, bf16[8,384]{1,0:T(8,128)(2,1)S(1)}, u32[]{:S(2)}, u32[]{:S(2)}) collective-permute-start(bf16[8,384]{1,0:T(8,128)(2,1)S(1)} %get-tuple-element.36), channel_id=1, source_target_pairs={{0,7},{1,6},{2,5},{3,4},{4,3},{5,2},{6,1},{7,0},{8,15},{9,14},{10,... | collective-permute-start | bytes 18440 | tf_op jit(solution)/shard_map/ppermute | solution.py:258
  16.7 4.0 %collective-permute-start.7 = (bf16[8,384]{1,0:T(8,128)(2,1)S(1)}, bf16[8,384]{1,0:T(8,128)(2,1)S(1)}, u32[]{:S(2)}, u32[]{:S(2)}) collective-permute-start(bf16[8,384]{1,0:T(8,128)(2,1)S(1)} %get-tuple-element.37), channel_id=1, source_target_pairs={{0,5},{1,4},{2,7},{3,6},{4,1},{5,0},{6,3},{7,2},{8,13},{9,12},{10,... | collective-permute-start | bytes 18440 | tf_op jit(solution)/shard_map/ppermute | solution.py:258
  16.8 3.9 %collective-permute-start.8 = (bf16[8,384]{1,0:T(8,128)(2,1)S(1)}, bf16[8,384]{1,0:T(8,128)(2,1)S(1)}, u32[]{:S(2)}, u32[]{:S(2)}) collective-permute-start(bf16[8,384]{1,0:T(8,128)(2,1)S(1)} %get-tuple-element.38), channel_id=1, source_target_pairs={{0,3},{1,2},{2,1},{3,0},{4,7},{5,6},{6,5},{7,4},{8,11},{9,10},{10,... | collective-permute-start | bytes 18440 | tf_op jit(solution)/shard_map/ppermute | solution.py:258
  20.8 3.3 %collective-permute-start.9 = (bf16[4,8,384]{2,1,0:T(8,128)(2,1)S(1)}, bf16[4,8,384]{2,1,0:T(8,128)(2,1)S(1)}, u32[]{:S(2)}, u32[]{:S(2)}) collective-permute-start(bf16[4,8,384]{2,1,0:T(8,128)(2,1)S(1)} %pad_maximum_fusion.refs_0_), channel_id=1, source_target_pairs={{0,9},{1,8},{8,1},{9,0},{2,11},{3,10},{10,3},{11,2},{4,13},{5,12},... | collective-permute-start | bytes 73736 | tf_op jit(solution)/shard_map/ppermute | solution.py:262

commit v11 on v9

--- a/solution.py
+++ b/solution.py
@@ -116,7 +116,8 @@
         total = None
         for k in range(slots):
             i = a * slots + k
-            term = diff[i] * rows[i : i + 1, :]
+            row, half = rows[i : i + 1, :], rows.shape[1] // 2
+            term = diff[i, :, :half] * row[:, :half] + diff[i, :, half:] * row[:, half:]
             total = term if total is None else total + term
         predicted = jnp.sum(total, axis=1, keepdims=True)
         weighted = turned[:, arcs + a : arcs + a + 1] * (turned[:, a : a + 1] - predicted)

time: 25.1 us -> 25.1 us (level)
  no operation moved by 1% of the time
where the time goes in v11:
time: 25.1 us; the launch traced here: 25 us
  starting transfers between devices  11.4 us (45%)
  waiting for transfers between devices  7.14 us (28%)
  Pallas kernels  6.38 us (25%)
    pallas_call x8, Pallas kernels, call(): pl.pallas_call(kernel, out_shape=outs, in_specs=[raw if i in anywhere els...  6.38 us
    ppermute x2, starting transfers between devices, per_device(): asked = {h: lax.ppermute(regions, names, crossing(*h)) for h in hands}  4.88 us
    ppermute x3, starting transfers between devices, per_device(): lax.ppermute(sent[k], names, crossing(k, k))  3.89 us
    ppermute x2, waiting for transfers between devices, per_device(): came[h] = lax.ppermute(rows, names, crossing(*h[::-1]))  3.17 us
    ppermute x3, waiting for transfers between devices, per_device(): lax.ppermute(sent[k], names, crossing(k, k))  1.45 us
    ppermute x1, starting transfers between devices, per_device(): early, late = ([mine], [lax.ppermute(mine, ('arc', 'sat'), over)])  1.36 us
    ppermute x1, waiting for transfers between devices, per_device(): early, late = ([mine], [lax.ppermute(mine, ('arc', 'sat'), over)])  0.98 us
    ppermute x2, waiting for transfers between devices, per_device(): asked = {h: lax.ppermute(regions, names, crossing(*h)) for h in hands}  0.8 us
  transfers between devices with their start and end apart: 10, of which 6 were waited for; matrix products, arithmetic and copies ran while one was open for 0% of the time, Pallas kernels for 18%

profile of v11, /device:TPU:0, one launch (start us, length us, event | category | flops | bytes accessed | tf_op | source)
XLA Modules:
  0.0 25.0 jit_solution(8362348618061096939)
XLA Ops:
  0.0 0.5 %collective-permute-start.5 = (bf16[4,8,1,128,256]{4,3,2,1,0:T(8,128)(2,1)}, bf16[4,8,1,128,256]{4,3,2,1,0:T(8,128)(2,1)S(1)}, u32[]{:S(2)}, u32[]{:S(2)}) collective-permute-start(bf16[4,8,1,128,256]{4,3,2,1,0:T(8,128)(2,1)} %param.6), channel_id=1, source_target_pairs={{0,1},{1,0},{2,3},{3,2},{4,5},{5,4},{6,7},{7,6},{8,9},{9,8},{10,11... | collective-permute-start | bytes 6291464 | tf_op jit(solution)/shard_map/ppermute | solution.py:196
  0.5 4.7 %collective-permute-start = (s32[4,8]{1,0:T(4,128)}, s32[4,8]{1,0:T(4,128)S(1)}, u32[]{:S(2)}, u32[]{:S(2)}) collective-permute-start(s32[4,8]{1,0:T(4,128)} %refs_0_.1), channel_id=1, source_target_pairs={{0,7},{1,4},{2,5},{3,6},{4,3},{5,0},{6,1},{7,2},{8,15},{9,12},{10,... | collective-permute-start | bytes 392 | tf_op jit(solution)/shard_map/ppermute | solution.py:195
  5.2 0.2 collective-permute-start.1
  5.3 1.8 %load.1 = (bf16[480,256]{1,0:T(8,128)(2,1)S(1)}, s32[4,8]{1,0:T(4,128)S(1)}, f32[4,128]{1,0:T(4,128)S(1)}, f32[4,128]{1,0:T(4,128)S(1)}, bf16[32,128,256]{2,1,0:T(8,128)(2,1)S(1)}) custom-call(f32[480,1,256]{2,1,0:T(1,128)} %mascons.3, s32[4,8]{1,0:T(4,128)} %refs_0_.1, f32[4,128]{1,0:T(4,128)} %refs_1_.1, f32[4,128]{1,0:T(4,128)} %refs_2_.1, ...), custom_call_target="tpu_custom_call" | custom-call | flops 122880 | bytes 491520 | tf_op jit(solution)/shard_map/load/pallas_call | solution.py:162
  7.2 0.0 collective-permute-done.refs_0_
  7.2 0.4 %lookup.2 = bf16[8,256]{1,0:T(8,128)(2,1)S(1)} custom-call(s32[4,8]{1,0:T(4,128)S(1)} %collective-permute-done.refs_0_, bf16[480,256]{1,0:T(8,128)(2,1)S(1)} %get-tuple-element.22.refs_1_.table), custom_call_target="tpu_custom_call" | custom-call | flops 7864320 | bytes 491520 | tf_op jit(solution)/shard_map/lookup/pallas_call | solution.py:162
  7.6 0.8 %collective-permute-done.1.refs_0_ = s32[4,8]{1,0:T(4,128)S(1)} collective-permute-done((s32[4,8]{1,0:T(4,128)}, s32[4,8]{1,0:T(4,128)S(1)}, u32[]{:S(2)}, u32[]{:S(2)}) %collective-permute-start.1) | collective-permute-done | bytes 160 | tf_op jit(solution)/shard_map/ppermute | solution.py:195
  8.4 0.0 collective-permute-start.2
  8.4 0.4 %lookup.3 = bf16[8,256]{1,0:T(8,128)(2,1)S(1)} custom-call(s32[4,8]{1,0:T(4,128)S(1)} %collective-permute-done.1.refs_0_, bf16[480,256]{1,0:T(8,128)(2,1)S(1)} %get-tuple-element.22.refs_1_.table), custom_call_target="tpu_custom_call" | custom-call | flops 7864320 | bytes 491520 | tf_op jit(solution)/shard_map/lookup/pallas_call | solution.py:162
  8.8 0.8 %collective-permute-start.4 = (bf16[8,256]{1,0:T(8,128)(2,1)S(1)}, bf16[8,256]{1,0:T(8,128)(2,1)S(1)}, u32[]{:S(2)}, u32[]{:S(2)}) collective-permute-start(bf16[8,256]{1,0:T(8,128)(2,1)S(1)} %lookup.3), channel_id=1, source_target_pairs={{0,3},{1,2},{2,1},{3,0},{4,7},{5,6},{6,5},{7,4},{8,11},{9,10},{10,... | collective-permute-start | bytes 12296 | tf_op jit(solution)/shard_map/ppermute | solution.py:222
  9.6 0.5 %plan.1 = (f32[32,256]{1,0:T(8,128)S(1)}, f32[32,24]{1,0:T(8,128)S(1)}, f32[32,32]{1,0:T(8,128)S(1)}, f32[32,128]{1,0:T(8,128)S(1)}, f32[128,8]{1,0:T(8,128)S(1)}) custom-call(s32[4,8]{1,0:T(4,128)S(1)} %get-tuple-element.25.ids, f32[4,128]{1,0:T(4,128)S(1)} %get-tuple-element.26.observed, f32[4,128]{1,0:T(4,128)S(1)} %get-tuple-element.27.weights, ...), custom_call_target="tpu_custom_call" | custom-call | flops 262144 | bytes 32768 | tf_op jit(solution)/shard_map/plan/pallas_call | solution.py:162
  10.1 3.2 %collective-permute-done.2.refs_0_ = bf16[8,256]{1,0:T(8,128)(2,1)S(1)} collective-permute-done((bf16[8,256]{1,0:T(8,128)(2,1)S(1)}, bf16[8,256]{1,0:T(8,128)(2,1)S(1)}, u32[]{:S(2)}, u32[]{:S(2)}) %collective-permute-start.2) | collective-permute-done | bytes 4128 | tf_op jit(solution)/shard_map/ppermute | solution.py:222
  13.2 0.0 collective-permute-start.3
  13.2 0.0 collective-permute-done.5
  13.2 0.4 %differ.1.refs_8_ = f32[32,128,256]{2,1,0:T(8,128)S(1)} custom-call(bf16[32,128,256]{2,1,0:T(8,128)(2,1)S(1)} %get-tuple-element.34.mine, bf16[32,128,256]{2,1,0:T(8,128)(2,1)S(1)} %bitcast.7), custom_call_target="tpu_custom_call" | custom-call | flops 1048576 | bytes 8388608 | tf_op jit(solution)/shard_map/differ/pallas_call | solution.py:162
  13.6 0.0 collective-permute-done.4.refs_2_
  13.6 0.7 %collective-permute-done.3.refs_1_ = bf16[8,256]{1,0:T(8,128)(2,1)S(1)} collective-permute-done((bf16[8,256]{1,0:T(8,128)(2,1)S(1)}, bf16[8,256]{1,0:T(8,128)(2,1)S(1)}, u32[]{:S(2)}, u32[]{:S(2)}) %collective-permute-start.3) | collective-permute-done | bytes 4128 | tf_op jit(solution)/shard_map/ppermute | solution.py:249
  14.4 0.0 copy-start
  14.4 1.0 %solve.1 = (bf16[8,384]{1,0:T(8,128)(2,1)S(1)}, bf16[8,384]{1,0:T(8,128)(2,1)S(1)}, bf16[8,384]{1,0:T(8,128)(2,1)S(1)}, bf16[8,384]{1,0:T(8,128)(2,1)S(1)}) custom-call(bf16[8,256]{1,0:T(8,128)(2,1)S(1)} %collective-permute-done.2.refs_0_, bf16[8,256]{1,0:T(8,128)(2,1)S(1)} %collective-permute-done.3.refs_1_, ...), custom_call_target="tpu_custom_call" | custom-call | flops 4194304 | bytes 4194304 | tf_op jit(solution)/shard_map/solve/pallas_call | solution.py:162
  15.4 1.3 %collective-permute-start.6 = (bf16[8,384]{1,0:T(8,128)(2,1)S(1)}, bf16[8,384]{1,0:T(8,128)(2,1)S(1)}, u32[]{:S(2)}, u32[]{:S(2)}) collective-permute-start(bf16[8,384]{1,0:T(8,128)(2,1)S(1)} %get-tuple-element.36), channel_id=1, source_target_pairs={{0,7},{1,6},{2,5},{3,4},{4,3},{5,2},{6,1},{7,0},{8,15},{9,14},{10,... | collective-permute-start | bytes 18440 | tf_op jit(solution)/shard_map/ppermute | solution.py:259
  16.7 0.1 collective-permute-start.7
  16.8 2.5 %collective-permute-start.8 = (bf16[8,384]{1,0:T(8,128)(2,1)S(1)}, bf16[8,384]{1,0:T(8,128)(2,1)S(1)}, u32[]{:S(2)}, u32[]{:S(2)}) collective-permute-start(bf16[8,384]{1,0:T(8,128)(2,1)S(1)} %get-tuple-element.38), channel_id=1, source_target_pairs={{0,3},{1,2},{2,1},{3,0},{4,7},{5,6},{6,5},{7,4},{8,11},{9,10},{10,... | collective-permute-start | bytes 18440 | tf_op jit(solution)/shard_map/ppermute | solution.py:259
  19.3 1.0 %collective-permute-done.6 = bf16[8,384]{1,0:T(8,128)(2,1)S(1)} collective-permute-done((bf16[8,384]{1,0:T(8,128)(2,1)S(1)}, bf16[8,384]{1,0:T(8,128)(2,1)S(1)}, u32[]{:S(2)}, u32[]{:S(2)}) %collective-permute-start.6) | collective-permute-done | bytes 6176 | tf_op jit(solution)/shard_map/ppermute | solution.py:259
  20.3 0.5 %collective-permute-done.7 = bf16[8,384]{1,0:T(8,128)(2,1)S(1)} collective-permute-done((bf16[8,384]{1,0:T(8,128)(2,1)S(1)}, bf16[8,384]{1,0:T(8,128)(2,1)S(1)}, u32[]{:S(2)}, u32[]{:S(2)}) %collective-permute-start.7) | collective-permute-done | bytes 6176 | tf_op jit(solution)/shard_map/ppermute | solution.py:259
  20.8 0.0 collective-permute-done.8
  20.8 1.4 %collective-permute-start.9 = (bf16[4,8,384]{2,1,0:T(8,128)(2,1)S(1)}, bf16[4,8,384]{2,1,0:T(8,128)(2,1)S(1)}, u32[]{:S(2)}, u32[]{:S(2)}) collective-permute-start(bf16[4,8,384]{2,1,0:T(8,128)(2,1)S(1)} %pad_maximum_fusion.refs_0_), channel_id=1, source_target_pairs={{0,9},{1,8},{8,1},{9,0},{2,11},{3,10},{10,3},{11,2},{4,13},{5,12},... | collective-permute-start | bytes 73736 | tf_op jit(solution)/shard_map/ppermute | solution.py:263
  22.1 0.0 copy-done
  22.1 1.0 %base.1.refs_1_ = f32[120,256]{1,0:T(8,128)S(1)} custom-call(f32[480,1,256]{2,1,0:T(1,128)} %mascons.3, f32[1,256]{1,0:T(1,128)S(1)} %bitcast.9, bf16[4,8,384]{2,1,0:T(8,128)(2,1)S(1)} %pad_maximum_fusion.refs_0_), custom_call_target="tpu_custom_call" | custom-call | flops 1966080 | bytes 245760 | tf_op jit(solution)/shard_map/base/pallas_call | solution.py:162
  23.1 1.0 %collective-permute-done.9.refs_0_ = bf16[4,8,384]{2,1,0:T(8,128)(2,1)S(1)} collective-permute-done((bf16[4,8,384]{2,1,0:T(8,128)(2,1)S(1)}, bf16[4,8,384]{2,1,0:T(8,128)(2,1)S(1)}, u32[]{:S(2)}, u32[]{:S(2)}) %collective-permute-start.9) | collective-permute-done | bytes 24608 | tf_op jit(solution)/shard_map/ppermute | solution.py:263
  24.1 0.9 %place.1 = f32[120,1,256]{2,1,0:T(1,128)} custom-call(bf16[4,8,384]{2,1,0:T(8,128)(2,1)S(1)} %collective-permute-done.9.refs_0_, f32[120,256]{1,0:T(8,128)S(1)} %base.1.refs_1_), custom_call_target="tpu_custom_call" | custom-call | flops 3932160 | bytes 245760 | tf_op jit(solution)/shard_map/place/pallas_call | solution.py:162
  (1 shorter events, 0.0 us)
Async XLA Ops:
  0.0 13.2 %collective-permute-start.5 = (bf16[4,8,1,128,256]{4,3,2,1,0:T(8,128)(2,1)}, bf16[4,8,1,128,256]{4,3,2,1,0:T(8,128)(2,1)S(1)}, u32[]{:S(2)}, u32[]{:S(2)}) collective-permute-start(bf16[4,8,1,128,256]{4,3,2,1,0:T(8,128)(2,1)} %param.6), channel_id=1, source_target_pairs={{0,1},{1,0},{2,3},{3,2},{4,5},{5,4},{6,7},{7,6},{8,9},{9,8},{10,11... | collective-permute-start | bytes 6291464 | tf_op jit(solution)/shard_map/ppermute | solution.py:196
  0.5 6.7 %collective-permute-start = (s32[4,8]{1,0:T(4,128)}, s32[4,8]{1,0:T(4,128)S(1)}, u32[]{:S(2)}, u32[]{:S(2)}) collective-permute-start(s32[4,8]{1,0:T(4,128)} %refs_0_.1), channel_id=1, source_target_pairs={{0,7},{1,4},{2,5},{3,6},{4,3},{5,0},{6,1},{7,2},{8,15},{9,12},{10,... | collective-permute-start | bytes 392 | tf_op jit(solution)/shard_map/ppermute | solution.py:195
  5.2 3.2 %collective-permute-start.1 = (s32[4,8]{1,0:T(4,128)}, s32[4,8]{1,0:T(4,128)S(1)}, u32[]{:S(2)}, u32[]{:S(2)}) collective-permute-start(s32[4,8]{1,0:T(4,128)} %refs_0_.1), channel_id=1, source_target_pairs={{0,3},{1,2},{2,1},{3,0},{4,7},{5,6},{6,5},{7,4},{8,11},{9,10},{10,... | collective-permute-start | bytes 392 | tf_op jit(solution)/shard_map/ppermute | solution.py:195
  8.4 4.8 %collective-permute-start.2 = (bf16[8,256]{1,0:T(8,128)(2,1)S(1)}, bf16[8,256]{1,0:T(8,128)(2,1)S(1)}, u32[]{:S(2)}, u32[]{:S(2)}) collective-permute-start(bf16[8,256]{1,0:T(8,128)(2,1)S(1)} %lookup.2), channel_id=1, source_target_pairs={{0,5},{1,6},{2,7},{3,4},{4,1},{5,2},{6,3},{7,0},{8,13},{9,14},{10,... | collective-permute-start | bytes 12296 | tf_op jit(solution)/shard_map/ppermute | solution.py:222
  8.8 4.9 %collective-permute-start.4 = (bf16[8,256]{1,0:T(8,128)(2,1)S(1)}, bf16[8,256]{1,0:T(8,128)(2,1)S(1)}, u32[]{:S(2)}, u32[]{:S(2)}) collective-permute-start(bf16[8,256]{1,0:T(8,128)(2,1)S(1)} %lookup.3), channel_id=1, source_target_pairs={{0,3},{1,2},{2,1},{3,0},{4,7},{5,6},{6,5},{7,4},{8,11},{9,10},{10,... | collective-permute-start | bytes 12296 | tf_op jit(solution)/shard_map/ppermute | solution.py:222
  13.2 1.2 %collective-permute-start.3 = (bf16[8,256]{1,0:T(8,128)(2,1)S(1)}, bf16[8,256]{1,0:T(8,128)(2,1)S(1)}, u32[]{:S(2)}, u32[]{:S(2)}) collective-permute-start(bf16[8,256]{1,0:T(8,128)(2,1)S(1)} %collective-permute-done.2.refs_0_), channel_id=1, source_target_pairs={{0,1},{1,0},{2,3},{3,2},{4,5},{5,4},{6,7},{7,6},{8,9},{9,8},{10,11... | collective-permute-start | bytes 12296 | tf_op jit(solution)/shard_map/ppermute | solution.py:249
  14.4 7.8 %copy-start = (f32[256]{0:T(256)S(1)}, f32[256]{0:T(256)}, u32[]{:S(2)}) copy-start(f32[256]{0:T(256)} %param.11) | copy-start | bytes 3076
  15.4 4.9 %collective-permute-start.6 = (bf16[8,384]{1,0:T(8,128)(2,1)S(1)}, bf16[8,384]{1,0:T(8,128)(2,1)S(1)}, u32[]{:S(2)}, u32[]{:S(2)}) collective-permute-start(bf16[8,384]{1,0:T(8,128)(2,1)S(1)} %get-tuple-element.36), channel_id=1, source_target_pairs={{0,7},{1,6},{2,5},{3,4},{4,3},{5,2},{6,1},{7,0},{8,15},{9,14},{10,... | collective-permute-start | bytes 18440 | tf_op jit(solution)/shard_map/ppermute | solution.py:259
  16.7 4.0 %collective-permute-start.7 = (bf16[8,384]{1,0:T(8,128)(2,1)S(1)}, bf16[8,384]{1,0:T(8,128)(2,1)S(1)}, u32[]{:S(2)}, u32[]{:S(2)}) collective-permute-start(bf16[8,384]{1,0:T(8,128)(2,1)S(1)} %get-tuple-element.37), channel_id=1, source_target_pairs={{0,5},{1,4},{2,7},{3,6},{4,1},{5,0},{6,3},{7,2},{8,13},{9,12},{10,... | collective-permute-start | bytes 18440 | tf_op jit(solution)/shard_map/ppermute | solution.py:259
  16.8 3.9 %collective-permute-start.8 = (bf16[8,384]{1,0:T(8,128)(2,1)S(1)}, bf16[8,384]{1,0:T(8,128)(2,1)S(1)}, u32[]{:S(2)}, u32[]{:S(2)}) collective-permute-start(bf16[8,384]{1,0:T(8,128)(2,1)S(1)} %get-tuple-element.38), channel_id=1, source_target_pairs={{0,3},{1,2},{2,1},{3,0},{4,7},{5,6},{6,5},{7,4},{8,11},{9,10},{10,... | collective-permute-start | bytes 18440 | tf_op jit(solution)/shard_map/ppermute | solution.py:259
  20.8 3.3 %collective-permute-start.9 = (bf16[4,8,384]{2,1,0:T(8,128)(2,1)S(1)}, bf16[4,8,384]{2,1,0:T(8,128)(2,1)S(1)}, u32[]{:S(2)}, u32[]{:S(2)}) collective-permute-start(bf16[4,8,384]{2,1,0:T(8,128)(2,1)S(1)} %pad_maximum_fusion.refs_0_), channel_id=1, source_target_pairs={{0,9},{1,8},{8,1},{9,0},{2,11},{3,10},{10,3},{11,2},{4,13},{5,12},... | collective-permute-start | bytes 73736 | tf_op jit(solution)/shard_map/ppermute | solution.py:263
